TPU v7x, 256 devices: a whole 4x4x8 slice. The times are simulated.
256 devices in a mesh: depth: 32 (over z, x_lo, core), height: 4 (over y), batch: 2 (over x_hi).
Axes of the slice: x: 4 (x_hi: 2, x_lo: 2; x = x_hi * 2 + x_lo), y: 4, z: 8, core: 2. Of those that a mesh axis runs over, the one named last changes fastest.
Arguments:
- volumes: bfloat16 [8, 4, 128, 32, 128], P('batch', None, 'depth', 'height'), may hold values from -6 to 6
- first_kernel: bfloat16 [3, 3, 3, 4, 32], replicated, may hold values from -0.625 to 0.625
- first_bias: float32 [32], replicated, may hold values from -3 to 3
- second_kernel: bfloat16 [3, 3, 3, 32, 64], replicated, may hold values from -0.21875 to 0.21875
- second_bias: float32 [64], replicated, may hold values from -3 to 3
- deep_grad: bfloat16 [8, 64, 32, 8, 32], P(('batch', 'height'), None, 'depth'), may hold values from -0.15917969 to 0.15917969
Outputs:
- deep_maps: bfloat16 [8, 64, 32, 8, 32], P(('batch', 'height'), None, 'depth')
- first_kernel_grad: float32 [3, 3, 3, 4, 32], replicated
- first_bias_grad: float32 [32], replicated
- second_kernel_grad: float32 [3, 3, 3, 32, 64], replicated
- second_bias_grad: float32 [64], replicated
All inputs are finite; a program needn't handle non-finite values.
Results may differ from a plain program's by a relative error of at most 0.0051.
Values may be sent and summed in bfloat16 or wider, within the bound.
No kernel may reach another device: no remote copies, remote signals or barrier semaphores. Data moves between devices by JAX's collectives and lax.ppermute only.
A program may use at most 128 MiB of HBM per device.

v0:
```python
import jax
import jax.numpy as jnp
from jax import lax
from jax.sharding import PartitionSpec as P


def padded_2(cells, sides, width):
    for axis, dim in sides:
        count = lax.axis_size(axis)
        ends = count - 1
        head = lax.slice_in_dim(cells, 0, width, axis=dim)
        tail = lax.slice_in_dim(cells, cells.shape[dim] - width, cells.shape[dim], axis=dim)
        cells = jnp.concatenate(
            [
                lax.ppermute(tail, axis, [(i, (i + 1) % count) for i in range(ends)]),
                cells,
                lax.ppermute(head, axis, [((i + 1) % count, i) for i in range(ends)]),
            ],
            axis=dim,
        )
    return cells


def framed(field):
    deeper = padded_2(field, (("depth", 2),), 1)
    return padded_2(deeper, (("height", 3),), 1)


def conv_valid(padded, kernel, layout):
    return lax.conv_general_dilated(
        padded,
        kernel,
        (1, 1, 1),
        ((0, 0), (0, 0), (1, 1)),
        dimension_numbers=("NCDHW", layout, "NCDHW"),
        preferred_element_type=jnp.float32,
    )


def kernel_grad(padded, cotangent):
    return lax.conv_general_dilated(
        padded,
        cotangent,
        (1, 1, 1),
        ((0, 0), (0, 0), (1, 1)),
        dimension_numbers=("CNDHW", "IODHW", "DHWNC"),
        preferred_element_type=jnp.float32,
    )


def pooled(field):
    count, chans, depth_len, height_len, width_len = field.shape
    blocks = field.reshape(count, chans, depth_len // 2, 2, height_len // 2, 2, width_len // 2, 2)
    return jnp.mean(blocks, axis=(3, 5, 7))


def widened(field):
    count, chans, depth_len, height_len, width_len = field.shape
    spread = jnp.broadcast_to(
        field[:, :, :, None, :, None, :, None],
        (count, chans, depth_len, 2, height_len, 2, width_len, 2),
    )
    return spread.reshape(count, chans, depth_len * 2, height_len * 2, width_len * 2)


def slope(values):
    sigma = jax.nn.sigmoid(values)
    return sigma * (1.0 + values * (1.0 - sigma))


def per_device(volumes, first_kernel, first_bias, second_kernel, second_bias, deep_grad):
    framed_in = framed(volumes)
    pre_first = conv_valid(framed_in, first_kernel, "DHWIO") + first_bias[None, :, None, None, None]
    pooled_first = pooled(jax.nn.silu(pre_first)).astype(jnp.bfloat16)
    framed_pool = framed(pooled_first)
    pre_second = (
        conv_valid(framed_pool, second_kernel, "DHWIO") + second_bias[None, :, None, None, None]
    )
    local_deep = pooled(jax.nn.silu(pre_second)).astype(jnp.bfloat16)
    deep_maps = lax.all_to_all(local_deep, "height", split_axis=0, concat_axis=3, tiled=True)
    local_grad = lax.all_to_all(deep_grad, "height", split_axis=3, concat_axis=0, tiled=True)
    grad_second = (widened(local_grad.astype(jnp.float32)) * 0.125 * slope(pre_second)).astype(
        jnp.bfloat16
    )
    second_kgrad = kernel_grad(framed_pool, grad_second)
    second_bgrad = jnp.sum(grad_second.astype(jnp.float32), axis=(0, 2, 3, 4))
    framed_grad = framed(grad_second)
    back_pool = conv_valid(framed_grad, second_kernel[::-1, ::-1, ::-1], "DHWOI")
    grad_first = (widened(back_pool) * 0.125 * slope(pre_first)).astype(jnp.bfloat16)
    first_kgrad = kernel_grad(framed_in, grad_first)
    first_bgrad = jnp.sum(grad_first.astype(jnp.float32), axis=(0, 2, 3, 4))
    first_kgrad, first_bgrad, second_kgrad, second_bgrad = lax.psum(
        (first_kgrad, first_bgrad, second_kgrad, second_bgrad), ("depth", "height", "batch")
    )
    return (deep_maps, first_kgrad, first_bgrad, second_kgrad, second_bgrad)


def solution(mesh):
    in_specs = (
        P("batch", None, "depth", "height", None),
        P(),
        P(),
        P(),
        P(),
        P(("batch", "height"), None, "depth", None, None),
    )
    out_specs = (P(("batch", "height"), None, "depth", None, None), P(), P(), P(), P())
    return jax.shard_map(
        per_device, mesh=mesh, in_specs=in_specs, out_specs=out_specs, check_vma=False
    )
```

profile of v0, /device:TPU:1, one launch (start us, length us, event | category | flops | bytes accessed | tf_op | source)
XLA Modules:
  0.0 428.9 jit_solution(7787568371372017705)
XLA Ops:
  8.0 4.5 %collective-permute-start = (bf16[4,4,1,8,128]{4,3,2,1,0:T(8,128)(2,1)S(1)}, bf16[4,4,1,8,128]{4,3,2,1,0:T(8,128)(2,1)S(1)}, u32[]{:S(2)}, u32[]{:S(2)}) collective-permute-start(bf16[4,4,1,8,128]{4,3,2,1,0:T(8,128)(2,1)S(1)} %get-tuple-element.27), channel_id=1, source_target_pairs={{0,8},{8,16},{16,24},{24,32},{32,40},{40,48},{48,56},{56,64},{64,7... | collective-permute-start | bytes 98312 | tf_op jit(solution)/shard_map/ppermute | solution.py:15
  12.5 1.9 collective-permute-start.1
  15.4 2.3 collective-permute-done.1
  17.9 3.2 collective-permute-start.2
  22.4 5.1 %copy.63 = bf16[4,4,6,8,128]{0,1,4,3,2:T(4,128)(2,1)} copy(bf16[4,4,6,8,128]{4,3,2,1,0:T(8,128)(2,1)S(1)} %constant_dynamic-update-slice_fusion) | data formatting | bytes 393216 | tf_op jit(solution)/shard_map/concatenate | solution.py:13
  28.7 8.4 %fusion.50 = bf16[4,6,10,4,128]{3,0,4,2,1:T(4,128)(2,1)S(1)} fusion(bf16[4,4,6,1,128]{0,1,4,3,2:T(4,128)(2,1)S(1)} %copy.64, bf16[4,4,6,8,128]{0,1,4,3,2:T(4,128)(2,1)} %copy.63, bf16[4,4,6,1,128]{0,1,4,3,2:T(4,128)(2,1)S(1)} %copy.62), kind=kLoop, calls=%fused_computation.67 | loop fusion | flops 245760 | bytes 491520 | tf_op jit(solution)/shard_map/concatenate | solution.py:13
  37.2 5.7 %pad = bf16[4,6,10,4,136]{3,0,4,2,1:T(4,128)(2,1)} pad(bf16[4,6,10,4,128]{3,0,4,2,1:T(4,128)(2,1)S(1)} %fusion.50, bf16[]{:T(256)} %constant.18), padding=0_0x0_0x0_0x0_0x1_7 | pad | bytes 506882 | tf_op jit(solution)/shard_map/concatenate | solution.py:13
  42.9 14.4 %copy.66 = bf16[4,6,10,4,8,17]{5,4,3,2,1,0:T(8,128)(2,1)S(1)} copy(bf16[4,6,10,4,8,17]{3,0,5,4,2,1:T(4,128)(2,1)} %bitcast.87) | data formatting | bytes 522240 | tf_op jit(solution)/shard_map/conv_general_dilated | solution.py:30
  57.8 2.6 fusion.23
  60.5 3.4 copy.67
  63.9 11.0 %add_multiply_fusion = (f32[4,8,32,17,32]{4,2,3,1,0:T(8,128)}, f32[4,8,32,17,32]{4,2,3,1,0:T(8,128)S(1)}) fusion(f32[32]{0:T(128)S(1)} %copy-done.10, pred[32,17]{0,1:T(8,128)(4,1)S(1)} %copy-done.12, bf16[4,6,10,32,19]{3,0,4,2,1:T(4,128)(2,1)S(1)} %copy.67, bf16[3,3,3,4,32]{4,3,2,1,0:T(4,128)(2,1)S(1)} %copy-done.9), kind=kOutput, calls=%fused_computation | convolution fusion | flops 125894656 | bytes 4755872 | tf_op jit(solution)/shard_map/conv_general_dilated | solution.py:30
  74.9 5.2 %copy.68 = f32[4,8,32,17,32]{4,1,3,2,0:T(8,128)S(1)} copy(f32[4,8,32,17,32]{4,2,3,1,0:T(8,128)S(1)} %get-tuple-element.13) | data formatting | bytes 4456448 | tf_op jit(solution)/shard_map/jit(silu)/mul | solution.py:74
  80.1 3.9 slice.59
  83.9 9.4 %reduce_sum.43 = f32[4,32,2,4,64]{1,3,4,0,2:T(4,128)S(1)} reduce(f32[4,32,2,2,4,2,64,2]{1,5,4,7,6,0,3,2:T(2,128)} %bitcast.86, f32[]{:T(128)} %constant.5.clone.1), dimensions={3,5,7}, to_apply=%region_0.1 | reduce | flops 458752 | bytes 2359300 | tf_op jit(solution)/shard_map/reduce_sum | solution.py:54
  94.3 2.2 collective-permute-start.4
  96.5 2.1 collective-permute-start.5
  98.8 9.5 %all_to_all.27 = bf16[4,2,2048]{2,1,0:T(2,128)(2,1)S(1)} all-to-all(bf16[4,2,2048]{2,1,0:T(2,128)(2,1)S(1)} %reshape.96), channel_id=1, replica_groups=mesh['depth'=32,'height'=4,'batch'=2] {'height'}, dimensions={0} | all-to-all | bytes 65536 | tf_op jit(solution)/shard_map/all_to_all | solution.py:81
  108.9 2.2 collective-permute-start.6
  112.6 12.2 %copy.80 = f32[4,8,32,17,32]{4,1,3,2,0:T(8,128)} copy(f32[4,8,32,17,32]{4,2,3,1,0:T(8,128)} %get-tuple-element.12) | data formatting | bytes 4456448 | tf_op jit(solution)/shard_map/mul | solution.py:68
  128.1 2.4 add_multiply_fusion.1
  132.2 5.6 %collective-permute-start.8 = (bf16[4,64,1,4,64]{1,3,4,0,2:T(4,128)(2,1)S(1)}, bf16[4,64,1,4,64]{1,3,4,0,2:T(4,128)(2,1)S(1)}, u32[]{:S(2)}, u32[]{:S(2)}) collective-permute-start(bf16[4,64,1,4,64]{1,3,4,0,2:T(4,128)(2,1)S(1)} %get-tuple-element.20), channel_id=1, source_target_pairs={{0,8},{8,16},{16,24},{24,32},{32,40},{40,48},{48,56},{56,64},{64,7... | collective-permute-start | bytes 393224 | tf_op jit(solution)/shard_map/ppermute | solution.py:15
  141.6 4.2 all-to-all-start
  147.9 4.7 %collective-permute-start.10 = (bf16[4,64,4,1,64]{1,3,4,0,2:T(2,128)(2,1)S(1)}, bf16[4,64,4,1,64]{1,3,4,0,2:T(2,128)(2,1)}, u32[]{:S(2)}, u32[]{:S(2)}) collective-permute-start(bf16[4,64,4,1,64]{1,3,4,0,2:T(2,128)(2,1)S(1)} %get-tuple-element.16), channel_id=1, source_target_pairs={{0,2},{2,4},{4,6},{1,3},{3,5},{5,7},{8,10},{10,12},{12,14},{9,11},... | collective-permute-start | bytes 393224 | tf_op jit(solution)/shard_map/ppermute | solution.py:15
  153.9 6.6 %fusion.41 = f32[3,3,3,32,64]{4,3,2,1,0:T(8,128)} fusion(bf16[4,64,2,4,64]{1,3,4,0,2:T(4,128)(2,1)S(1)} %get-tuple-element.9, bf16[4,32,4,1,64]{1,0,4,3,2:T(4,128)(2,1)} %copy-done.7, bf16[4,32,1,4,64]{1,0,4,3,2:T(4,128)(2,1)S(1)} %collective-permute-done.5, bf16[4,32,2,4,64]{1,0,4,3,2:T(4,128)(2,1)S(1)} %fusion.40, ...), kind=kOutput, calls=%fused_computation.50 | convolution fusion | flops 226099200 | bytes 876544 | tf_op jit(solution)/shard_map/conv_general_dilated | solution.py:41
  161.3 3.7 collective-permute-done.11
  165.0 3.8 maximum_bitcast_fusion
  170.0 4.5 %fusion.33 = f32[2,4,32,9,32]{4,2,3,1,0:T(8,128)S(1)} fusion(bf16[3,3,3,32,64]{4,3,2,1,0:T(8,128)(2,1)S(1)} %copy-done, bf16[64,4,6,4,7,2]{0,4,3,5,2,1:T(8,128)(2,1)S(1)} %slice.69, bf16[64,4,6,4,8,9]{0,4,3,5,2,1:T(8,128)(2,1)S(1)} %copy.78, pred[32,9]{0,1:T(8,128)(4,1)S(1)} %copy-done.13), kind=kOutput, calls=%fused_computation.36 | convolution fusion | flops 258195456 | bytes 1462560 | tf_op jit(solution)/shard_map/conv_general_dilated | solution.py:30
  175.4 5.9 %broadcast_in_dim.8 = f32[4,32,2,2,4,2,64,2]{1,5,4,7,6,0,3,2:T(2,128)} broadcast(f32[4,32,2,4,64]{1,3,4,0,2:T(4,128)S(1)} %slice_bitcast_fusion.1), dimensions={0,1,2,4,6} | broadcast | bytes 2359296 | tf_op jit(solution)/shard_map/broadcast_in_dim | solution.py:59
  181.4 7.3 %convert_reduce_fusion = (f32[32]{0:T(128)S(1)}, bf16[4,32,4,8,128]{1,3,4,0,2:T(8,128)(2,1)S(1)}) fusion(f32[4,32,4,8,128]{1,3,4,0,2:T(8,128)} %bitcast.85, f32[4,8,4,136,32]{4,1,3,2,0:T(8,128)} %bitcast.83), kind=kLoop, calls=%fused_computation.7 | loop fusion | flops 2097120 | bytes 5243008 | tf_op jit(solution)/shard_map/reduce_sum | solution.py:91
  188.9 13.3 %fusion.5 = f32[3,3,3,4,32]{4,3,2,1,0:T(4,128)S(1)} fusion(bf16[4,32,4,8,128]{1,3,4,0,2:T(8,128)(2,1)S(1)} %get-tuple-element.11, bf16[4,4,6,1,128]{0,1,4,3,2:T(4,128)(2,1)S(1)} %copy-done.5, bf16[4,4,6,8,128]{0,1,4,3,2:T(4,128)(2,1)S(1)} %bitcast.89, bf16[4,4,6,1,128]{0,1,4,3,2:T(4,128)(2,1)S(1)} %copy-done.3), kind=kOutput, calls=%fused_computation.13 | convolution fusion | flops 113393664 | bytes 1308160 | tf_op jit(solution)/shard_map/conv_general_dilated | solution.py:41
  202.1 84.8 %all-reduce = (f32[3,3,3,4,32]{4,3,2,1,0:T(4,128)}, f32[32]{0:T(128)}, f32[64]{0:T(128)}) all-reduce(f32[3,3,3,4,32]{4,3,2,1,0:T(4,128)S(1)} %fusion.5, f32[32]{0:T(128)S(1)} %get-tuple-element.10, f32[64]{0:T(128)S(1)} %get-tuple-element.8), channel_id=1, replica_groups=mesh['depth'=32,'height'=4,'batch'=2] {'depth','height','batch'}, use_global_device_ids=true, to_apply=%region_3.4 | all-reduce | flops 3552 | bytes 28416 | tf_op jit(solution)/shard_map/psum | solution.py:92
  287.0 133.1 %all-reduce.3.cloned.1.call-done = f32[3,3,3,32,64]{4,3,2,1,0:T(8,128)} async-done(((f32[3,3,3,32,64]{4,3,2,1,0:T(8,128)}), f32[3,3,3,32,64]{4,3,2,1,0:T(8,128)}) %all-reduce.3.cloned.1.call-update) | async-done | bytes 221200 | tf_op jit(solution)/shard_map/psum | solution.py:92
  (91 shorter events, 24.8 us)
Async XLA Ops:
  7.2 120.8 %copy-start = (bf16[3,3,3,32,64]{4,3,2,1,0:T(8,128)(2,1)S(1)}, bf16[3,3,3,32,64]{4,3,2,1,0:T(8,128)(2,1)}, u32[]{:S(2)}) copy-start(bf16[3,3,3,32,64]{4,3,2,1,0:T(8,128)(2,1)} %param.9) | copy-start | bytes 331780
  8.0 6.4 %collective-permute-start = (bf16[4,4,1,8,128]{4,3,2,1,0:T(8,128)(2,1)S(1)}, bf16[4,4,1,8,128]{4,3,2,1,0:T(8,128)(2,1)S(1)}, u32[]{:S(2)}, u32[]{:S(2)}) collective-permute-start(bf16[4,4,1,8,128]{4,3,2,1,0:T(8,128)(2,1)S(1)} %get-tuple-element.27), channel_id=1, source_target_pairs={{0,8},{8,16},{16,24},{24,32},{32,40},{40,48},{48,56},{56,64},{64,7... | collective-permute-start | bytes 98312 | tf_op jit(solution)/shard_map/ppermute | solution.py:15
  12.5 5.2 %collective-permute-start.1 = (bf16[4,4,1,8,128]{4,3,2,1,0:T(8,128)(2,1)S(1)}, bf16[4,4,1,8,128]{4,3,2,1,0:T(8,128)(2,1)S(1)}, u32[]{:S(2)}, u32[]{:S(2)}) collective-permute-start(bf16[4,4,1,8,128]{4,3,2,1,0:T(8,128)(2,1)S(1)} %get-tuple-element.26), channel_id=1, source_target_pairs={{8,0},{16,8},{24,16},{32,24},{40,32},{48,40},{56,48},{64,56},{72,6... | collective-permute-start | bytes 98312 | tf_op jit(solution)/shard_map/ppermute | solution.py:17
  17.9 9.6 %collective-permute-start.2 = (bf16[4,4,6,1,128]{4,1,3,2,0:T(4,128)(2,1)S(1)}, bf16[4,4,6,1,128]{4,1,3,2,0:T(4,128)(2,1)S(1)}, u32[]{:S(2)}, u32[]{:S(2)}) collective-permute-start(bf16[4,4,6,1,128]{4,1,3,2,0:T(4,128)(2,1)S(1)} %copy.83), channel_id=1, source_target_pairs={{0,2},{2,4},{4,6},{1,3},{3,5},{5,7},{8,10},{10,12},{12,14},{9,11},... | collective-permute-start | bytes 73736 | tf_op jit(solution)/shard_map/ppermute | solution.py:15
  21.1 7.0 %collective-permute-start.3 = (bf16[4,4,6,1,128]{4,1,3,2,0:T(4,128)(2,1)S(1)}, bf16[4,4,6,1,128]{4,1,3,2,0:T(4,128)(2,1)S(1)}, u32[]{:S(2)}, u32[]{:S(2)}) collective-permute-start(bf16[4,4,6,1,128]{4,1,3,2,0:T(4,128)(2,1)S(1)} %copy.84), channel_id=1, source_target_pairs={{2,0},{4,2},{6,4},{3,1},{5,3},{7,5},{10,8},{12,10},{14,12},{11,9},... | collective-permute-start | bytes 73736 | tf_op jit(solution)/shard_map/ppermute | solution.py:17
  28.1 9.1 %copy-start.2 = (bf16[4,4,6,1,128]{0,1,4,3,2:T(4,128)(2,1)}, bf16[4,4,6,1,128]{0,1,4,3,2:T(4,128)(2,1)S(1)}, u32[]{:S(2)}) copy-start(bf16[4,4,6,1,128]{0,1,4,3,2:T(4,128)(2,1)S(1)} %copy.62) | copy-start | bytes 73732
  28.7 8.5 %copy-start.4 = (bf16[4,4,6,1,128]{0,1,4,3,2:T(4,128)(2,1)}, bf16[4,4,6,1,128]{0,1,4,3,2:T(4,128)(2,1)S(1)}, u32[]{:S(2)}) copy-start(bf16[4,4,6,1,128]{0,1,4,3,2:T(4,128)(2,1)S(1)} %copy.64) | copy-start | bytes 73732
  60.5 3.4 copy-start.9
  60.5 3.4 copy-start.10
  60.5 3.4 copy-start.12
  93.3 5.3 %copy-start.8 = (bf16[1,64,1,8,32]{1,4,3,2,0:T(8,128)(2,1)S(1)}, bf16[1,64,1,8,32]{1,4,3,2,0:T(8,128)(2,1)}, u32[]{:S(2)}) copy-start(bf16[1,64,1,8,32]{1,4,3,2,0:T(8,128)(2,1)} %param.11) | copy-start | bytes 98308
  94.3 14.1 %collective-permute-start.4 = (bf16[4,32,1,4,64]{1,0,4,3,2:T(4,128)(2,1)S(1)}, bf16[4,32,1,4,64]{1,0,4,3,2:T(4,128)(2,1)S(1)}, u32[]{:S(2)}, u32[]{:S(2)}) collective-permute-start(bf16[4,32,1,4,64]{1,0,4,3,2:T(4,128)(2,1)S(1)} %get-tuple-element.22), channel_id=1, source_target_pairs={{0,8},{8,16},{16,24},{24,32},{32,40},{40,48},{48,56},{56,64},{64,7... | collective-permute-start | bytes 196616 | tf_op jit(solution)/shard_map/ppermute | solution.py:15
  96.5 11.9 %collective-permute-start.5 = (bf16[4,32,1,4,64]{1,0,4,3,2:T(4,128)(2,1)S(1)}, bf16[4,32,1,4,64]{1,0,4,3,2:T(4,128)(2,1)S(1)}, u32[]{:S(2)}, u32[]{:S(2)}) collective-permute-start(bf16[4,32,1,4,64]{1,0,4,3,2:T(4,128)(2,1)S(1)} %get-tuple-element.23), channel_id=1, source_target_pairs={{8,0},{16,8},{24,16},{32,24},{40,32},{48,40},{56,48},{64,56},{72,6... | collective-permute-start | bytes 196616 | tf_op jit(solution)/shard_map/ppermute | solution.py:17
  108.9 15.8 %collective-permute-start.6 = (bf16[4,32,4,1,64]{1,0,4,3,2:T(4,128)(2,1)S(1)}, bf16[4,32,4,1,64]{1,0,4,3,2:T(4,128)(2,1)S(1)}, u32[]{:S(2)}, u32[]{:S(2)}) collective-permute-start(bf16[4,32,4,1,64]{1,0,4,3,2:T(4,128)(2,1)S(1)} %get-tuple-element.18), channel_id=1, source_target_pairs={{0,2},{2,4},{4,6},{1,3},{3,5},{5,7},{8,10},{10,12},{12,14},{9,11},... | collective-permute-start | bytes 196616 | tf_op jit(solution)/shard_map/ppermute | solution.py:15
  111.1 13.6 %collective-permute-start.7 = (bf16[4,32,4,1,64]{1,0,4,3,2:T(4,128)(2,1)S(1)}, bf16[4,32,4,1,64]{1,0,4,3,2:T(4,128)(2,1)S(1)}, u32[]{:S(2)}, u32[]{:S(2)}) collective-permute-start(bf16[4,32,4,1,64]{1,0,4,3,2:T(4,128)(2,1)S(1)} %get-tuple-element.19), channel_id=1, source_target_pairs={{2,0},{4,2},{6,4},{3,1},{5,3},{7,5},{10,8},{12,10},{14,12},{11,9},... | collective-permute-start | bytes 196616 | tf_op jit(solution)/shard_map/ppermute | solution.py:17
  124.7 2.7 copy-start.6
  124.7 2.7 copy-start.7
  127.4 0.7 copy-start.11
  127.4 0.7 copy-start.13
  132.2 13.6 %collective-permute-start.8 = (bf16[4,64,1,4,64]{1,3,4,0,2:T(4,128)(2,1)S(1)}, bf16[4,64,1,4,64]{1,3,4,0,2:T(4,128)(2,1)S(1)}, u32[]{:S(2)}, u32[]{:S(2)}) collective-permute-start(bf16[4,64,1,4,64]{1,3,4,0,2:T(4,128)(2,1)S(1)} %get-tuple-element.20), channel_id=1, source_target_pairs={{0,8},{8,16},{16,24},{24,32},{32,40},{40,48},{48,56},{56,64},{64,7... | collective-permute-start | bytes 393224 | tf_op jit(solution)/shard_map/ppermute | solution.py:15
  137.8 8.1 %collective-permute-start.9 = (bf16[4,64,1,4,64]{1,3,4,0,2:T(4,128)(2,1)S(1)}, bf16[4,64,1,4,64]{1,3,4,0,2:T(4,128)(2,1)S(1)}, u32[]{:S(2)}, u32[]{:S(2)}) collective-permute-start(bf16[4,64,1,4,64]{1,3,4,0,2:T(4,128)(2,1)S(1)} %get-tuple-element.21), channel_id=1, source_target_pairs={{8,0},{16,8},{24,16},{32,24},{40,32},{48,40},{56,48},{64,56},{72,6... | collective-permute-start | bytes 393224 | tf_op jit(solution)/shard_map/ppermute | solution.py:17
  141.6 18.9 %all-to-all-start = ((bf16[4,2,2048]{2,1,0:T(2,128)(2,1)}), bf16[4,2,2048]{2,1,0:T(2,128)(2,1)S(1)}, u32[]{:S(2)}, u32[]{:S(2)}) async-start(bf16[4,2,2048]{2,1,0:T(2,128)(2,1)} %reshape.94), calls=%async_computation | async-start | bytes 65536 | tf_op jit(solution)/shard_map/all_to_all | solution.py:80
  145.9 274.2 %all-reduce.3.cloned.1.call-start = ((), (), s32[]{:S(2)}) async-start(), calls=%async_computation.2 | async-start | bytes 884736 | tf_op jit(solution)/shard_map/psum | solution.py:92
  147.9 13.4 %collective-permute-start.10 = (bf16[4,64,4,1,64]{1,3,4,0,2:T(2,128)(2,1)S(1)}, bf16[4,64,4,1,64]{1,3,4,0,2:T(2,128)(2,1)}, u32[]{:S(2)}, u32[]{:S(2)}) collective-permute-start(bf16[4,64,4,1,64]{1,3,4,0,2:T(2,128)(2,1)S(1)} %get-tuple-element.16), channel_id=1, source_target_pairs={{0,2},{2,4},{4,6},{1,3},{3,5},{5,7},{8,10},{10,12},{12,14},{9,11},... | collective-permute-start | bytes 393224 | tf_op jit(solution)/shard_map/ppermute | solution.py:15
  152.6 12.4 %collective-permute-start.11 = (bf16[4,64,4,1,64]{1,3,4,0,2:T(2,128)(2,1)S(1)}, bf16[4,64,4,1,64]{1,3,4,0,2:T(2,128)(2,1)}, u32[]{:S(2)}, u32[]{:S(2)}) collective-permute-start(bf16[4,64,4,1,64]{1,3,4,0,2:T(2,128)(2,1)S(1)} %get-tuple-element.17), channel_id=1, source_target_pairs={{2,0},{4,2},{6,4},{3,1},{5,3},{7,5},{10,8},{12,10},{14,12},{11,9},... | collective-permute-start | bytes 393224 | tf_op jit(solution)/shard_map/ppermute | solution.py:17
  175.4 13.3 %slice-start = ((s8[6291456]{0:T(1024)(128)(4,1)}), s8[2097152]{0:T(1024)(128)(4,1)S(1)}, s32[]{:S(2)}) async-start(s8[6291456]{0:T(1024)(128)(4,1)} %bitcast.88), calls=%async_computation.3 | async-start | bytes 4194304
  181.4 7.3 %slice-start.1 = ((s8[6291456]{0:T(1024)(128)(4,1)}), s8[4194304]{0:T(1024)(128)(4,1)S(1)}, s32[]{:S(2)}) async-start(s8[6291456]{0:T(1024)(128)(4,1)} %bitcast.88), calls=%async_computation.4 | async-start | bytes 8388608
  181.4 7.3 %copy-start.3 = (bf16[4,4,6,1,128]{0,1,4,3,2:T(4,128)(2,1)S(1)}, bf16[4,4,6,1,128]{0,1,4,3,2:T(4,128)(2,1)}, u32[]{:S(2)}) copy-start(bf16[4,4,6,1,128]{0,1,4,3,2:T(4,128)(2,1)} %copy-done.2) | copy-start | bytes 73732
  181.4 7.5 %copy-start.5 = (bf16[4,4,6,1,128]{0,1,4,3,2:T(4,128)(2,1)S(1)}, bf16[4,4,6,1,128]{0,1,4,3,2:T(4,128)(2,1)}, u32[]{:S(2)}) copy-start(bf16[4,4,6,1,128]{0,1,4,3,2:T(4,128)(2,1)} %copy-done.4) | copy-start | bytes 73732
  188.9 233.0 %copy-start.1 = (bf16[3,3,3,32,64]{4,3,2,1,0:T(8,128)(2,1)S(1)}, bf16[3,3,3,32,64]{4,3,2,1,0:T(8,128)(2,1)}, u32[]{:S(2)}) copy-start(bf16[3,3,3,32,64]{4,3,2,1,0:T(8,128)(2,1)} %param.9) | copy-start | bytes 331780
Sparse Core Ops, SparseCore 0:
  160.7 259.3 all-reduce.2
where the time goes:
time: 437 us; the launch traced here: 429 us
  waiting for transfers between devices  139 us (32%)
  blocking collectives  94.3 us (22%)
  local copies, waits for them, and re-layouts  69.4 us (16%)
  matrix products  37.9 us (9%)
  other arithmetic  36.8 us (8%)
  starting transfers between devices  36.4 us (8%)
  between operations  14.8 us (3%)
    psum x1, waiting for transfers between devices, per_device(): lax.psum((first_kgrad, first_bgrad, second_kgrad, second_bgrad), ('depth'...  133 us
    psum x1, blocking collectives, per_device(): lax.psum((first_kgrad, first_bgrad, second_kgrad, second_bgrad), ('depth'...  84.8 us
    ppermute x6, starting transfers between devices, padded_2(): lax.ppermute(tail, axis, [(i, (i + 1) % count) for i in range(ends)])  22.3 us
    conv_general_dilated x2, matrix products, kernel_grad(): lax.conv_general_dilated(padded, cotangent, (1, 1, 1), ((0, 0), (0, 0), (...  19.9 us
    conv_general_dilated x7, local copies, waits for them, and re-layouts, conv_valid(): lax.conv_general_dilated(padded, kernel, (1, 1, 1), ((0, 0), (0, 0), (1,...  19.2 us
    conv_general_dilated x3, matrix products, conv_valid(): lax.conv_general_dilated(padded, kernel, (1, 1, 1), ((0, 0), (0, 0), (1,...  18 us
    concatenate x4, other arithmetic, padded_2(): jnp.concatenate([lax.ppermute(tail, axis, [(i, (i + 1) % count) for i in...  15 us
    mul x2, local copies, waits for them, and re-layouts, slope(): return sigma * (1.0 + values * (1.0 - sigma))  12.9 us
  transfers between devices with their start and end apart: 14, of which 3 were waited for; matrix products, arithmetic and copies ran while one was open for 16% of the time, Pallas kernels for 0%

commit v1 on v0

v1 whole, which is shorter than its diff:
```python
import jax
import jax.numpy as jnp
import numpy as np
from jax import lax
from jax.experimental import pallas as pl
from jax.experimental.pallas import tpu as pltpu
from jax.sharding import PartitionSpec as P

F32 = jnp.float32
BF16 = jnp.bfloat16
AXES = ("depth", "height", "batch")
ROWS = 512
NT = (((1,), (1,)), ((), ()))


def window_index(a4, b4, k4, ch):
    half, low = divmod(a4, 2)
    hb, hs = ((1, 1), (0, 0), (1, 0), (0, 1))[b4]
    wb, ws = ((1, 1), (0, 0), (1, 0), (0, 1))[k4]
    return half * 128 + (hs * 2 + ws) * 32 + hb * 16 + wb * 8 + low * 4 + ch


def select_taps():
    sel = np.zeros((128, 2048), np.float32)
    for pos in range(8):
        dz, dy, dx = pos // 4, pos // 2 % 2, pos % 2
        for a in range(3):
            for b in range(3):
                for c in range(3):
                    for ch in range(4):
                        tap = ((a * 3 + b) * 3 + c) * 4 + ch
                        sel[tap, pos * 256 + window_index(a + dz, b + dy, c + dx, ch)] = 1.0
    return sel


def split_width():
    out = np.zeros((256, 256), np.float32)
    for row in range(2):
        for cell in range(128):
            out[row * 128 + cell, (cell % 2) * 128 + row * 64 + cell // 2] = 1.0
    return out


def pool_lanes():
    out = np.zeros((512, 128), np.float32)
    for lane in range(512):
        out[lane, lane // 128 * 32 + lane % 64 // 2] = 0.125
    return out


def dot(a, b):
    return jnp.dot(a, b, preferred_element_type=F32)


def dot_nt(a, b):
    return lax.dot_general(a, b, NT, preferred_element_type=F32)


def prep_kernel(k1_ref, k2_ref, sel_ref, w1_ref, w2_ref, wb_ref):
    flat = lax.dot_general(k1_ref[...], sel_ref[...], (((0,), (0,)), ((), ())), preferred_element_type=F32)
    for pos in range(8):
        w1_ref[pos * 32 : pos * 32 + 32, :] = (0.5 * flat[:, pos * 256 : pos * 256 + 256]).astype(BF16)
    rows = lax.broadcasted_iota(jnp.int32, (64, 64), 0)
    cols = lax.broadcasted_iota(jnp.int32, (64, 64), 1)
    half_eye = jnp.where(rows == cols, 0.5, 0.0).astype(BF16)
    for a in range(3):
        w2_ref[a] = dot_nt(half_eye, k2_ref[a * 288 : a * 288 + 288, :]).astype(BF16)
        blocks = []
        for b in range(3):
            for c in range(3):
                at = ((a * 3 + 2 - b) * 3 + 2 - c) * 32
                blocks.append(k2_ref[at : at + 32, :].astype(F32))
        wb_ref[a * 32 : a * 32 + 32, :] = jnp.concatenate(blocks, axis=1).astype(BF16)


def lane_masks(rows):
    lane = lax.broadcasted_iota(jnp.int32, (rows, 128), 1)
    cell = lane % 64
    return lane < 64, cell != 0, cell != 63


def width_shift(tiles, step, masks):
    _, not_first, not_last = masks
    if step < 0:
        return [jnp.where(not_first, pltpu.roll(t, 1, 1), 0.0) for t in tiles]
    return [jnp.where(not_last, pltpu.roll(t, 127, 1), 0.0) for t in tiles]


def height_shift(tiles, steps, masks):
    low = masks[0]
    swapped = [pltpu.roll(t, 64, 1) for t in tiles]
    zero = jnp.zeros_like(tiles[0])
    out = []
    for step in steps:
        if step < 0:
            before = [zero] + swapped[:-1]
            out.append([jnp.where(low, before[i], swapped[i]) for i in range(len(tiles))])
        else:
            after = swapped[1:] + [zero]
            out.append([jnp.where(low, swapped[i], after[i]) for i in range(len(tiles))])
    return out


def store_shifts(tiles, put, masks):
    for c in range(3):
        moved = tiles if c == 1 else width_shift(tiles, c - 1, masks)
        before, after = height_shift(moved, (-1, 1), masks)
        for b, group in enumerate((before, moved, after)):
            for t in range(8):
                put(b * 3 + c, t, group[t])


def main_kernel(
    own_ref, chip_ref, link_ref, dg_ref, w1_ref, w2_ref, wb_ref, b1_ref, b2_ref, sel_ref, split_ref, pool_ref,
    deep_ref, packed_ref,
    f_ref, l_ref, g_ref, x_ref, slope_ref, y_ref, z_ref, g2_ref, gz_ref, back_ref, ds_ref, g1_ref, kg_ref,
):
    place = lax.axis_index("depth")
    parity = place % 2
    keep_low = jnp.where(place > 0, 1.0, 0.0).astype(F32)
    keep_high = jnp.where(place < lax.axis_size("depth") - 1, 1.0, 0.0).astype(F32)

    def fill(ref, plane, at):
        for y in range(4):
            for ch in range(4):
                f_ref[pl.ds((at * 4 + ch) * 32 + y * 8, 8), :] = ref[y, ch, plane].astype(F32)

    for plane in range(4):
        fill(own_ref, plane, 3 + plane)

    @pl.when(parity == 0)
    def _():
        for plane in range(3):
            fill(link_ref, plane + 1, plane)
            fill(chip_ref, plane, 7 + plane)

    @pl.when(parity == 1)
    def _():
        for plane in range(3):
            fill(chip_ref, plane + 1, plane)
            fill(link_ref, plane, 7 + plane)

    for hb in range(2):
        for qq in range(8):
            for low in range(2):
                l_ref[pl.ds((hb * 8 + qq) * 40, 40), low * 128 : low * 128 + 128] = f_ref[
                    pl.ds(4 * qq + 2 * low + hb, 40, stride=32), :
                ]
    g_ref[...] = dot(l_ref[...].astype(BF16), split_ref[...])

    masks8 = lane_masks(8)
    for pair in range(5):
        for hb in range(2):
            still, moved = [], []
            for wb in range(2):
                tiles = [
                    g_ref[(hb * 8 + qq) * 40 + pair * 8 : (hb * 8 + qq) * 40 + pair * 8 + 8, wb * 128 : wb * 128 + 128]
                    for qq in range(8)
                ]
                still.append(tiles)
                moved.append(width_shift(tiles, 1 if wb == 0 else -1, masks8))
            for ws, group in enumerate((still, moved)):
                step = 1 if hb == 0 else -1
                raised = [height_shift(group[wb], (step,), masks8)[0] for wb in range(2)]
                for hs, part in enumerate((group, raised)):
                    at = pair * 128 + (hs * 2 + ws) * 32 + hb * 16
                    for qq in range(8):
                        both = jnp.concatenate([part[0][qq], part[1][qq]], axis=0)
                        x_ref[at : at + 16, qq * 128 : qq * 128 + 128] = both.astype(BF16)

    bias1 = jnp.broadcast_to(0.5 * b1_ref[...], (32, 256))
    for plane in range(4):
        for t in range(4):
            lanes = slice(t * 256, t * 256 + 256)
            pre = dot(w1_ref[...], x_ref[plane * 128 : plane * 128 + 256, lanes])
            total = jnp.zeros((32, 256), F32)
            for pos in range(8):
                u = pre[pos * 32 : pos * 32 + 32] + bias1
                tanh = jnp.tanh(u)
                w = 1.0 + tanh
                silu = u * w
                slope_ref[plane, pos * 32 : pos * 32 + 32, lanes] = w + silu * (1.0 - tanh)
                total = total + silu
            scale = 0.125
            if plane == 0:
                scale = 0.125 * keep_low
            if plane == 3:
                scale = 0.125 * keep_high
            y_ref[plane, :, lanes] = total * scale

    masks32 = lane_masks(32)
    for plane in range(4):

        def put(at, t, value, plane=plane):
            z_ref[plane, at * 32 : at * 32 + 32, t * 128 : t * 128 + 128] = value.astype(BF16)

        store_shifts([y_ref[plane, :, t * 128 : t * 128 + 128] for t in range(8)], put, masks32)

    bias2 = jnp.broadcast_to(0.5 * b2_ref[...], (64, 256))
    sum2 = jnp.zeros((64, 128), F32)
    for plane in range(2):
        for t in range(4):
            lanes = slice(t * 256, t * 256 + 256)
            if plane == 0 and t % 2 == 0:
                wide = dot_nt(dg_ref[:, t * 64 : t * 64 + 128], pool_ref[...])
                g2_ref[0, :, t * 256 : t * 256 + 512] = wide
                g2_ref[1, :, t * 256 : t * 256 + 512] = wide
            u = bias2
            for a in range(3):
                u = u + dot(w2_ref[a], z_ref[plane + a, :, lanes])
            tanh = jnp.tanh(u)
            w = 1.0 + tanh
            silu = u * w
            if plane == 0:
                ds_ref[:, lanes] = silu
            else:
                ds_ref[:, lanes] = ds_ref[:, lanes] + silu
            grad = (0.5 * g2_ref[plane, :, lanes]) * (w + silu * (1.0 - tanh))
            g2_ref[plane, :, lanes] = grad
            sum2 = sum2 + grad[:, :128] + grad[:, 128:]

    for half in range(2):
        part = ds_ref[:, half * 512 : half * 512 + 512]
        high = part.astype(BF16)
        low = (part - high.astype(F32)).astype(BF16)
        deep = dot(high, pool_ref[...]) + dot(low, pool_ref[...])
        deep_ref[:, half * 128 : half * 128 + 128] = deep.astype(BF16)

    masks64 = lane_masks(64)
    for plane in range(2):

        def put(at, t, value, plane=plane):
            gz_ref[plane, at * 64 : at * 64 + 64, t * 128 : t * 128 + 128] = value.astype(BF16)

        store_shifts([g2_ref[plane, :, t * 128 : t * 128 + 128] for t in range(8)], put, masks64)

    for a in range(3):
        total = dot_nt(z_ref[a], gz_ref[0, 256:320, :]) + dot_nt(z_ref[a + 1], gz_ref[1, 256:320, :])
        kg_ref[a * 288 : a * 288 + 288, :] = total

    for t in range(4):
        lanes = slice(t * 256, t * 256 + 256)
        one = dot(wb_ref[...], gz_ref[0, :, lanes])
        two = dot(wb_ref[...], gz_ref[1, :, lanes])
        back_ref[0, :, lanes] = one[0:32] * (0.0625 * keep_low)
        back_ref[1, :, lanes] = (one[32:64] + two[0:32]) * 0.0625
        back_ref[2, :, lanes] = (one[64:96] + two[32:64]) * 0.0625
        back_ref[3, :, lanes] = two[64:96] * (0.0625 * keep_high)

    sum1 = jnp.zeros((32, 128), F32)
    grads = jnp.zeros((256, 256), F32)
    for plane in range(4):
        for t in range(4):
            lanes = slice(t * 256, t * 256 + 256)
            back = back_ref[plane, :, lanes]
            for pos in range(8):
                grad = back * slope_ref[plane, pos * 32 : pos * 32 + 32, lanes]
                g1_ref[pos * 32 : pos * 32 + 32, lanes] = grad.astype(BF16)
                sum1 = sum1 + grad[:, :128] + grad[:, 128:]
        grads = grads + dot_nt(g1_ref[...], x_ref[plane * 128 : plane * 128 + 256, :])

    first = jnp.zeros((128, 32), F32)
    for pos in range(8):
        part = grads[pos * 32 : pos * 32 + 32]
        high = part.astype(BF16)
        low = (part - high.astype(F32)).astype(BF16)
        sel = sel_ref[:, pos * 256 : pos * 256 + 256]
        first = first + dot_nt(sel, high) + dot_nt(sel, low)

    ones = jnp.ones((8, 128), F32)
    bias_rows = [
        lax.dot_general(ones, s, NT, precision=lax.Precision.HIGHEST, preferred_element_type=F32) for s in (sum1, sum2)
    ]
    packed_ref[0:432, :] = jnp.concatenate([kg_ref[0:432, :], kg_ref[432:864, :]], axis=1)
    packed_ref[432:464, :] = jnp.concatenate([first[32 * i : 32 * i + 32] for i in range(4)], axis=1)
    packed_ref[464:472, :] = jnp.concatenate(bias_rows + [jnp.zeros((8, 32), F32)], axis=1)
    packed_ref[472:512, :] = jnp.zeros((40, 128), F32)


def sum_kernel(in_ref, out_ref):
    total = in_ref[0:8, :]
    for i in range(1, ROWS // 8):
        total = total + in_ref[8 * i : 8 * i + 8, :]
    total = total + pltpu.roll(total, 4, 0)
    total = total + pltpu.roll(total, 2, 0)
    for i in range(ROWS // 8):
        out_ref[8 * i : 8 * i + 8, :] = total


def unpack_kernel(in_ref, second_ref, first_ref, bias1_ref, bias2_ref):
    second_ref[0:432, :] = in_ref[0:432, 0:64]
    second_ref[432:864, :] = in_ref[0:432, 64:128]
    for g in range(4):
        for m in range(8):
            if 8 * g + m < 27:
                first_ref[8 * g + m] = in_ref[432 + 4 * m : 436 + 4 * m, 32 * g : 32 * g + 32]
    bias1_ref[...] = in_ref[464:465, 0:32]
    bias2_ref[...] = in_ref[464:465, 32:96]


def vmem(count):
    return [pl.BlockSpec(memory_space=pltpu.VMEM) for _ in range(count)]


def call(kernel, outs, inputs, scratch=(), limit=None):
    params = pltpu.CompilerParams(vmem_limit_bytes=limit) if limit else None
    return pl.pallas_call(
        kernel,
        out_shape=outs,
        in_specs=vmem(len(inputs)),
        out_specs=vmem(len(outs)),
        scratch_shapes=[pltpu.VMEM(shape, dtype) for shape, dtype in scratch],
        compiler_params=params,
    )(*inputs)


def shape(dims, dtype):
    return jax.ShapeDtypeStruct(dims, dtype)


def per_device(volumes, first_kernel, first_bias, second_kernel, second_bias, deep_grad):
    count = lax.axis_size("depth")
    own = lax.all_to_all(volumes, "height", split_axis=0, concat_axis=0, tiled=True)
    chip = lax.ppermute(own, "depth", [(i, i ^ 1) for i in range(count)])
    pairs = [(i, i + 1) for i in range(1, count - 1, 2)]
    link = lax.ppermute(own, "depth", pairs + [(j, i) for i, j in pairs])

    sel = jnp.asarray(select_taps(), BF16)
    k1 = jnp.pad(first_kernel.reshape(108, 32), ((0, 20), (0, 0)))
    w1, w2, wb = call(
        prep_kernel,
        (shape((256, 256), BF16), shape((3, 64, 288), BF16), shape((96, 576), BF16)),
        (k1, second_kernel.reshape(864, 64), sel),
    )
    deep, packed = call(
        main_kernel,
        (shape((64, 256), BF16), shape((ROWS, 128), F32)),
        (
            own, chip, link, deep_grad.reshape(64, 256), w1, w2, wb,
            first_bias.reshape(32, 1), second_bias.reshape(64, 1), sel,
            jnp.asarray(split_width(), BF16), jnp.asarray(pool_lanes(), BF16),
        ),
        (
            ((1280, 128), F32), ((640, 256), F32), ((640, 256), F32), ((640, 1024), BF16),
            ((4, 256, 1024), F32), ((4, 32, 1024), F32), ((4, 288, 1024), BF16), ((2, 64, 1024), F32),
            ((2, 576, 1024), BF16), ((4, 32, 1024), F32), ((64, 1024), F32), ((256, 1024), BF16), ((864, 64), F32),
        ),
        40 * 1024 * 1024,
    )
    pieces = lax.all_to_all(packed.reshape(256, 2, 128), AXES, split_axis=0, concat_axis=0, tiled=True)
    (copies,) = call(sum_kernel, (shape((ROWS, 128), F32),), (pieces.reshape(ROWS, 128),))
    whole = lax.all_to_all(copies.reshape(256, 2, 128), AXES, split_axis=0, concat_axis=0, tiled=True)
    second, first, bias1, bias2 = call(
        unpack_kernel,
        (shape((864, 64), F32), shape((27, 4, 32), F32), shape((1, 32), F32), shape((1, 64), F32)),
        (whole.reshape(ROWS, 128),),
    )
    return (
        deep.reshape(1, 64, 1, 8, 32),
        first.reshape(3, 3, 3, 4, 32),
        bias1.reshape(32),
        second.reshape(3, 3, 3, 32, 64),
        bias2.reshape(64),
    )


def solution(mesh):
    in_specs = (
        P("batch", None, "depth", "height", None),
        P(),
        P(),
        P(),
        P(),
        P(("batch", "height"), None, "depth", None, None),
    )
    out_specs = (P(("batch", "height"), None, "depth", None, None), P(), P(), P(), P())
    return jax.shard_map(
        per_device, mesh=mesh, in_specs=in_specs, out_specs=out_specs, check_vma=False
    )
```

time: 437 us -> 84.2 us (0.19); the launches traced: 429 us -> 83.7 us
  waiting for transfers between devices: 139 us -> 14.9 us
  local copies, waits for them, and re-layouts: 69.4 us -> 5.09 us
  blocking collectives: 94.3 us -> 39.8 us
  matrix products: 37.9 us -> 0 us
  other arithmetic: 36.8 us -> 0 us
  starting transfers between devices: 36.4 us -> 10.5 us
  between operations: 14.8 us -> 0.75 us
  Pallas kernels: 0 us -> 12.6 us
    psum x1 -> x0, waiting for transfers between devices: 133 us -> none  [per_device(): lax.psum((first_kgrad, first_bgrad, second_kgrad, second_bgrad), ('depth'...]
    psum x1 -> x0, blocking collectives: 84.8 us -> none  [per_device(): lax.psum((first_kgrad, first_bgrad, second_kgrad, second_bgrad), ('depth'...]
    conv_general_dilated x5 -> x0, matrix products: 37.9 us -> none  [the longest x2 19.9 us: kernel_grad(): lax.conv_general_dilated(padded, cotangent, (1, 1, 1), ((0, 0), (0, 0), (...]
    all_to_all x1 -> x2, blocking collectives: 9.52 us -> 39.8 us  [the longest x1 29.8 us: per_device(): lax.all_to_all(packed.reshape(256, 2, 128), AXES, split_axis=0, concat_ax...]
    ppermute x12 -> x2, starting transfers between devices: 32.2 us -> 5.32 us  [the longest x1 5.23 us: per_device(): link = lax.ppermute(own, 'depth', pairs + [(j, i) for i, j in pairs])]
    mul x7 -> x0, local copies, waits for them, and re-layouts: 22.9 us -> none  [the longest x2 12.9 us: slope(): return sigma * (1.0 + values * (1.0 - sigma))]
    conv_general_dilated x7 -> x0, local copies, waits for them, and re-layouts: 19.2 us -> none  [conv_valid(): lax.conv_general_dilated(padded, kernel, (1, 1, 1), ((0, 0), (0, 0), (1,...]
    reduce_sum x4 -> x0, other arithmetic: 17.9 us -> none  [the longest x2 10 us: pooled(): return jnp.mean(blocks, axis=(3, 5, 7))]
  transfers between devices with their start and end apart: 14 -> 3, of which waited for: 3 -> 1; matrix products, arithmetic and copies ran while one was open for 16% -> 2% of each run, Pallas kernels for 0% -> 3%
where the time goes in v1:
time: 84.2 us; the launch traced here: 83.7 us
  blocking collectives  39.8 us (47%)
  waiting for transfers between devices  14.9 us (18%)
  Pallas kernels  12.6 us (15%)
  starting transfers between devices  10.5 us (12%)
  local copies, waits for them, and re-layouts  5.09 us (6%)
    all_to_all x1, blocking collectives, per_device(): lax.all_to_all(packed.reshape(256, 2, 128), AXES, split_axis=0, concat_ax...  29.8 us
    all_to_all x1, waiting for transfers between devices, per_device(): lax.all_to_all(copies.reshape(256, 2, 128), AXES, split_axis=0, concat_ax...  14.9 us
    pallas_call x4, Pallas kernels, call(): pl.pallas_call(kernel, out_shape=outs, in_specs=vmem(len(inputs)), out_sp...  12.6 us
    all_to_all x1, blocking collectives, per_device(): lax.all_to_all(volumes, 'height', split_axis=0, concat_axis=0, tiled=True)  9.98 us
    ppermute x1, starting transfers between devices, per_device(): link = lax.ppermute(own, 'depth', pairs + [(j, i) for i, j in pairs])  5.23 us
    all_to_all x1, starting transfers between devices, per_device(): lax.all_to_all(copies.reshape(256, 2, 128), AXES, split_axis=0, concat_ax...  5.17 us
    unnamed x22, local copies, waits for them, and re-layouts  3.43 us
  transfers between devices with their start and end apart: 3, of which 1 were waited for; matrix products, arithmetic and copies ran while one was open for 2% of the time, Pallas kernels for 3%

profile of v1, /device:TPU:1, one launch (start us, length us, event | category | flops | bytes accessed | tf_op | source)
XLA Modules:
  0.0 83.7 jit_solution(15174600651056200990)
XLA Ops:
  0.6 0.0 copy-start.10
  0.6 0.0 copy-start.8
  0.7 0.0 copy-start.9
  0.7 10.0 %all_to_all.15.own_ref = bf16[4,4,4,8,128]{4,3,2,1,0:T(8,128)(2,1)S(1)} all-to-all(bf16[4,4,4,8,128]{4,3,2,1,0:T(8,128)(2,1)} %param.9), channel_id=1, replica_groups=mesh['depth'=32,'height'=4,'batch'=2] {'height'}, dimensions={0} | all-to-all | bytes 262144 | tf_op jit(solution)/shard_map/all_to_all | solution.py:323
  10.6 5.2 %collective-permute-start.1 = (bf16[4,4,4,8,128]{4,3,2,1,0:T(8,128)(2,1)S(1)}, bf16[4,4,4,8,128]{4,3,2,1,0:T(8,128)(2,1)S(1)}, u32[]{:S(2)}, u32[]{:S(2)}) collective-permute-start(bf16[4,4,4,8,128]{4,3,2,1,0:T(8,128)(2,1)S(1)} %all_to_all.15.own_ref), channel_id=1, source_target_pairs={{8,16},{24,32},{40,48},{56,64},{72,80},{88,96},{104,112},{120,128}... | collective-permute-start | bytes 393224 | tf_op jit(solution)/shard_map/ppermute | solution.py:326
  15.9 0.1 collective-permute-start
  16.0 0.0 copy-done.10
  16.0 0.0 copy-start
  16.0 0.1 copy.19.b1_ref
  16.1 0.0 copy-done.8
  16.1 0.0 copy-done.9
  16.1 0.1 copy.20.b2_ref
  16.2 0.0 copy-done.7
  16.2 0.1 copy.18.dg_ref
  16.3 0.6 pad.4.k1_ref
  17.0 2.2 %shard_map.128 = (bf16[256,256]{1,0:T(8,128)(2,1)}, bf16[3,64,288]{2,1,0:T(8,128)(2,1)}, bf16[96,576]{1,0:T(8,128)(2,1)}) custom-call(bf16[128,32]{1,0:T(8,128)(2,1)} %pad.4.k1_ref, bf16[864,64]{1,0:T(8,128)(2,1)} %bitcast.17, bf16[128,2048]{1,0:T(8,128)(2,1)} %constant.9.clone.sel_ref), custom_call_target="tpu_custom_call" | custom-call | tf_op jit(solution)/shard_map/pallas_call | solution.py:307
  19.2 0.0 collective-permute-done.1.link_ref
  19.2 0.0 collective-permute-done.chip_ref
  19.2 0.0 copy-done
  19.2 0.0 copy-done.2
  19.2 0.0 copy-start.1
  19.2 0.9 %copy-done.1 = bf16[3,64,288]{2,1,0:T(8,128)(2,1)S(1)} copy-done((bf16[3,64,288]{2,1,0:T(8,128)(2,1)S(1)}, bf16[3,64,288]{2,1,0:T(8,128)(2,1)}, u32[]{:S(2)}) %copy-start.1) | copy-done | bytes 110616
  20.1 0.9 %copy-done.4 = bf16[256,256]{1,0:T(8,128)(2,1)S(1)} copy-done((bf16[256,256]{1,0:T(8,128)(2,1)S(1)}, bf16[256,256]{1,0:T(8,128)(2,1)}, u32[]{:S(2)}) %copy-start.4) | copy-done | bytes 131096
  21.0 0.9 %copy-done.5 = bf16[96,576]{1,0:T(8,128)(2,1)S(1)} copy-done((bf16[96,576]{1,0:T(8,128)(2,1)S(1)}, bf16[96,576]{1,0:T(8,128)(2,1)}, u32[]{:S(2)}) %copy-start.5) | copy-done | bytes 110616
  21.9 6.8 %shard_map.129 = (bf16[64,256]{1,0:T(8,128)(2,1)S(1)}, f32[512,128]{1,0:T(8,128)S(1)}) custom-call(bf16[4,4,4,8,128]{4,3,2,1,0:T(8,128)(2,1)S(1)} %all_to_all.15.own_ref, bf16[4,4,4,8,128]{4,3,2,1,0:T(8,128)(2,1)S(1)} %collective-permute-done.chip_ref, bf16[4,4,4,8,128]{4,3,2,1,0:T(8,128)(2,1)S(1)} %collective-permute-done.1.link_ref, ...), custom_call_target="tpu_custom_call" | custom-call | tf_op jit(solution)/shard_map/pallas_call | solution.py:307
  28.7 29.8 %all_to_all.16 = f32[256,2,128]{2,1,0:T(2,128)} all-to-all(f32[256,2,128]{2,1,0:T(2,128)S(1)} %bitcast.13), channel_id=1, replica_groups=mesh['depth'=32,'height'=4,'batch'=2] {'depth','height','batch'}, dimensions={0} | all-to-all | bytes 524288 | tf_op jit(solution)/shard_map/all_to_all | solution.py:350
  58.6 1.7 %shard_map.130 = f32[512,128]{1,0:T(8,128)} custom-call(f32[512,128]{1,0:T(8,128)} %bitcast.16), custom_call_target="tpu_custom_call" | custom-call | tf_op jit(solution)/shard_map/pallas_call | solution.py:307
  60.3 5.2 %all-to-all-start.2 = ((f32[256,2,128]{2,1,0:T(2,128)}), f32[256,2,128]{2,1,0:T(2,128)S(1)}, u32[]{:S(2)}, u32[]{:S(2)}) async-start(f32[256,2,128]{2,1,0:T(2,128)} %bitcast.15), calls=%async_computation.2 | async-start | bytes 524288 | tf_op jit(solution)/shard_map/all_to_all | solution.py:352
  65.5 0.7 copy.21
  66.2 14.9 %all-to-all-done.2 = f32[256,2,128]{2,1,0:T(2,128)S(1)} async-done(((f32[256,2,128]{2,1,0:T(2,128)}), f32[256,2,128]{2,1,0:T(2,128)S(1)}, u32[]{:S(2)}, u32[]{:S(2)}) %all-to-all-start.2) | async-done | bytes 262176 | tf_op jit(solution)/shard_map/all_to_all | solution.py:352
  81.1 0.7 copy-done.6
  81.8 1.9 %shard_map.131 = (f32[864,64]{1,0:T(8,128)}, f32[27,4,32]{2,1,0:T(4,128)}, f32[1,32]{1,0:T(1,128)}, f32[1,64]{1,0:T(1,128)}) custom-call(f32[512,128]{1,0:T(8,128)} %bitcast.14), custom_call_target="tpu_custom_call" | custom-call | tf_op jit(solution)/shard_map/pallas_call | solution.py:307
  (8 shorter events, 0.0 us)
Async XLA Ops:
  0.6 15.4 %copy-start.10 = (f32[32]{0:T(128)S(1)}, f32[32]{0:T(128)}, u32[]{:S(2)}) copy-start(f32[32]{0:T(128)} %param.11) | copy-start | bytes 388
  0.6 15.5 %copy-start.8 = (bf16[3,3,3,4,32]{4,3,2,1,0:T(4,128)(2,1)S(1)}, bf16[3,3,3,4,32]{4,3,2,1,0:T(4,128)(2,1)}, u32[]{:S(2)}) copy-start(bf16[3,3,3,4,32]{4,3,2,1,0:T(4,128)(2,1)} %param.10) | copy-start | bytes 20740
  0.7 15.5 %copy-start.9 = (f32[64]{0:T(128)S(1)}, f32[64]{0:T(128)}, u32[]{:S(2)}) copy-start(f32[64]{0:T(128)} %param.13) | copy-start | bytes 772
  10.6 5.6 %copy-start.7 = (bf16[1,64,1,8,32]{1,4,3,2,0:T(8,128)(2,1)S(1)}, bf16[1,64,1,8,32]{1,4,3,2,0:T(8,128)(2,1)}, u32[]{:S(2)}) copy-start(bf16[1,64,1,8,32]{1,4,3,2,0:T(8,128)(2,1)} %param.14) | copy-start | bytes 98308
  10.6 8.5 %collective-permute-start.1 = (bf16[4,4,4,8,128]{4,3,2,1,0:T(8,128)(2,1)S(1)}, bf16[4,4,4,8,128]{4,3,2,1,0:T(8,128)(2,1)S(1)}, u32[]{:S(2)}, u32[]{:S(2)}) collective-permute-start(bf16[4,4,4,8,128]{4,3,2,1,0:T(8,128)(2,1)S(1)} %all_to_all.15.own_ref), channel_id=1, source_target_pairs={{8,16},{24,32},{40,48},{56,64},{72,80},{88,96},{104,112},{120,128}... | collective-permute-start | bytes 393224 | tf_op jit(solution)/shard_map/ppermute | solution.py:326
  15.9 3.3 %collective-permute-start = (bf16[4,4,4,8,128]{4,3,2,1,0:T(8,128)(2,1)S(1)}, bf16[4,4,4,8,128]{4,3,2,1,0:T(8,128)(2,1)S(1)}, u32[]{:S(2)}, u32[]{:S(2)}) collective-permute-start(bf16[4,4,4,8,128]{4,3,2,1,0:T(8,128)(2,1)S(1)} %all_to_all.15.own_ref), channel_id=1, source_target_pairs={{0,8},{8,0},{16,24},{24,16},{32,40},{40,32},{48,56},{56,48},{64,72... | collective-permute-start | bytes 393224 | tf_op jit(solution)/shard_map/ppermute | solution.py:324
  16.0 3.2 %copy-start = (bf16[128,2048]{1,0:T(8,128)(2,1)S(1)}, bf16[128,2048]{1,0:T(8,128)(2,1)}, u32[]{:S(2)}) copy-start(bf16[128,2048]{1,0:T(8,128)(2,1)} %constant.9.clone.sel_ref) | copy-start | bytes 1572868
  17.0 2.2 %copy-start.2 = (bf16[512,128]{1,0:T(8,128)(2,1)S(1)}, bf16[512,128]{1,0:T(8,128)(2,1)}, u32[]{:S(2)}) copy-start(bf16[512,128]{1,0:T(8,128)(2,1)} %constant.11.clone.pool_ref) | copy-start | bytes 393220
  17.0 2.2 %copy-start.3 = (bf16[256,256]{1,0:T(8,128)(2,1)S(1)}, bf16[256,256]{1,0:T(8,128)(2,1)}, u32[]{:S(2)}) copy-start(bf16[256,256]{1,0:T(8,128)(2,1)} %constant.10.clone.split_ref) | copy-start | bytes 393220
  19.2 0.9 %copy-start.1 = (bf16[3,64,288]{2,1,0:T(8,128)(2,1)S(1)}, bf16[3,64,288]{2,1,0:T(8,128)(2,1)}, u32[]{:S(2)}) copy-start(bf16[3,64,288]{2,1,0:T(8,128)(2,1)} %get-tuple-element.15.w2_ref) | copy-start | bytes 331780
  20.1 0.9 %copy-start.4 = (bf16[256,256]{1,0:T(8,128)(2,1)S(1)}, bf16[256,256]{1,0:T(8,128)(2,1)}, u32[]{:S(2)}) copy-start(bf16[256,256]{1,0:T(8,128)(2,1)} %get-tuple-element.14.w1_ref) | copy-start | bytes 393220
  21.0 0.9 %copy-start.5 = (bf16[96,576]{1,0:T(8,128)(2,1)S(1)}, bf16[96,576]{1,0:T(8,128)(2,1)}, u32[]{:S(2)}) copy-start(bf16[96,576]{1,0:T(8,128)(2,1)} %get-tuple-element.16.wb_ref) | copy-start | bytes 331780
  60.3 20.8 %all-to-all-start.2 = ((f32[256,2,128]{2,1,0:T(2,128)}), f32[256,2,128]{2,1,0:T(2,128)S(1)}, u32[]{:S(2)}, u32[]{:S(2)}) async-start(f32[256,2,128]{2,1,0:T(2,128)} %bitcast.15), calls=%async_computation.2 | async-start | bytes 524288 | tf_op jit(solution)/shard_map/all_to_all | solution.py:352
  81.1 0.7 copy-start.6

commit v2 on v1

--- a/solution.py
+++ b/solution.py
@@ -4,12 +4,14 @@
 from jax import lax
 from jax.experimental import pallas as pl
 from jax.experimental.pallas import tpu as pltpu
-from jax.sharding import PartitionSpec as P
+from jax.sharding import Mesh, PartitionSpec as P
 
 F32 = jnp.float32
 BF16 = jnp.bfloat16
-AXES = ("depth", "height", "batch")
+DEPTH = ("z", "x_lo", "core")
+PLANE = ("x_lo", "core", "y", "x_hi")
 ROWS = 512
+MIB = 1024 * 1024
 NT = (((1,), (1,)), ((), ()))
 
 
@@ -57,7 +59,7 @@
 
 
 def prep_kernel(k1_ref, k2_ref, sel_ref, w1_ref, w2_ref, wb_ref):
-    flat = lax.dot_general(k1_ref[...], sel_ref[...], (((0,), (0,)), ((), ())), preferred_element_type=F32)
+    flat = lax.dot_general(k1_ref[...], sel_ref[0:108, :], (((0,), (0,)), ((), ())), preferred_element_type=F32)
     for pos in range(8):
         w1_ref[pos * 32 : pos * 32 + 32, :] = (0.5 * flat[:, pos * 256 : pos * 256 + 256]).astype(BF16)
     rows = lax.broadcasted_iota(jnp.int32, (64, 64), 0)
@@ -115,10 +117,10 @@
     deep_ref, packed_ref,
     f_ref, l_ref, g_ref, x_ref, slope_ref, y_ref, z_ref, g2_ref, gz_ref, back_ref, ds_ref, g1_ref, kg_ref,
 ):
-    place = lax.axis_index("depth")
+    place = lax.axis_index(DEPTH)
     parity = place % 2
     keep_low = jnp.where(place > 0, 1.0, 0.0).astype(F32)
-    keep_high = jnp.where(place < lax.axis_size("depth") - 1, 1.0, 0.0).astype(F32)
+    keep_high = jnp.where(place < lax.axis_size(DEPTH) - 1, 1.0, 0.0).astype(F32)
 
     def fill(ref, plane, at):
         for y in range(4):
@@ -278,13 +280,11 @@
 
 
 def sum_kernel(in_ref, out_ref):
-    total = in_ref[0:8, :]
-    for i in range(1, ROWS // 8):
-        total = total + in_ref[8 * i : 8 * i + 8, :]
-    total = total + pltpu.roll(total, 4, 0)
-    total = total + pltpu.roll(total, 2, 0)
-    for i in range(ROWS // 8):
-        out_ref[8 * i : 8 * i + 8, :] = total
+    total = in_ref[0:16, :]
+    for i in range(1, in_ref.shape[0] // 16):
+        total = total + in_ref[16 * i : 16 * i + 16, :]
+    for i in range(out_ref.shape[0] // 16):
+        out_ref[16 * i : 16 * i + 16, :] = total
 
 
 def unpack_kernel(in_ref, second_ref, first_ref, bias1_ref, bias2_ref):
@@ -318,19 +318,24 @@
     return jax.ShapeDtypeStruct(dims, dtype)
 
 
+def exchange(rows, axes):
+    blocks = rows.reshape(-1, 16, 128)
+    return lax.all_to_all(blocks, axes, split_axis=0, concat_axis=0, tiled=True).reshape(-1, 128)
+
+
 def per_device(volumes, first_kernel, first_bias, second_kernel, second_bias, deep_grad):
-    count = lax.axis_size("depth")
-    own = lax.all_to_all(volumes, "height", split_axis=0, concat_axis=0, tiled=True)
-    chip = lax.ppermute(own, "depth", [(i, i ^ 1) for i in range(count)])
+    count = lax.axis_size(DEPTH)
+    own = lax.all_to_all(volumes, "y", split_axis=0, concat_axis=0, tiled=True)
+    chip = lax.ppermute(own, DEPTH, [(i, i ^ 1) for i in range(count)])
     pairs = [(i, i + 1) for i in range(1, count - 1, 2)]
-    link = lax.ppermute(own, "depth", pairs + [(j, i) for i, j in pairs])
+    link = lax.ppermute(own, DEPTH, pairs + [(j, i) for i, j in pairs])
 
     sel = jnp.asarray(select_taps(), BF16)
-    k1 = jnp.pad(first_kernel.reshape(108, 32), ((0, 20), (0, 0)))
     w1, w2, wb = call(
         prep_kernel,
         (shape((256, 256), BF16), shape((3, 64, 288), BF16), shape((96, 576), BF16)),
-        (k1, second_kernel.reshape(864, 64), sel),
+        (first_kernel.reshape(108, 32), second_kernel.reshape(864, 64), sel),
+        limit=8 * MIB,
     )
     deep, packed = call(
         main_kernel,
@@ -345,15 +350,18 @@
             ((4, 256, 1024), F32), ((4, 32, 1024), F32), ((4, 288, 1024), BF16), ((2, 64, 1024), F32),
             ((2, 576, 1024), BF16), ((4, 32, 1024), F32), ((64, 1024), F32), ((256, 1024), BF16), ((864, 64), F32),
         ),
-        40 * 1024 * 1024,
+        24 * MIB,
     )
-    pieces = lax.all_to_all(packed.reshape(256, 2, 128), AXES, split_axis=0, concat_axis=0, tiled=True)
-    (copies,) = call(sum_kernel, (shape((ROWS, 128), F32),), (pieces.reshape(ROWS, 128),))
-    whole = lax.all_to_all(copies.reshape(256, 2, 128), AXES, split_axis=0, concat_axis=0, tiled=True)
+    pieces = exchange(packed, PLANE)
+    (copies,) = call(sum_kernel, (shape((128, 128), F32),), (pieces,), limit=2 * MIB)
+    parts = exchange(copies, "z")
+    (copies,) = call(sum_kernel, (shape((ROWS, 128), F32),), (parts,), limit=2 * MIB)
+    whole = exchange(copies, PLANE)
     second, first, bias1, bias2 = call(
         unpack_kernel,
         (shape((864, 64), F32), shape((27, 4, 32), F32), shape((1, 32), F32), shape((1, 64), F32)),
-        (whole.reshape(ROWS, 128),),
+        (whole,),
+        limit=4 * MIB,
     )
     return (
         deep.reshape(1, 64, 1, 8, 32),
@@ -365,15 +373,8 @@
 
 
 def solution(mesh):
-    in_specs = (
-        P("batch", None, "depth", "height", None),
-        P(),
-        P(),
-        P(),
-        P(),
-        P(("batch", "height"), None, "depth", None, None),
-    )
-    out_specs = (P(("batch", "height"), None, "depth", None, None), P(), P(), P(), P())
-    return jax.shard_map(
-        per_device, mesh=mesh, in_specs=in_specs, out_specs=out_specs, check_vma=False
-    )
+    split = Mesh(mesh.devices.reshape(-1, 2, 2, *mesh.devices.shape[1:]), DEPTH + ("y", "x_hi"))
+    samples = P(("x_hi", "y"), None, DEPTH, None, None)
+    in_specs = (P("x_hi", None, DEPTH, "y", None), P(), P(), P(), P(), samples)
+    out_specs = (samples, P(), P(), P(), P())
+    return jax.shard_map(per_device, mesh=split, in_specs=in_specs, out_specs=out_specs, check_vma=False)

time: 84.2 us -> 73.7 us (0.88)
  waiting for transfers between devices: 14.9 us -> 9.15 us
  Pallas kernels: 12.6 us -> 8.79 us
  local copies, waits for them, and re-layouts: 5.09 us -> 2.75 us
  blocking collectives: 39.8 us -> 41.3 us
    all_to_all x1, waiting for transfers between devices: 14.9 us -> 8.32 us  [exchange(): lax.all_to_all(blocks, axes, split_axis=0, concat_axis=0, tiled=True)]
    pallas_call x4 -> x5, Pallas kernels: 12.6 us -> 8.79 us  [call(): pl.pallas_call(kernel, out_shape=outs, in_specs=vmem(len(inputs)), out_sp...]
    unnamed x22 -> x18, local copies, waits for them, and re-layouts: 3.43 us -> 1.72 us
    all_to_all x2 -> x3, blocking collectives: 39.8 us -> 41.3 us  [the longest x2 31.3 us: exchange(): lax.all_to_all(blocks, axes, split_axis=0, concat_axis=0, tiled=True)]
  transfers between devices with their start and end apart: 3 -> 3, of which waited for: 1 -> 2; matrix products, arithmetic and copies ran while one was open for 2% -> 1% of each run, Pallas kernels for 3% -> 0%
where the time goes in v2:
time: 73.7 us; the launch traced here: 73.3 us
  blocking collectives  41.3 us (56%)
  starting transfers between devices  10.5 us (14%)
  waiting for transfers between devices  9.15 us (12%)
  Pallas kernels  8.79 us (12%)
  local copies, waits for them, and re-layouts  2.75 us (4%)
  between operations  0.75 us (1%)
    all_to_all x2, blocking collectives, exchange(): lax.all_to_all(blocks, axes, split_axis=0, concat_axis=0, tiled=True)  31.3 us
    all_to_all x1, blocking collectives, per_device(): own = lax.all_to_all(volumes, 'y', split_axis=0, concat_axis=0, tiled=True)  9.98 us
    pallas_call x5, Pallas kernels, call(): pl.pallas_call(kernel, out_shape=outs, in_specs=vmem(len(inputs)), out_sp...  8.79 us
    all_to_all x1, waiting for transfers between devices, exchange(): lax.all_to_all(blocks, axes, split_axis=0, concat_axis=0, tiled=True)  8.32 us
    ppermute x1, starting transfers between devices, per_device(): link = lax.ppermute(own, DEPTH, pairs + [(j, i) for i, j in pairs])  5.23 us
    all_to_all x1, starting transfers between devices, exchange(): lax.all_to_all(blocks, axes, split_axis=0, concat_axis=0, tiled=True)  5.21 us
    unnamed x18, local copies, waits for them, and re-layouts  1.72 us
  transfers between devices with their start and end apart: 3, of which 2 were waited for; matrix products, arithmetic and copies ran while one was open for 1% of the time, Pallas kernels for 0%

profile of v2, /device:TPU:1, one launch (start us, length us, event | category | flops | bytes accessed | tf_op | source)
XLA Modules:
  0.0 73.3 jit_solution(6412744205659925087)
XLA Ops:
  0.6 0.0 copy-start.8
  0.6 0.0 copy-start.6
  0.7 0.0 copy-start.2
  0.7 10.0 %all_to_all.20.own_ref = bf16[4,4,4,8,128]{4,3,2,1,0:T(8,128)(2,1)S(1)} all-to-all(bf16[4,4,4,8,128]{4,3,2,1,0:T(8,128)(2,1)} %param.9), channel_id=1, replica_groups=mesh['z'=8,'x_lo'=2,'core'=2,'y'=4,'x_hi'=2] {'y'}, dimensions={0} | all-to-all | bytes 262144 | tf_op jit(solution)/shard_map/all_to_all | solution.py:328
  10.6 0.0 copy-start.5
  10.6 5.2 %collective-permute-start.1 = (bf16[4,4,4,8,128]{4,3,2,1,0:T(8,128)(2,1)S(1)}, bf16[4,4,4,8,128]{4,3,2,1,0:T(8,128)(2,1)S(1)}, u32[]{:S(2)}, u32[]{:S(2)}) collective-permute-start(bf16[4,4,4,8,128]{4,3,2,1,0:T(8,128)(2,1)S(1)} %all_to_all.20.own_ref), channel_id=1, source_target_pairs={{8,16},{24,32},{40,48},{56,64},{72,80},{88,96},{104,112},{120,128}... | collective-permute-start | bytes 393224 | tf_op jit(solution)/shard_map/ppermute | solution.py:331
  15.9 0.1 collective-permute-start
  16.0 0.0 copy-done.8
  16.0 0.1 copy.19.b1_ref
  16.1 0.0 copy-done.6
  16.1 0.0 copy-start.7
  16.1 0.6 copy-done.7
  16.8 0.1 copy.20.b2_ref
  16.9 0.0 copy-done.5
  16.9 0.1 copy.18.dg_ref
  17.0 0.0 copy-done.2
  17.0 0.0 copy-start
  17.0 1.0 %copy-done = bf16[128,2048]{1,0:T(8,128)(2,1)S(1)} copy-done((bf16[128,2048]{1,0:T(8,128)(2,1)S(1)}, bf16[128,2048]{1,0:T(8,128)(2,1)}, u32[]{:S(2)}) %copy-start) | copy-done | bytes 524312
  18.0 0.3 shard_map.128
  18.4 0.8 %collective-permute-done.1.link_ref = bf16[4,4,4,8,128]{4,3,2,1,0:T(8,128)(2,1)S(1)} collective-permute-done((bf16[4,4,4,8,128]{4,3,2,1,0:T(8,128)(2,1)S(1)}, bf16[4,4,4,8,128]{4,3,2,1,0:T(8,128)(2,1)S(1)}, u32[]{:S(2)}, u32[]{:S(2)}) %collective-permute-start.1) | collective-permute-done | bytes 131104 | tf_op jit(solution)/shard_map/ppermute | solution.py:331
  19.2 0.0 collective-permute-done.chip_ref
  19.2 0.0 copy-done.4
  19.2 0.0 copy-done.1
  19.2 0.0 copy-done.3
  19.2 6.8 %shard_map.129 = (bf16[64,256]{1,0:T(8,128)(2,1)S(1)}, f32[512,128]{1,0:T(8,128)S(1)}) custom-call(bf16[4,4,4,8,128]{4,3,2,1,0:T(8,128)(2,1)S(1)} %all_to_all.20.own_ref, bf16[4,4,4,8,128]{4,3,2,1,0:T(8,128)(2,1)S(1)} %collective-permute-done.chip_ref, bf16[4,4,4,8,128]{4,3,2,1,0:T(8,128)(2,1)S(1)} %collective-permute-done.1.link_ref, ...), custom_call_target="tpu_custom_call" | custom-call | tf_op jit(solution)/shard_map/pallas_call | solution.py:307
  26.0 15.1 %all_to_all.21 = f32[32,16,128]{2,1,0:T(8,128)S(1)} all-to-all(f32[32,16,128]{2,1,0:T(8,128)S(1)} %bitcast.19), channel_id=1, replica_groups=mesh['z'=8,'x_lo'=2,'core'=2,'y'=4,'x_hi'=2] {'x_lo','core','y','x_hi'}, dimensions={0} | all-to-all | bytes 524288 | tf_op jit(solution)/shard_map/all_to_all | solution.py:323
  41.1 16.2 %all_to_all.22 = f32[8,16,128]{2,1,0:T(8,128)S(1)} all-to-all(f32[8,16,128]{2,1,0:T(8,128)S(1)} %bitcast.17), channel_id=1, replica_groups=mesh['z'=8,'x_lo'=2,'core'=2,'y'=4,'x_hi'=2] {'z'}, dimensions={0} | all-to-all | bytes 131072 | tf_op jit(solution)/shard_map/all_to_all | solution.py:323
  57.3 0.7 shard_map.131
  58.1 5.2 %all-to-all-start.3 = ((f32[32,16,128]{2,1,0:T(8,128)}), f32[32,16,128]{2,1,0:T(8,128)S(1)}, u32[]{:S(2)}, u32[]{:S(2)}) async-start(f32[32,16,128]{2,1,0:T(8,128)} %bitcast.9), calls=%async_computation.3 | async-start | bytes 524288 | tf_op jit(solution)/shard_map/all_to_all | solution.py:323
  63.3 0.7 %copy.21 = bf16[64,256]{0,1:T(8,128)(2,1)} copy(bf16[64,256]{1,0:T(8,128)(2,1)S(1)} %get-tuple-element.17) | data formatting | bytes 65536 | tf_op jit(solution)/shard_map/pallas_call | solution.py:307
  64.0 8.3 %all-to-all-done.3 = f32[32,16,128]{2,1,0:T(8,128)S(1)} async-done(((f32[32,16,128]{2,1,0:T(8,128)}), f32[32,16,128]{2,1,0:T(8,128)S(1)}, u32[]{:S(2)}, u32[]{:S(2)}) %all-to-all-start.3) | async-done | bytes 262176 | tf_op jit(solution)/shard_map/all_to_all | solution.py:323
  72.3 0.9 %shard_map.132 = (f32[864,64]{1,0:T(8,128)}, f32[27,4,32]{2,1,0:T(4,128)}, f32[1,32]{1,0:T(1,128)}, f32[1,64]{1,0:T(1,128)}) custom-call(f32[512,128]{1,0:T(8,128)S(1)} %bitcast.16), custom_call_target="tpu_custom_call" | custom-call | tf_op jit(solution)/shard_map/pallas_call | solution.py:307
  (5 shorter events, 0.1 us)
Async XLA Ops:
  0.6 15.4 %copy-start.8 = (f32[32]{0:T(128)S(1)}, f32[32]{0:T(128)}, u32[]{:S(2)}) copy-start(f32[32]{0:T(128)} %param.11) | copy-start | bytes 388
  0.6 15.4 %copy-start.6 = (bf16[3,3,3,4,32]{4,3,2,1,0:T(4,128)(2,1)S(1)}, bf16[3,3,3,4,32]{4,3,2,1,0:T(4,128)(2,1)}, u32[]{:S(2)}) copy-start(bf16[3,3,3,4,32]{4,3,2,1,0:T(4,128)(2,1)} %param.10) | copy-start | bytes 20740
  0.7 16.3 %copy-start.2 = (bf16[3,3,3,32,64]{4,3,2,1,0:T(8,128)(2,1)S(1)}, bf16[3,3,3,32,64]{4,3,2,1,0:T(8,128)(2,1)}, u32[]{:S(2)}) copy-start(bf16[3,3,3,32,64]{4,3,2,1,0:T(8,128)(2,1)} %param.12) | copy-start | bytes 331780
  10.6 6.2 %copy-start.5 = (bf16[1,64,1,8,32]{1,4,3,2,0:T(8,128)(2,1)S(1)}, bf16[1,64,1,8,32]{1,4,3,2,0:T(8,128)(2,1)}, u32[]{:S(2)}) copy-start(bf16[1,64,1,8,32]{1,4,3,2,0:T(8,128)(2,1)} %param.14) | copy-start | bytes 98308
  10.6 8.5 %collective-permute-start.1 = (bf16[4,4,4,8,128]{4,3,2,1,0:T(8,128)(2,1)S(1)}, bf16[4,4,4,8,128]{4,3,2,1,0:T(8,128)(2,1)S(1)}, u32[]{:S(2)}, u32[]{:S(2)}) collective-permute-start(bf16[4,4,4,8,128]{4,3,2,1,0:T(8,128)(2,1)S(1)} %all_to_all.20.own_ref), channel_id=1, source_target_pairs={{8,16},{24,32},{40,48},{56,64},{72,80},{88,96},{104,112},{120,128}... | collective-permute-start | bytes 393224 | tf_op jit(solution)/shard_map/ppermute | solution.py:331
  15.9 3.3 %collective-permute-start = (bf16[4,4,4,8,128]{4,3,2,1,0:T(8,128)(2,1)S(1)}, bf16[4,4,4,8,128]{4,3,2,1,0:T(8,128)(2,1)S(1)}, u32[]{:S(2)}, u32[]{:S(2)}) collective-permute-start(bf16[4,4,4,8,128]{4,3,2,1,0:T(8,128)(2,1)S(1)} %all_to_all.20.own_ref), channel_id=1, source_target_pairs={{0,8},{8,0},{16,24},{24,16},{32,40},{40,32},{48,56},{56,48},{64,72... | collective-permute-start | bytes 393224 | tf_op jit(solution)/shard_map/ppermute | solution.py:329
  16.1 0.7 copy-start.7
  16.8 2.4 %copy-start.4 = (bf16[256,256]{1,0:T(8,128)(2,1)S(1)}, bf16[256,256]{1,0:T(8,128)(2,1)}, u32[]{:S(2)}) copy-start(bf16[256,256]{1,0:T(8,128)(2,1)} %constant.7.clone.split_ref) | copy-start | bytes 393220
  17.0 1.0 %copy-start = (bf16[128,2048]{1,0:T(8,128)(2,1)S(1)}, bf16[128,2048]{1,0:T(8,128)(2,1)}, u32[]{:S(2)}) copy-start(bf16[128,2048]{1,0:T(8,128)(2,1)} %constant.6.clone.sel_ref) | copy-start | bytes 1572868
  18.0 1.2 %copy-start.1 = (bf16[128,2048]{1,0:T(8,128)(2,1)S(1)}, bf16[128,2048]{1,0:T(8,128)(2,1)}, u32[]{:S(2)}) copy-start(bf16[128,2048]{1,0:T(8,128)(2,1)} %constant.6.clone.sel_ref) | copy-start | bytes 1572868
  18.0 1.2 %copy-start.3 = (bf16[512,128]{1,0:T(8,128)(2,1)S(1)}, bf16[512,128]{1,0:T(8,128)(2,1)}, u32[]{:S(2)}) copy-start(bf16[512,128]{1,0:T(8,128)(2,1)} %constant.8.clone.pool_ref) | copy-start | bytes 393220
  58.1 14.3 %all-to-all-start.3 = ((f32[32,16,128]{2,1,0:T(8,128)}), f32[32,16,128]{2,1,0:T(8,128)S(1)}, u32[]{:S(2)}, u32[]{:S(2)}) async-start(f32[32,16,128]{2,1,0:T(8,128)} %bitcast.9), calls=%async_computation.3 | async-start | bytes 524288 | tf_op jit(solution)/shard_map/all_to_all | solution.py:323

commit v3 on v2

--- a/solution.py
+++ b/solution.py
@@ -44,9 +44,9 @@
 
 
 def pool_lanes():
-    out = np.zeros((512, 128), np.float32)
+    out = np.zeros((128, 512), np.float32)
     for lane in range(512):
-        out[lane, lane // 128 * 32 + lane % 64 // 2] = 0.125
+        out[lane // 128 * 32 + lane % 64 // 2, lane] = 0.125
     return out
 
 
@@ -58,8 +58,12 @@
     return lax.dot_general(a, b, NT, preferred_element_type=F32)
 
 
+def dot_tn(a, b):
+    return lax.dot_general(a, b, (((0,), (0,)), ((), ())), preferred_element_type=F32)
+
+
 def prep_kernel(k1_ref, k2_ref, sel_ref, w1_ref, w2_ref, wb_ref):
-    flat = lax.dot_general(k1_ref[...], sel_ref[0:108, :], (((0,), (0,)), ((), ())), preferred_element_type=F32)
+    flat = dot_tn(k1_ref[...], sel_ref[0:108, :])
     for pos in range(8):
         w1_ref[pos * 32 : pos * 32 + 32, :] = (0.5 * flat[:, pos * 256 : pos * 256 + 256]).astype(BF16)
     rows = lax.broadcasted_iota(jnp.int32, (64, 64), 0)
@@ -113,7 +117,7 @@
 
 
 def main_kernel(
-    own_ref, chip_ref, link_ref, dg_ref, w1_ref, w2_ref, wb_ref, b1_ref, b2_ref, sel_ref, split_ref, pool_ref,
+    pair_ref, chip_ref, dg_ref, w1_ref, w2_ref, wb_ref, b1_ref, b2_ref, sel_ref, split_ref, pool_ref,
     deep_ref, packed_ref,
     f_ref, l_ref, g_ref, x_ref, slope_ref, y_ref, z_ref, g2_ref, gz_ref, back_ref, ds_ref, g1_ref, kg_ref,
 ):
@@ -122,25 +126,25 @@
     keep_low = jnp.where(place > 0, 1.0, 0.0).astype(F32)
     keep_high = jnp.where(place < lax.axis_size(DEPTH) - 1, 1.0, 0.0).astype(F32)
 
-    def fill(ref, plane, at):
+    def fill(ref, cell, at, keep=None):
         for y in range(4):
             for ch in range(4):
-                f_ref[pl.ds((at * 4 + ch) * 32 + y * 8, 8), :] = ref[y, ch, plane].astype(F32)
-
-    for plane in range(4):
-        fill(own_ref, plane, 3 + plane)
+                part = ref[cell // 4 * 4 + y, ch, cell % 4].astype(F32)
+                f_ref[pl.ds((at * 4 + ch) * 32 + y * 8, 8), :] = part if keep is None else part * keep
 
     @pl.when(parity == 0)
     def _():
-        for plane in range(3):
-            fill(link_ref, plane + 1, plane)
-            fill(chip_ref, plane, 7 + plane)
+        for cell in range(1, 8):
+            fill(pair_ref, cell, cell - 1, keep_low if cell < 4 else None)
+        for cell in range(3):
+            fill(chip_ref, cell, 7 + cell)
 
     @pl.when(parity == 1)
     def _():
-        for plane in range(3):
-            fill(chip_ref, plane + 1, plane)
-            fill(link_ref, plane, 7 + plane)
+        for cell in range(7):
+            fill(pair_ref, cell, cell + 3, keep_high if cell >= 4 else None)
+        for cell in range(5, 8):
+            fill(chip_ref, cell, cell - 5)
 
     for hb in range(2):
         for qq in range(8):
@@ -204,7 +208,7 @@
         for t in range(4):
             lanes = slice(t * 256, t * 256 + 256)
             if plane == 0 and t % 2 == 0:
-                wide = dot_nt(dg_ref[:, t * 64 : t * 64 + 128], pool_ref[...])
+                wide = dot_tn(dg_ref[t * 64 : t * 64 + 128, :], pool_ref[...])
                 g2_ref[0, :, t * 256 : t * 256 + 512] = wide
                 g2_ref[1, :, t * 256 : t * 256 + 512] = wide
             u = bias2
@@ -225,8 +229,8 @@
         part = ds_ref[:, half * 512 : half * 512 + 512]
         high = part.astype(BF16)
         low = (part - high.astype(F32)).astype(BF16)
-        deep = dot(high, pool_ref[...]) + dot(low, pool_ref[...])
-        deep_ref[:, half * 128 : half * 128 + 128] = deep.astype(BF16)
+        deep = dot_nt(pool_ref[...], high) + dot_nt(pool_ref[...], low)
+        deep_ref[half * 128 : half * 128 + 128, :] = deep.astype(BF16)
 
     masks64 = lane_masks(64)
     for plane in range(2):
@@ -302,8 +306,8 @@
     return [pl.BlockSpec(memory_space=pltpu.VMEM) for _ in range(count)]
 
 
-def call(kernel, outs, inputs, scratch=(), limit=None):
-    params = pltpu.CompilerParams(vmem_limit_bytes=limit) if limit else None
+def call(kernel, outs, inputs, scratch=(), limit=None, cost=None):
+    params = pltpu.CompilerParams(vmem_limit_bytes=limit)
     return pl.pallas_call(
         kernel,
         out_shape=outs,
@@ -311,6 +315,7 @@
         out_specs=vmem(len(outs)),
         scratch_shapes=[pltpu.VMEM(shape, dtype) for shape, dtype in scratch],
         compiler_params=params,
+        cost_estimate=cost,
     )(*inputs)
 
 
@@ -325,10 +330,13 @@
 
 def per_device(volumes, first_kernel, first_bias, second_kernel, second_bias, deep_grad):
     count = lax.axis_size(DEPTH)
-    own = lax.all_to_all(volumes, "y", split_axis=0, concat_axis=0, tiled=True)
-    chip = lax.ppermute(own, DEPTH, [(i, i ^ 1) for i in range(count)])
-    pairs = [(i, i + 1) for i in range(1, count - 1, 2)]
-    link = lax.ppermute(own, DEPTH, pairs + [(j, i) for i, j in pairs])
+    groups = [
+        [slab % count * 4 + y for slab in (odd, odd + 1) for y in range(4)] for odd in range(1, count, 2)
+    ]
+    pair = lax.all_to_all(
+        jnp.concatenate([volumes, volumes]), DEPTH + ("y",), 0, 0, axis_index_groups=groups, tiled=True
+    )
+    chip = lax.ppermute(pair, "core", [(0, 1), (1, 0)])
 
     sel = jnp.asarray(select_taps(), BF16)
     w1, w2, wb = call(
@@ -336,12 +344,13 @@
         (shape((256, 256), BF16), shape((3, 64, 288), BF16), shape((96, 576), BF16)),
         (first_kernel.reshape(108, 32), second_kernel.reshape(864, 64), sel),
         limit=8 * MIB,
+        cost=pl.CostEstimate(flops=10**8, bytes_accessed=10**6, transcendentals=0),
     )
     deep, packed = call(
         main_kernel,
-        (shape((64, 256), BF16), shape((ROWS, 128), F32)),
+        (shape((256, 64), BF16), shape((ROWS, 128), F32)),
         (
-            own, chip, link, deep_grad.reshape(64, 256), w1, w2, wb,
+            pair, chip, deep_grad.reshape(64, 256).T, w1, w2, wb,
             first_bias.reshape(32, 1), second_bias.reshape(64, 1), sel,
             jnp.asarray(split_width(), BF16), jnp.asarray(pool_lanes(), BF16),
         ),
@@ -364,7 +373,7 @@
         limit=4 * MIB,
     )
     return (
-        deep.reshape(1, 64, 1, 8, 32),
+        deep.T.reshape(1, 64, 1, 8, 32),
         first.reshape(3, 3, 3, 4, 32),
         bias1.reshape(32),
         second.reshape(3, 3, 3, 32, 64),

time: 73.7 us -> 70.6 us (0.958)
  blocking collectives: 41.3 us -> 54.2 us
  waiting for transfers between devices: 9.15 us -> 0.01 us
  starting transfers between devices: 10.5 us -> 4.58 us
  local copies, waits for them, and re-layouts: 2.75 us -> 1.5 us
  other arithmetic: 0 us -> 1.05 us
    all_to_all x2 -> x3, blocking collectives: 31.3 us -> 41.1 us  [exchange(): lax.all_to_all(blocks, axes, split_axis=0, concat_axis=0, tiled=True)]
    all_to_all x1 -> x0, waiting for transfers between devices: 8.32 us -> none  [exchange(): lax.all_to_all(blocks, axes, split_axis=0, concat_axis=0, tiled=True)]
    all_to_all x1 -> x0, starting transfers between devices: 5.21 us -> none  [exchange(): lax.all_to_all(blocks, axes, split_axis=0, concat_axis=0, tiled=True)]
    all_to_all x1, blocking collectives: 9.98 us -> 13.1 us  [per_device(): lax.all_to_all(jnp.concatenate([volumes, volumes]), DEPTH + ('y',), 0, 0,...]
    concatenate x0 -> x1, other arithmetic: none -> 1.05 us  [per_device(): jnp.concatenate([volumes, volumes])]
    ppermute x2 -> x1, waiting for transfers between devices: 0.83 us -> 0.01 us  [per_device(): chip = lax.ppermute(pair, 'core', [(0, 1), (1, 0)])]
    ppermute x2 -> x1, starting transfers between devices: 5.32 us -> 4.58 us  [per_device(): chip = lax.ppermute(pair, 'core', [(0, 1), (1, 0)])]
    unnamed x18 -> x16, local copies, waits for them, and re-layouts: 1.72 us -> 1.29 us
  transfers between devices with their start and end apart: 3 -> 1, of which waited for: 2 -> 0; matrix products, arithmetic and copies ran while one was open for 1% -> 0% of each run, Pallas kernels for 0% -> 0%
where the time goes in v3:
time: 70.6 us; the launch traced here: 70.3 us
  blocking collectives  54.2 us (77%)
  Pallas kernels  8.22 us (12%)
  starting transfers between devices  4.58 us (6%)
  local copies, waits for them, and re-layouts  1.5 us (2%)
  other arithmetic  1.05 us (1%)
  between operations  0.72 us (1%)
    all_to_all x3, blocking collectives, exchange(): lax.all_to_all(blocks, axes, split_axis=0, concat_axis=0, tiled=True)  41.1 us
    all_to_all x1, blocking collectives, per_device(): lax.all_to_all(jnp.concatenate([volumes, volumes]), DEPTH + ('y',), 0, 0,...  13.1 us
    pallas_call x5, Pallas kernels, call(): pl.pallas_call(kernel, out_shape=outs, in_specs=vmem(len(inputs)), out_sp...  8.22 us
    ppermute x1, starting transfers between devices, per_device(): chip = lax.ppermute(pair, 'core', [(0, 1), (1, 0)])  4.58 us
  transfers between devices with their start and end apart: 1, of which 0 were waited for; matrix products, arithmetic and copies ran while one was open for 0% of the time, Pallas kernels for 0%

profile of v3, /device:TPU:1, one launch (start us, length us, event | category | flops | bytes accessed | tf_op | source)
XLA Modules:
  0.0 70.3 jit_solution(15701318221390132912)
XLA Ops:
  0.6 0.0 copy-start
  0.6 1.1 %pad_maximum_fusion = bf16[8,4,4,8,128]{4,3,2,1,0:T(8,128)(2,1)S(1)} fusion(bf16[4,4,4,8,128]{4,3,2,1,0:T(8,128)(2,1)} %param.9), kind=kLoop, calls=%fused_computation | loop fusion | flops 131072 | bytes 393216 | tf_op jit(solution)/shard_map/concatenate | solution.py:337
  1.7 0.0 copy-start.5
  1.7 0.0 copy-start.1
  1.7 13.1 %all_to_all.20.pair_ref = bf16[8,4,4,8,128]{4,3,2,1,0:T(8,128)(2,1)S(1)} all-to-all(bf16[8,4,4,8,128]{4,3,2,1,0:T(8,128)(2,1)S(1)} %pad_maximum_fusion), channel_id=1, replica_groups={{8,10,12,14,16,18,20,22},{24,26,28,30,32,34,36,38},{40,42,44,46,48,50,5..., dimensions={0} | all-to-all | bytes 524288 | tf_op jit(solution)/shard_map/all_to_all | solution.py:336
  14.8 0.0 copy-start.7
  14.8 4.6 %collective-permute-start = (bf16[8,4,4,8,128]{4,3,2,1,0:T(8,128)(2,1)S(1)}, bf16[8,4,4,8,128]{4,3,2,1,0:T(8,128)(2,1)S(1)}, u32[]{:S(2)}, u32[]{:S(2)}) collective-permute-start(bf16[8,4,4,8,128]{4,3,2,1,0:T(8,128)(2,1)S(1)} %all_to_all.20.pair_ref), channel_id=1, source_target_pairs={{0,8},{8,0},{1,9},{9,1},{2,10},{10,2},{3,11},{11,3},{4,12},{12,4},... | collective-permute-start | bytes 786440 | tf_op jit(solution)/shard_map/ppermute | solution.py:339
  19.4 0.0 copy-done.7
  19.4 0.1 copy.16.b1_ref
  19.5 0.0 copy-done.5
  19.5 0.0 copy-start.6
  19.5 0.6 copy-done.6
  20.2 0.1 copy.17.b2_ref
  20.3 0.0 copy-done
  20.3 0.0 copy-done.1
  20.3 0.0 copy-start.2
  20.3 0.0 copy-start.3
  20.3 0.0 copy-start.4
  20.3 0.3 shard_map.128
  20.6 0.0 collective-permute-done.chip_ref
  20.6 0.5 copy-done.2
  21.2 0.1 copy-done.3
  21.3 0.0 copy-done.4
  21.3 6.9 %shard_map.129 = (bf16[256,64]{1,0:T(8,128)(2,1)}, f32[512,128]{1,0:T(8,128)S(1)}) custom-call(bf16[8,4,4,8,128]{4,3,2,1,0:T(8,128)(2,1)S(1)} %all_to_all.20.pair_ref, bf16[8,4,4,8,128]{4,3,2,1,0:T(8,128)(2,1)S(1)} %collective-permute-done.chip_ref, bf16[256,64]{1,0:T(8,128)(2,1)S(1)} %bitcast.26, bf16[256,256]{1,0:T(8,128)(2,1)S(1)} %get-tuple-element.14.w1_ref, ...), custom_call_target="tpu_custom_call" | custom-call | tf_op jit(solution)/shard_map/pallas_call | solution.py:311
  28.2 14.0 %all_to_all.21 = f32[32,16,128]{2,1,0:T(8,128)S(1)} all-to-all(f32[32,16,128]{2,1,0:T(8,128)S(1)} %bitcast.24), channel_id=1, replica_groups=mesh['z'=8,'x_lo'=2,'core'=2,'y'=4,'x_hi'=2] {'x_lo','core','y','x_hi'}, dimensions={0} | all-to-all | bytes 524288 | tf_op jit(solution)/shard_map/all_to_all | solution.py:328
  42.2 13.0 %all_to_all.22 = f32[8,16,128]{2,1,0:T(8,128)S(1)} all-to-all(f32[8,16,128]{2,1,0:T(8,128)S(1)} %bitcast.22), channel_id=1, replica_groups=mesh['z'=8,'x_lo'=2,'core'=2,'y'=4,'x_hi'=2] {'z'}, dimensions={0} | all-to-all | bytes 131072 | tf_op jit(solution)/shard_map/all_to_all | solution.py:328
  55.3 14.1 %all_to_all.23 = f32[32,16,128]{2,1,0:T(8,128)S(1)} all-to-all(f32[32,16,128]{2,1,0:T(8,128)S(1)} %bitcast.20), channel_id=1, replica_groups=mesh['z'=8,'x_lo'=2,'core'=2,'y'=4,'x_hi'=2] {'x_lo','core','y','x_hi'}, dimensions={0} | all-to-all | bytes 524288 | tf_op jit(solution)/shard_map/all_to_all | solution.py:328
  69.4 0.9 %shard_map.132 = (f32[864,64]{1,0:T(8,128)}, f32[27,4,32]{2,1,0:T(4,128)}, f32[1,32]{1,0:T(1,128)}, f32[1,64]{1,0:T(1,128)}) custom-call(f32[512,128]{1,0:T(8,128)S(1)} %bitcast.21), custom_call_target="tpu_custom_call" | custom-call | tf_op jit(solution)/shard_map/pallas_call | solution.py:311
  (3 shorter events, 0.1 us)
Async XLA Ops:
  0.6 19.6 %copy-start = (bf16[128,2048]{1,0:T(8,128)(2,1)S(1)}, bf16[128,2048]{1,0:T(8,128)(2,1)}, u32[]{:S(2)}) copy-start(bf16[128,2048]{1,0:T(8,128)(2,1)} %constant.6.clone.sel_ref) | copy-start | bytes 1572868
  1.7 17.8 %copy-start.5 = (bf16[3,3,3,4,32]{4,3,2,1,0:T(4,128)(2,1)S(1)}, bf16[3,3,3,4,32]{4,3,2,1,0:T(4,128)(2,1)}, u32[]{:S(2)}) copy-start(bf16[3,3,3,4,32]{4,3,2,1,0:T(4,128)(2,1)} %param.10) | copy-start | bytes 20740
  1.7 18.6 %copy-start.1 = (bf16[3,3,3,32,64]{4,3,2,1,0:T(8,128)(2,1)S(1)}, bf16[3,3,3,32,64]{4,3,2,1,0:T(8,128)(2,1)}, u32[]{:S(2)}) copy-start(bf16[3,3,3,32,64]{4,3,2,1,0:T(8,128)(2,1)} %param.12) | copy-start | bytes 331780
  14.8 4.6 %copy-start.7 = (f32[32]{0:T(128)S(1)}, f32[32]{0:T(128)}, u32[]{:S(2)}) copy-start(f32[32]{0:T(128)} %param.11) | copy-start | bytes 388
  14.8 5.8 %collective-permute-start = (bf16[8,4,4,8,128]{4,3,2,1,0:T(8,128)(2,1)S(1)}, bf16[8,4,4,8,128]{4,3,2,1,0:T(8,128)(2,1)S(1)}, u32[]{:S(2)}, u32[]{:S(2)}) collective-permute-start(bf16[8,4,4,8,128]{4,3,2,1,0:T(8,128)(2,1)S(1)} %all_to_all.20.pair_ref), channel_id=1, source_target_pairs={{0,8},{8,0},{1,9},{9,1},{2,10},{10,2},{3,11},{11,3},{4,12},{12,4},... | collective-permute-start | bytes 786440 | tf_op jit(solution)/shard_map/ppermute | solution.py:339
  19.5 0.7 copy-start.6
  20.3 0.9 %copy-start.2 = (bf16[128,512]{1,0:T(8,128)(2,1)S(1)}, bf16[128,512]{1,0:T(8,128)(2,1)}, u32[]{:S(2)}) copy-start(bf16[128,512]{1,0:T(8,128)(2,1)} %constant.8.clone.pool_ref) | copy-start | bytes 393220
  20.3 1.0 %copy-start.3 = (bf16[256,256]{1,0:T(8,128)(2,1)S(1)}, bf16[256,256]{1,0:T(8,128)(2,1)}, u32[]{:S(2)}) copy-start(bf16[256,256]{1,0:T(8,128)(2,1)} %constant.7.clone.split_ref) | copy-start | bytes 393220
  20.3 1.0 %copy-start.4 = (bf16[1,64,1,8,32]{1,4,3,2,0:T(8,128)(2,1)S(1)}, bf16[1,64,1,8,32]{1,4,3,2,0:T(8,128)(2,1)}, u32[]{:S(2)}) copy-start(bf16[1,64,1,8,32]{1,4,3,2,0:T(8,128)(2,1)} %param.14) | copy-start | bytes 98308

commit v4 on v3

v4 whole, which is shorter than its diff:
```python
import jax
import jax.numpy as jnp
from jax import lax
from jax.experimental import pallas as pl
from jax.experimental.pallas import tpu as pltpu
from jax.sharding import Mesh, PartitionSpec as P

F32 = jnp.float32
BF16 = jnp.bfloat16
DEPTH = ("z", "x_lo", "core")
PLANE = ("x_lo", "core", "y", "x_hi")
ROWS = 512
PLAIN = 27
MIB = 1024 * 1024
NT = (((1,), (1,)), ((), ()))


def iota(dims, dim):
    return lax.broadcasted_iota(jnp.int32, dims, dim)


def window_cell(shifted, odd):
    return jnp.where(shifted == 1, 3 - 3 * odd, 1 + odd)


def select_taps(pos):
    row = iota((1, 256), 1)
    a = (row >> 7) * 2 + ((row >> 2) & 1) - pos // 4
    b = window_cell((row >> 6) & 1, (row >> 4) & 1) - pos // 2 % 2
    c = window_cell((row >> 5) & 1, (row >> 3) & 1) - pos % 2
    low = jnp.minimum(jnp.minimum(a, b), c)
    high = jnp.maximum(jnp.maximum(a, b), c)
    tap = jnp.where((low >= 0) & (high <= 2), ((a * 3 + b) * 3 + c) * 4 + (row & 3), -1)
    return jnp.where(iota((128, 256), 0) == tap, 1.0, 0.0).astype(BF16)


def split_width():
    col = iota((1, 256), 1)
    at = ((col >> 6) & 1) * 128 + 2 * (col & 63) + (col >> 7)
    return jnp.where(iota((256, 256), 0) == at, 1.0, 0.0).astype(BF16)


def pool_lanes():
    lane = iota((1, 512), 1)
    at = (lane >> 7) * 32 + ((lane & 63) >> 1)
    return jnp.where(iota((128, 512), 0) == at, 0.125, 0.0).astype(BF16)


def half_column(row, size):
    spread = jnp.broadcast_to(0.5 * row, (size, size))
    eye = iota((size, size), 0) == iota((size, size), 1)
    return jnp.broadcast_to(jnp.sum(jnp.where(eye, spread, 0.0), axis=1, keepdims=True), (size, 128))


def dot(a, b):
    return jnp.dot(a, b, preferred_element_type=F32)


def dot_nt(a, b):
    return lax.dot_general(a, b, NT, preferred_element_type=F32)


def dot_tn(a, b):
    return lax.dot_general(a, b, (((0,), (0,)), ((), ())), preferred_element_type=F32)


def prep_kernel(
    k1_ref, k2_ref, b1_ref, b2_ref, dg_in_ref,
    w1_ref, w2_ref, wb_ref, bias1_ref, bias2_ref, dg_ref, sel_ref, split_ref, pool_ref,
):
    split_ref[...] = split_width()
    pool_ref[...] = pool_lanes()
    dg_ref[...] = dg_in_ref[...]
    bias1_ref[...] = half_column(b1_ref[...], 32)
    bias2_ref[...] = half_column(b2_ref[...], 64)
    for pos in range(8):
        sel = select_taps(pos)
        sel_ref[:, pos * 256 : pos * 256 + 256] = sel
        w1_ref[pos * 32 : pos * 32 + 32, :] = (0.5 * dot_tn(k1_ref[...], sel[0:108, :])).astype(BF16)
    half_eye = jnp.where(iota((64, 64), 0) == iota((64, 64), 1), 0.5, 0.0).astype(BF16)
    none = jnp.zeros((288, 64), BF16)
    for plane in range(2):
        stack = [none, k2_ref[...]] if plane else [k2_ref[...], none]
        w2_ref[plane * 64 : plane * 64 + 64, :] = dot_nt(half_eye, jnp.concatenate(stack, axis=0)).astype(BF16)
    blank = jnp.zeros((32, 64), F32)
    for target in range(4):
        blocks = []
        for plane in range(2):
            for b in range(3):
                for c in range(3):
                    a = target - plane
                    at = ((a * 3 + 2 - b) * 3 + 2 - c) * 32
                    blocks.append(k2_ref[at : at + 32, :].astype(F32) if 0 <= a <= 2 else blank)
        wb_ref[target * 32 : target * 32 + 32, :] = jnp.concatenate(blocks, axis=1).astype(BF16)


def lane_masks(rows):
    lane = iota((rows, 128), 1)
    cell = lane % 64
    return lane < 64, cell != 0, cell != 63


def width_shift(tiles, step, masks):
    _, not_first, not_last = masks
    if step < 0:
        return [jnp.where(not_first, pltpu.roll(t, 1, 1), 0.0) for t in tiles]
    return [jnp.where(not_last, pltpu.roll(t, 127, 1), 0.0) for t in tiles]


def height_shift(tiles, steps, masks):
    low = masks[0]
    swapped = [pltpu.roll(t, 64, 1) for t in tiles]
    zero = jnp.zeros_like(tiles[0])
    out = []
    for step in steps:
        if step < 0:
            before = [zero] + swapped[:-1]
            out.append([jnp.where(low, before[i], swapped[i]) for i in range(len(tiles))])
        else:
            after = swapped[1:] + [zero]
            out.append([jnp.where(low, swapped[i], after[i]) for i in range(len(tiles))])
    return out


def store_shifts(tiles, put, masks):
    for c in range(3):
        moved = tiles if c == 1 else width_shift(tiles, c - 1, masks)
        before, after = height_shift(moved, (-1, 1), masks)
        for b, group in enumerate((before, moved, after)):
            for t in range(8):
                put(b * 3 + c, t, group[t])


def main_kernel(
    pair_ref, chip_ref, w1_ref, w2_ref, wb_ref, b1_ref, b2_ref, dg_ref, sel_ref, split_ref, pool_ref,
    deep_ref, packed_ref,
    f_ref, l_ref, g_ref, x_ref, slope_ref, y_ref, z_ref, g2_ref, gg_ref, gz_ref, back_ref, ds_ref, g1_ref, kg_ref,
):
    place = lax.axis_index(DEPTH)
    parity = place % 2
    keep_low = jnp.where(place > 0, 1.0, 0.0).astype(F32)
    keep_high = jnp.where(place < lax.axis_size(DEPTH) - 1, 1.0, 0.0).astype(F32)

    def fill(ref, cell, at, keep=None):
        for y in range(4):
            for ch in range(4):
                part = ref[cell // 4 * 4 + y, ch, cell % 4].astype(F32)
                f_ref[pl.ds((at * 4 + ch) * 32 + y * 8, 8), :] = part if keep is None else part * keep

    @pl.when(parity == 0)
    def _():
        for cell in range(1, 8):
            fill(pair_ref, cell, cell - 1, keep_low if cell < 4 else None)
        for cell in range(3):
            fill(chip_ref, cell, 7 + cell)

    @pl.when(parity == 1)
    def _():
        for cell in range(7):
            fill(pair_ref, cell, cell + 3, keep_high if cell >= 4 else None)
        for cell in range(5, 8):
            fill(chip_ref, cell, cell - 5)

    for hb in range(2):
        for qq in range(8):
            for low in range(2):
                l_ref[pl.ds((hb * 8 + qq) * 40, 40), low * 128 : low * 128 + 128] = f_ref[
                    pl.ds(4 * qq + 2 * low + hb, 40, stride=32), :
                ]
    g_ref[...] = dot(l_ref[...].astype(BF16), split_ref[...])

    masks8 = lane_masks(8)
    for pair in range(5):
        for hb in range(2):
            still, moved = [], []
            for wb in range(2):
                tiles = [
                    g_ref[(hb * 8 + qq) * 40 + pair * 8 : (hb * 8 + qq) * 40 + pair * 8 + 8, wb * 128 : wb * 128 + 128]
                    for qq in range(8)
                ]
                still.append(tiles)
                moved.append(width_shift(tiles, 1 if wb == 0 else -1, masks8))
            for ws, group in enumerate((still, moved)):
                step = 1 if hb == 0 else -1
                raised = [height_shift(group[wb], (step,), masks8)[0] for wb in range(2)]
                for hs, part in enumerate((group, raised)):
                    at = pair * 128 + (hs * 2 + ws) * 32 + hb * 16
                    for qq in range(8):
                        both = jnp.concatenate([part[0][qq], part[1][qq]], axis=0)
                        x_ref[at : at + 16, qq * 128 : qq * 128 + 128] = both.astype(BF16)

    bias1 = jnp.concatenate([b1_ref[...], b1_ref[...]], axis=1)
    for plane in range(4):
        for t in range(4):
            lanes = slice(t * 256, t * 256 + 256)
            pre = dot(w1_ref[...], x_ref[plane * 128 : plane * 128 + 256, lanes])
            total = jnp.zeros((32, 256), F32)
            for pos in range(8):
                u = pre[pos * 32 : pos * 32 + 32] + bias1
                tanh = jnp.tanh(u)
                w = 1.0 + tanh
                silu = u * w
                slope_ref[plane, pos * 32 : pos * 32 + 32, lanes] = w + silu * (1.0 - tanh)
                total = total + silu
            scale = 0.125
            if plane == 0:
                scale = 0.125 * keep_low
            if plane == 3:
                scale = 0.125 * keep_high
            y_ref[plane, :, lanes] = total * scale

    masks32 = lane_masks(32)
    for plane in range(4):

        def put(at, t, value, plane=plane):
            row = plane * 288 + at * 32
            z_ref[row : row + 32, t * 128 : t * 128 + 128] = value.astype(BF16)

        store_shifts([y_ref[plane, :, t * 128 : t * 128 + 128] for t in range(8)], put, masks32)

    bias2 = jnp.concatenate([b2_ref[...], b2_ref[...]], axis=1)
    sum2 = jnp.zeros((64, 128), F32)
    for half in range(2):
        wide = dot_tn(dg_ref[half * 128 : half * 128 + 128, :], pool_ref[...])
        g2_ref[0, :, half * 512 : half * 512 + 512] = wide
    for t in range(4):
        lanes = slice(t * 256, t * 256 + 256)
        pre = dot(w2_ref[...], z_ref[:, lanes])
        given = 0.5 * g2_ref[0, :, lanes]
        total = jnp.zeros((64, 256), F32)
        for plane in range(2):
            u = pre[plane * 64 : plane * 64 + 64] + bias2
            tanh = jnp.tanh(u)
            w = 1.0 + tanh
            silu = u * w
            total = total + silu
            grad = given * (w + silu * (1.0 - tanh))
            g2_ref[plane, :, lanes] = grad
            gg_ref[plane * 64 : plane * 64 + 64, lanes] = grad.astype(BF16)
            sum2 = sum2 + grad[:, :128] + grad[:, 128:]
        ds_ref[:, lanes] = total

    for half in range(2):
        part = ds_ref[:, half * 512 : half * 512 + 512]
        high, low = halves(part)
        deep = dot_nt(pool_ref[...], jnp.concatenate([high, low], axis=0))
        deep_ref[half * 128 : half * 128 + 128, :] = (deep[:, :64] + deep[:, 64:]).astype(BF16)

    masks64 = lane_masks(64)
    for plane in range(2):

        def put(at, t, value, plane=plane):
            row = plane * 576 + at * 64
            gz_ref[row : row + 64, t * 128 : t * 128 + 128] = value.astype(BF16)

        store_shifts([g2_ref[plane, :, t * 128 : t * 128 + 128] for t in range(8)], put, masks64)

    kg_ref[...] = dot_nt(z_ref[...], gg_ref[...])

    for t in range(4):
        lanes = slice(t * 256, t * 256 + 256)
        back = dot(wb_ref[...], gz_ref[:, lanes])
        back_ref[0:32, lanes] = back[0:32] * (0.0625 * keep_low)
        back_ref[32:96, lanes] = back[32:96] * 0.0625
        back_ref[96:128, lanes] = back[96:128] * (0.0625 * keep_high)

    sum1 = jnp.zeros((32, 128), F32)
    grads = jnp.zeros((256, 256), F32)
    for plane in range(4):
        for t in range(4):
            lanes = slice(t * 256, t * 256 + 256)
            back = back_ref[plane * 32 : plane * 32 + 32, lanes]
            for pos in range(8):
                grad = back * slope_ref[plane, pos * 32 : pos * 32 + 32, lanes]
                g1_ref[pos * 32 : pos * 32 + 32, lanes] = grad.astype(BF16)
                sum1 = sum1 + grad[:, :128] + grad[:, 128:]
        grads = grads + dot_nt(g1_ref[...], x_ref[plane * 128 : plane * 128 + 256, :])

    spread = jnp.concatenate([grads[pos * 32 : pos * 32 + 32] for pos in range(8)], axis=1)
    high, low = halves(spread)
    first = dot_nt(jnp.concatenate([high, low], axis=0), sel_ref[...])
    biases = lax.dot_general(
        jnp.ones((8, 128), F32),
        jnp.concatenate([sum1, sum2, jnp.zeros((32, 128), F32)], axis=0),
        NT,
        precision=lax.Precision.HIGHEST,
        preferred_element_type=F32,
    )

    low_lanes = iota((432, 128), 1) < 64
    left = kg_ref[0:432, :] + pltpu.roll(kg_ref[288:720, :], 64, 1)
    right = pltpu.roll(kg_ref[432:864, :], 64, 1) + kg_ref[720:1152, :]
    packed_ref[0:432, :] = jnp.where(low_lanes, left, right).astype(BF16)
    first = first[:32] + first[32:]
    for block in range(5):
        rows = first[block * 8 : block * 8 + 8] if block < 4 else biases
        at = PLAIN * 16 + block * 16
        packed_ref[at : at + 16, :] = jnp.concatenate(halves(rows), axis=0)


def halves(rows):
    high = rows.astype(BF16)
    return high, (rows - high.astype(F32)).astype(BF16)


def block_sum(ref):
    total = ref[0:16, :].astype(F32)
    for i in range(1, ref.shape[0] // 16):
        total = total + ref[16 * i : 16 * i + 16, :].astype(F32)
    return total


def plane_sum_kernel(in_ref, out_ref):
    total = block_sum(in_ref)
    split = lax.axis_index(PLANE) >= PLAIN
    rows = total[0:8] + total[8:16]
    total = jnp.where(split, jnp.concatenate([rows, rows], axis=0), total)
    for i in range(out_ref.shape[0] // 16):
        out_ref[16 * i : 16 * i + 16, :] = total


def whole_sum_kernel(in_ref, out_ref):
    total = block_sum(in_ref)
    split = lax.axis_index(PLANE) >= PLAIN
    rows = total[0:8]
    rest = jnp.where(split, rows - rows.astype(BF16).astype(F32), total[8:16])
    total = jnp.concatenate([rows, rest], axis=0).astype(BF16)
    for i in range(out_ref.shape[0] // 16):
        out_ref[16 * i : 16 * i + 16, :] = total


def unpack_kernel(in_ref, second_ref, first_ref, bias1_ref, bias2_ref):
    second_ref[0:432, :] = in_ref[0:432, 0:64].astype(F32)
    second_ref[432:864, :] = in_ref[0:432, 64:128].astype(F32)
    blocks = [in_ref[at : at + 16, :].astype(F32) for at in range(PLAIN * 16, ROWS, 16)]
    rows = [block[0:8] + block[8:16] for block in blocks]
    first = jnp.concatenate(rows[:4], axis=0).T
    for tap in range(27):
        first_ref[tap] = first[4 * tap : 4 * tap + 4, :]
    bias1_ref[...] = rows[4][0:1, 0:32]
    bias2_ref[...] = rows[4][0:1, 32:96]


def vmem(count):
    return [pl.BlockSpec(memory_space=pltpu.VMEM) for _ in range(count)]


def call(kernel, outs, inputs, scratch=(), limit=None, cost=None):
    params = pltpu.CompilerParams(vmem_limit_bytes=limit)
    return pl.pallas_call(
        kernel,
        out_shape=outs,
        in_specs=vmem(len(inputs)),
        out_specs=vmem(len(outs)),
        scratch_shapes=[pltpu.VMEM(shape, dtype) for shape, dtype in scratch],
        compiler_params=params,
        cost_estimate=cost,
    )(*inputs)


def shape(dims, dtype):
    return jax.ShapeDtypeStruct(dims, dtype)


def exchange(rows, axes):
    blocks = rows.reshape(-1, 16, 128)
    return lax.all_to_all(blocks, axes, split_axis=0, concat_axis=0, tiled=True).reshape(-1, 128)


def per_device(volumes, first_kernel, first_bias, second_kernel, second_bias, deep_grad):
    count = lax.axis_size(DEPTH)
    groups = [
        [slab % count * 4 + y for slab in (odd, odd + 1) for y in range(4)] for odd in range(1, count, 2)
    ]
    twice = jnp.concatenate([volumes, volumes])
    pair = lax.all_to_all(twice, DEPTH + ("y",), 0, 0, axis_index_groups=groups, tiled=True)
    prepared = call(
        prep_kernel,
        (
            shape((256, 256), BF16), shape((128, 1152), BF16), shape((128, 1152), BF16), shape((32, 128), F32),
            shape((64, 128), F32), shape((256, 64), BF16), shape((128, 2048), BF16), shape((256, 256), BF16),
            shape((128, 512), BF16),
        ),
        (
            first_kernel.reshape(108, 32), second_kernel.reshape(864, 64), first_bias.reshape(1, 32),
            second_bias.reshape(1, 64), deep_grad.reshape(64, 256).T,
        ),
        limit=8 * MIB,
        cost=pl.CostEstimate(flops=10**8, bytes_accessed=10**6, transcendentals=0),
    )
    chip = lax.ppermute(pair, "core", [(0, 1), (1, 0)])
    deep, packed = call(
        main_kernel,
        (shape((256, 64), BF16), shape((ROWS, 128), BF16)),
        (pair, chip, *prepared),
        (
            ((1280, 128), F32), ((640, 256), F32), ((640, 256), F32), ((640, 1024), BF16),
            ((4, 256, 1024), F32), ((4, 32, 1024), F32), ((1152, 1024), BF16), ((2, 64, 1024), F32),
            ((128, 1024), BF16), ((1152, 1024), BF16), ((128, 1024), F32), ((64, 1024), F32), ((256, 1024), BF16),
            ((1152, 128), F32),
        ),
        24 * MIB,
    )
    pieces = exchange(packed, PLANE)
    (copies,) = call(plane_sum_kernel, (shape((128, 128), F32),), (pieces,), limit=2 * MIB)
    parts = exchange(copies, "z")
    (copies,) = call(whole_sum_kernel, (shape((ROWS, 128), BF16),), (parts,), limit=2 * MIB)
    whole = exchange(copies, PLANE)
    second, first, bias1, bias2 = call(
        unpack_kernel,
        (shape((864, 64), F32), shape((27, 4, 32), F32), shape((1, 32), F32), shape((1, 64), F32)),
        (whole,),
        limit=4 * MIB,
    )
    return (
        deep.T.reshape(1, 64, 1, 8, 32),
        first.reshape(3, 3, 3, 4, 32),
        bias1.reshape(32),
        second.reshape(3, 3, 3, 32, 64),
        bias2.reshape(64),
    )


def solution(mesh):
    split = Mesh(mesh.devices.reshape(-1, 2, 2, *mesh.devices.shape[1:]), DEPTH + ("y", "x_hi"))
    samples = P(("x_hi", "y"), None, DEPTH, None, None)
    in_specs = (P("x_hi", None, DEPTH, "y", None), P(), P(), P(), P(), samples)
    out_specs = (samples, P(), P(), P(), P())
    return jax.shard_map(per_device, mesh=split, in_specs=in_specs, out_specs=out_specs, check_vma=False)
```

time: 70.6 us -> 65.6 us (0.929)
  blocking collectives: 54.2 us -> 51 us
  Pallas kernels: 8.22 us -> 7.34 us
  local copies, waits for them, and re-layouts: 1.5 us -> 0.68 us
    all_to_all x3, blocking collectives: 41.1 us -> 38 us  [exchange(): lax.all_to_all(blocks, axes, split_axis=0, concat_axis=0, tiled=True)]
    pallas_call x5, Pallas kernels: 8.22 us -> 7.34 us  [call(): pl.pallas_call(kernel, out_shape=outs, in_specs=vmem(len(inputs)), out_sp...]
  transfers between devices with their start and end apart: 1 -> 1, of which waited for: 0 -> 0; matrix products, arithmetic and copies ran while one was open for 0% -> 0% of each run, Pallas kernels for 0% -> 1%
where the time goes in v4:
time: 65.6 us; the launch traced here: 65.4 us
  blocking collectives  51 us (78%)
  Pallas kernels  7.34 us (11%)
  starting transfers between devices  4.58 us (7%)
  other arithmetic  1 us (2%)
  between operations  0.72 us (1%)
  local copies, waits for them, and re-layouts  0.68 us (1%)
    all_to_all x3, blocking collectives, exchange(): lax.all_to_all(blocks, axes, split_axis=0, concat_axis=0, tiled=True)  38 us
    all_to_all x1, blocking collectives, per_device(): lax.all_to_all(twice, DEPTH + ('y',), 0, 0, axis_index_groups=groups, til...  13.1 us
    pallas_call x5, Pallas kernels, call(): pl.pallas_call(kernel, out_shape=outs, in_specs=vmem(len(inputs)), out_sp...  7.34 us
    ppermute x1, starting transfers between devices, per_device(): chip = lax.ppermute(pair, 'core', [(0, 1), (1, 0)])  4.58 us
  transfers between devices with their start and end apart: 1, of which 0 were waited for; matrix products, arithmetic and copies ran while one was open for 0% of the time, Pallas kernels for 1%

profile of v4, /device:TPU:1, one launch (start us, length us, event | category | flops | bytes accessed | tf_op | source)
XLA Modules:
  0.0 65.4 jit_solution(9267223916032205835)
XLA Ops:
  0.6 1.0 %pad_maximum_fusion = bf16[8,4,4,8,128]{4,3,2,1,0:T(8,128)(2,1)S(1)} fusion(bf16[4,4,4,8,128]{4,3,2,1,0:T(8,128)(2,1)} %param.6), kind=kLoop, calls=%fused_computation | loop fusion | flops 131072 | bytes 393216 | tf_op jit(solution)/shard_map/concatenate | solution.py:375
  1.6 0.0 copy-start.4
  1.6 0.0 copy-start
  1.7 0.0 copy-start.1
  1.7 13.1 %all_to_all.20.pair_ref = bf16[8,4,4,8,128]{4,3,2,1,0:T(8,128)(2,1)S(1)} all-to-all(bf16[8,4,4,8,128]{4,3,2,1,0:T(8,128)(2,1)S(1)} %pad_maximum_fusion), channel_id=1, replica_groups={{8,10,12,14,16,18,20,22},{24,26,28,30,32,34,36,38},{40,42,44,46,48,50,5..., dimensions={0} | all-to-all | bytes 524288 | tf_op jit(solution)/shard_map/all_to_all | solution.py:376
  14.8 4.6 %collective-permute-start = (bf16[8,4,4,8,128]{4,3,2,1,0:T(8,128)(2,1)S(1)}, bf16[8,4,4,8,128]{4,3,2,1,0:T(8,128)(2,1)S(1)}, u32[]{:S(2)}, u32[]{:S(2)}) collective-permute-start(bf16[8,4,4,8,128]{4,3,2,1,0:T(8,128)(2,1)S(1)} %all_to_all.20.pair_ref), channel_id=1, source_target_pairs={{0,8},{8,0},{1,9},{9,1},{2,10},{10,2},{3,11},{11,3},{4,12},{12,4},... | collective-permute-start | bytes 786440 | tf_op jit(solution)/shard_map/ppermute | solution.py:391
  19.3 0.0 copy-done.4
  19.4 0.0 copy-start.2
  19.4 0.0 copy-start.3
  19.4 0.0 copy-done
  19.4 0.0 copy-done.1
  19.4 0.6 copy-done.2
  20.0 0.0 copy-done.3
  20.0 0.6 shard_map.101
  20.6 0.0 collective-permute-done.chip_ref
  20.7 5.8 %shard_map.102 = (bf16[256,64]{1,0:T(8,128)(2,1)}, bf16[512,128]{1,0:T(8,128)(2,1)S(1)}) custom-call(bf16[8,4,4,8,128]{4,3,2,1,0:T(8,128)(2,1)S(1)} %all_to_all.20.pair_ref, bf16[8,4,4,8,128]{4,3,2,1,0:T(8,128)(2,1)S(1)} %collective-permute-done.chip_ref, bf16[256,256]{1,0:T(8,128)(2,1)S(1)} %get-tuple-element.20.w1_ref, ...), custom_call_target="tpu_custom_call" | custom-call | tf_op jit(solution)/shard_map/pallas_call | solution.py:350
  26.5 12.2 %all_to_all.21 = bf16[32,16,128]{2,1,0:T(8,128)(2,1)S(1)} all-to-all(bf16[32,16,128]{2,1,0:T(8,128)(2,1)S(1)} %bitcast.24), channel_id=1, replica_groups=mesh['z'=8,'x_lo'=2,'core'=2,'y'=4,'x_hi'=2] {'x_lo','core','y','x_hi'}, dimensions={0} | all-to-all | bytes 262144 | tf_op jit(solution)/shard_map/all_to_all | solution.py:367
  38.7 13.0 %all_to_all.22 = f32[8,16,128]{2,1,0:T(8,128)S(1)} all-to-all(f32[8,16,128]{2,1,0:T(8,128)S(1)} %bitcast.22), channel_id=1, replica_groups=mesh['z'=8,'x_lo'=2,'core'=2,'y'=4,'x_hi'=2] {'z'}, dimensions={0} | all-to-all | bytes 131072 | tf_op jit(solution)/shard_map/all_to_all | solution.py:367
  51.7 12.8 %all_to_all.23 = bf16[32,16,128]{2,1,0:T(8,128)(2,1)S(1)} all-to-all(bf16[32,16,128]{2,1,0:T(8,128)(2,1)S(1)} %bitcast.21), channel_id=1, replica_groups=mesh['z'=8,'x_lo'=2,'core'=2,'y'=4,'x_hi'=2] {'x_lo','core','y','x_hi'}, dimensions={0} | all-to-all | bytes 262144 | tf_op jit(solution)/shard_map/all_to_all | solution.py:367
  64.5 0.9 %shard_map.105 = (f32[864,64]{1,0:T(8,128)}, f32[27,4,32]{2,1,0:T(4,128)}, f32[1,32]{1,0:T(1,128)}, f32[1,64]{1,0:T(1,128)}) custom-call(bf16[512,128]{1,0:T(8,128)(2,1)S(1)} %bitcast.19), custom_call_target="tpu_custom_call" | custom-call | tf_op jit(solution)/shard_map/pallas_call | solution.py:350
  (3 shorter events, 0.1 us)
Async XLA Ops:
  1.6 17.7 %copy-start.4 = (bf16[3,3,3,4,32]{4,3,2,1,0:T(4,128)(2,1)S(1)}, bf16[3,3,3,4,32]{4,3,2,1,0:T(4,128)(2,1)}, u32[]{:S(2)}) copy-start(bf16[3,3,3,4,32]{4,3,2,1,0:T(4,128)(2,1)} %param.7) | copy-start | bytes 20740
  1.6 17.8 %copy-start = (bf16[3,3,3,32,64]{4,3,2,1,0:T(8,128)(2,1)S(1)}, bf16[3,3,3,32,64]{4,3,2,1,0:T(8,128)(2,1)}, u32[]{:S(2)}) copy-start(bf16[3,3,3,32,64]{4,3,2,1,0:T(8,128)(2,1)} %param.9) | copy-start | bytes 331780
  1.7 17.7 %copy-start.1 = (bf16[1,64,1,8,32]{1,4,3,2,0:T(8,128)(2,1)S(1)}, bf16[1,64,1,8,32]{1,4,3,2,0:T(8,128)(2,1)}, u32[]{:S(2)}) copy-start(bf16[1,64,1,8,32]{1,4,3,2,0:T(8,128)(2,1)} %param.11) | copy-start | bytes 98308
  14.8 5.9 %collective-permute-start = (bf16[8,4,4,8,128]{4,3,2,1,0:T(8,128)(2,1)S(1)}, bf16[8,4,4,8,128]{4,3,2,1,0:T(8,128)(2,1)S(1)}, u32[]{:S(2)}, u32[]{:S(2)}) collective-permute-start(bf16[8,4,4,8,128]{4,3,2,1,0:T(8,128)(2,1)S(1)} %all_to_all.20.pair_ref), channel_id=1, source_target_pairs={{0,8},{8,0},{1,9},{9,1},{2,10},{10,2},{3,11},{11,3},{4,12},{12,4},... | collective-permute-start | bytes 786440 | tf_op jit(solution)/shard_map/ppermute | solution.py:391
  19.4 0.7 %copy-start.2 = (f32[32]{0:T(128)S(1)}, f32[32]{0:T(128)}, u32[]{:S(2)}) copy-start(f32[32]{0:T(128)} %param.8) | copy-start | bytes 388
  19.4 0.7 %copy-start.3 = (f32[64]{0:T(128)S(1)}, f32[64]{0:T(128)}, u32[]{:S(2)}) copy-start(f32[64]{0:T(128)} %param.10) | copy-start | bytes 772

commit v5 on v4

v5 whole, which is shorter than its diff:
```python
import jax
import jax.numpy as jnp
from jax import lax
from jax.experimental import pallas as pl
from jax.experimental.pallas import tpu as pltpu
from jax.sharding import Mesh, PartitionSpec as P

F32 = jnp.float32
BF16 = jnp.bfloat16
DEPTH = ("z", "x_lo", "core")
PLANE = ("x_lo", "core", "y", "x_hi")
LINE = ("z",)
ROWS = 512
CHUNK = 16
PLAIN = 27
MIB = 1024 * 1024
NT = (((1,), (1,)), ((), ()))


def iota(dims, dim):
    return lax.broadcasted_iota(jnp.int32, dims, dim)


def window_cell(shifted, odd):
    return jnp.where(shifted == 1, 3 - 3 * odd, 1 + odd)


def select_taps(pos):
    row = iota((1, 256), 1)
    a = (row >> 7) * 2 + ((row >> 2) & 1) - pos // 4
    b = window_cell((row >> 6) & 1, (row >> 4) & 1) - pos // 2 % 2
    c = window_cell((row >> 5) & 1, (row >> 3) & 1) - pos % 2
    low = jnp.minimum(jnp.minimum(a, b), c)
    high = jnp.maximum(jnp.maximum(a, b), c)
    tap = jnp.where((low >= 0) & (high <= 2), ((a * 3 + b) * 3 + c) * 4 + (row & 3), -1)
    return jnp.where(iota((128, 256), 0) == tap, 1.0, 0.0).astype(BF16)


def split_width():
    col = iota((1, 256), 1)
    at = ((col >> 6) & 1) * 128 + 2 * (col & 63) + (col >> 7)
    return jnp.where(iota((256, 256), 0) == at, 1.0, 0.0).astype(BF16)


def pool_lanes():
    lane = iota((1, 512), 1)
    at = (lane >> 7) * 32 + ((lane & 63) >> 1)
    return jnp.where(iota((128, 512), 0) == at, 0.125, 0.0).astype(BF16)


def half_column(row, size):
    spread = jnp.broadcast_to(0.5 * row, (size, size))
    eye = iota((size, size), 0) == iota((size, size), 1)
    return jnp.broadcast_to(jnp.sum(jnp.where(eye, spread, 0.0), axis=1, keepdims=True), (size, 128))


def dot(a, b):
    return jnp.dot(a, b, preferred_element_type=F32)


def dot_nt(a, b):
    return lax.dot_general(a, b, NT, preferred_element_type=F32)


def dot_tn(a, b):
    return lax.dot_general(a, b, (((0,), (0,)), ((), ())), preferred_element_type=F32)


def front_kernel(
    volumes_hbm, k1_hbm, k2_hbm, b1_hbm, b2_hbm, dg_hbm,
    twice_ref, w1_ref, w2_ref, wb_ref, bias1_ref, bias2_ref, dg_ref, sel_ref, split_ref, pool_ref,
    k1_in, k1_ref, k2_ref, b1_ref, b2_ref, sems,
):
    pairs = (
        (k1_hbm, k1_in), (k2_hbm, k2_ref), (b1_hbm, b1_ref), (b2_hbm, b2_ref), (dg_hbm, dg_ref),
        (volumes_hbm, twice_ref.at[pl.ds(0, 4)]), (volumes_hbm, twice_ref.at[pl.ds(4, 4)]),
    )
    copies = [pltpu.make_async_copy(src, dst, sems.at[n]) for n, (src, dst) in enumerate(pairs)]
    for copy in copies:
        copy.start()
    split_ref[...] = split_width()
    pool_ref[...] = pool_lanes()
    sels = [select_taps(pos) for pos in range(8)]
    for pos in range(8):
        sel_ref[:, pos * 256 : pos * 256 + 256] = sels[pos]
    for copy in copies[:5]:
        copy.wait()
    bias1_ref[...] = half_column(b1_ref[...], 32)
    bias2_ref[...] = half_column(b2_ref[...], 64)
    for tap in range(27):
        k1_ref[4 * tap : 4 * tap + 4, :] = 0.5 * k1_in[tap].astype(F32)
    k1_ref[108:128, :] = jnp.zeros((20, 32), F32)
    k1 = k1_ref[...].astype(BF16)
    for pos in range(8):
        w1_ref[pos * 32 : pos * 32 + 32, :] = dot_tn(k1, sels[pos]).astype(BF16)
    half_eye = jnp.where(iota((64, 64), 0) == iota((64, 64), 1), 0.5, 0.0).astype(BF16)
    none = jnp.zeros((32, 64), BF16)

    def tap(a, b, c):
        at = ((a * 3 + b) * 3 + c) * 32
        return k2_ref[at : at + 32, :] if 0 <= a <= 2 else none

    for c in range(3):
        for plane in range(2):
            stack = [tap(rim - plane, b, c) for rim in range(4) for b in range(3)]
            at = (c * 2 + plane) * 64
            w2_ref[at : at + 64, :] = dot_nt(half_eye, jnp.concatenate(stack, axis=0)).astype(BF16)
        for rim in range(4):
            row = [tap(rim - plane, 2 - b, 2 - c).astype(F32) for plane in range(2) for b in range(3)]
            at = (c * 4 + rim) * 32
            wb_ref[at : at + 32, :] = jnp.concatenate(row, axis=1).astype(BF16)
    for copy in copies[5:]:
        copy.wait()


def lane_masks(rows):
    lane = iota((rows, 128), 1)
    cell = lane % 64
    return lane < 64, cell != 0, cell != 63


def width_shift(tiles, step, masks):
    _, not_first, not_last = masks
    if step < 0:
        return [jnp.where(not_first, pltpu.roll(t, 1, 1), 0.0) for t in tiles]
    return [jnp.where(not_last, pltpu.roll(t, 127, 1), 0.0) for t in tiles]


def height_shift(tiles, steps, masks):
    low = masks[0]
    swapped = [pltpu.roll(t, 64, 1) for t in tiles]
    zero = jnp.zeros_like(tiles[0])
    out = []
    for step in steps:
        if step < 0:
            before = [zero] + swapped[:-1]
            out.append([jnp.where(low, before[i], swapped[i]) for i in range(len(tiles))])
        else:
            after = swapped[1:] + [zero]
            out.append([jnp.where(low, swapped[i], after[i]) for i in range(len(tiles))])
    return out


def store_height_shifts(ref, put, masks):
    tiles = [ref[:, t * 128 : t * 128 + 128] for t in range(8)]
    before, after = height_shift(tiles, (-1, 1), masks)
    for b, group in enumerate((before, tiles, after)):
        for t in range(8):
            put(b, t, group[t].astype(BF16))


def add_width_shifts(parts, masks):
    sides = []
    for half in range(2):
        one, two, three = (part[:, half * 128 : half * 128 + 128] for part in parts)
        sides.append(two + width_shift([one], -1, masks)[0] + width_shift([three], 1, masks)[0])
    return jnp.concatenate(sides, axis=1)


def grid_ends():
    place = lax.axis_index(DEPTH)
    keep_low = jnp.where(place > 0, 1.0, 0.0).astype(F32)
    keep_high = jnp.where(place < lax.axis_size(DEPTH) - 1, 1.0, 0.0).astype(F32)
    return place % 2, keep_low, keep_high


def fill(f_ref, ref, cell, at, keep=None):
    for y in range(4):
        for ch in range(4):
            part = ref[cell // 4 * 4 + y, ch, cell % 4].astype(F32)
            f_ref[pl.ds((at * 4 + ch) * 32 + y * 8, 8), :] = part if keep is None else part * keep


def split_rows(f_ref, l_ref, g_ref, split_ref, rows):
    for hb in range(2):
        for qq in range(8):
            for low in range(2):
                l_ref[pl.ds((hb * 8 + qq) * rows, rows), low * 128 : low * 128 + 128] = f_ref[
                    pl.ds(4 * qq + 2 * low + hb, rows, stride=32), :
                ]
    g_ref[...] = dot(l_ref[...].astype(BF16), split_ref[...])


def store_windows(g_ref, rows, pair, put):
    masks = lane_masks(8)
    for hb in range(2):
        still, moved = [], []
        for wb in range(2):
            starts = [(hb * 8 + qq) * rows + pair * 8 for qq in range(8)]
            tiles = [g_ref[at : at + 8, wb * 128 : wb * 128 + 128] for at in starts]
            still.append(tiles)
            moved.append(width_shift(tiles, 1 if wb == 0 else -1, masks))
        for ws, group in enumerate((still, moved)):
            step = 1 if hb == 0 else -1
            raised = [height_shift(group[wb], (step,), masks)[0] for wb in range(2)]
            for hs, part in enumerate((group, raised)):
                for qq in range(8):
                    both = jnp.concatenate([part[0][qq], part[1][qq]], axis=0)
                    put((hs * 2 + ws) * 32 + hb * 16, qq, both.astype(BF16))


def first_conv(x_ref, w1_ref, b1_ref, slope_ref, y_ref, scales):
    bias = jnp.concatenate([b1_ref[...], b1_ref[...]], axis=1)
    for plane in range(2):
        for t in range(4):
            lanes = slice(t * 256, t * 256 + 256)
            pre = dot(w1_ref[...], x_ref[plane * 128 : plane * 128 + 256, lanes])
            total = jnp.zeros((32, 256), F32)
            for pos in range(8):
                u = pre[pos * 32 : pos * 32 + 32] + bias
                tanh = jnp.tanh(u)
                w = 1.0 + tanh
                silu = u * w
                slope_ref[plane, pos * 32 : pos * 32 + 32, lanes] = w + silu * (1.0 - tanh)
                total = total + silu
            y_ref[plane, :, lanes] = total * scales[plane]


def store_second_windows(y_ref, put):
    masks = lane_masks(32)
    for plane in range(2):
        store_height_shifts(y_ref.at[plane], lambda b, t, value, plane=plane: put(plane * 96 + b * 32, t, value), masks)


def early_kernel(
    pair_ref, w1_ref, b1_ref, split_ref, x_ref, slope_ref, z_ref, f_ref, l_ref, g_ref, y_ref
):
    _, keep_low, keep_high = grid_ends()
    for cell in range(1, 7):
        fill(f_ref, pair_ref, cell, cell - 1, keep_low if cell < 4 else keep_high)
    split_rows(f_ref, l_ref, g_ref, split_ref, 24)
    for pair in range(3):

        def put(row, t, value, pair=pair):
            x_ref[pair * 128 + row : pair * 128 + row + 16, t * 128 : t * 128 + 128] = value

        store_windows(g_ref, 24, pair, put)
    first_conv(x_ref, w1_ref, b1_ref, slope_ref, y_ref, (0.125 * keep_low, 0.125 * keep_high))

    def put_second(row, t, value):
        z_ref[row : row + 32, t * 128 : t * 128 + 128] = value

    store_second_windows(y_ref, put_second)


def main_kernel(
    pair_ref, chip_ref, early_x_ref, early_slope_ref, early_z_ref,
    w1_ref, w2_ref, wb_ref, b1_ref, b2_ref, dg_ref, sel_ref, split_ref, pool_ref,
    deep_ref, packed_ref,
    f_ref, l_ref, g_ref, x_ref, slope_ref, y_ref, z_ref, g2_ref, gg_ref, gz_ref, back_ref, ds_ref, g1_ref, kg_ref,
):
    parity, keep_low, keep_high = grid_ends()

    @pl.when(parity == 0)
    def _():
        fill(f_ref, pair_ref, 7, 0)
        for cell in range(3):
            fill(f_ref, chip_ref, cell, 1 + cell)

    @pl.when(parity == 1)
    def _():
        for cell in range(3):
            fill(f_ref, chip_ref, 5 + cell, cell)
        fill(f_ref, pair_ref, 0, 3)

    split_rows(f_ref, l_ref, g_ref, split_ref, 16)
    fresh = pl.multiple_of(128 * (1 - parity), 128)
    shared = pl.multiple_of(256 * parity, 128)
    x_ref[pl.ds(shared, 128), :] = early_x_ref[pl.ds(pl.multiple_of(256 * (1 - parity), 128), 128), :]
    for pair in range(2):

        def put(row, t, value, pair=pair):
            x_ref[pl.ds(pl.multiple_of(fresh + (pair * 128 + row), 16), 16), t * 128 : t * 128 + 128] = value

        store_windows(g_ref, 16, pair, put)
    first_conv(x_ref, w1_ref, b1_ref, slope_ref, y_ref, (0.125, 0.125))

    early_at = pl.multiple_of(192 * parity, 16)
    late_at = pl.multiple_of(192 * (1 - parity), 16)
    z_ref[pl.ds(early_at, 192), :] = early_z_ref[...]

    def put_second(row, t, value):
        z_ref[pl.ds(pl.multiple_of(late_at + row, 16), 32), t * 128 : t * 128 + 128] = value

    store_second_windows(y_ref, put_second)

    bias2 = jnp.concatenate([b2_ref[...], b2_ref[...]], axis=1)
    sum2 = jnp.zeros((64, 128), F32)
    masks64, masks128 = lane_masks(64), lane_masks(128)
    for half in range(2):
        wide = dot_tn(dg_ref[half * 128 : half * 128 + 128, :], pool_ref[...])
        g2_ref[0, :, half * 512 : half * 512 + 512] = wide
    for t in range(4):
        lanes = slice(t * 256, t * 256 + 256)
        taps = dot(w2_ref[...], z_ref[:, lanes])
        pre = add_width_shifts([taps[c * 128 : c * 128 + 128] for c in range(3)], masks128)
        given = 0.5 * g2_ref[0, :, lanes]
        total = jnp.zeros((64, 256), F32)
        for plane in range(2):
            u = pre[plane * 64 : plane * 64 + 64] + bias2
            tanh = jnp.tanh(u)
            w = 1.0 + tanh
            silu = u * w
            total = total + silu
            grad = given * (w + silu * (1.0 - tanh))
            g2_ref[plane, :, lanes] = grad
            for half in range(2):
                tile = grad[:, half * 128 : half * 128 + 128]
                at = t * 256 + half * 128
                for c, part in enumerate((width_shift([tile], 1, masks64), [tile], width_shift([tile], -1, masks64))):
                    row = c * 128 + plane * 64
                    gg_ref[row : row + 64, at : at + 128] = part[0].astype(BF16)
            sum2 = sum2 + grad[:, :128] + grad[:, 128:]
        ds_ref[:, lanes] = total

    for half in range(2):
        part = ds_ref[:, half * 512 : half * 512 + 512]
        high, low = halves(part)
        deep = dot_nt(pool_ref[...], jnp.concatenate([high, low], axis=0))
        deep_ref[half * 128 : half * 128 + 128, :] = (deep[:, :64] + deep[:, 64:]).astype(BF16)

    for plane in range(2):

        def put(b, t, value, plane=plane):
            row = plane * 192 + b * 64
            gz_ref[row : row + 64, t * 128 : t * 128 + 128] = value

        store_height_shifts(g2_ref.at[plane], put, masks64)
    for t in range(4):
        lanes = slice(t * 256, t * 256 + 256)
        taps = dot(wb_ref[...], gz_ref[:, lanes])
        back = add_width_shifts([taps[c * 128 : c * 128 + 128] for c in range(3)], masks128)
        back_ref[0:32, lanes] = back[0:32] * (0.0625 * keep_low)
        back_ref[32:96, lanes] = back[32:96] * 0.0625
        back_ref[96:128, lanes] = back[96:128] * (0.0625 * keep_high)

    kg_ref[...] = dot_nt(z_ref[...], gg_ref[...])

    sum1 = jnp.zeros((32, 128), F32)
    grads = jnp.zeros((256, 256), F32)
    for early in range(2):
        windows_ref, slopes_ref = ((x_ref, slope_ref), (early_x_ref, early_slope_ref))[early]
        start = 64 * (parity if early else 1 - parity)
        for plane in range(2):
            at = pl.multiple_of(start + plane * 32, 32)
            for t in range(4):
                lanes = slice(t * 256, t * 256 + 256)
                back = back_ref[pl.ds(at, 32), lanes]
                for pos in range(8):
                    grad = back * slopes_ref[plane, pos * 32 : pos * 32 + 32, lanes]
                    g1_ref[pos * 32 : pos * 32 + 32, lanes] = grad.astype(BF16)
                    sum1 = sum1 + grad[:, :128] + grad[:, 128:]
            grads = grads + dot_nt(g1_ref[...], windows_ref[plane * 128 : plane * 128 + 256, :])

    spread = jnp.concatenate([grads[pos * 32 : pos * 32 + 32] for pos in range(8)], axis=1)
    high, low = halves(spread)
    first = dot_nt(jnp.concatenate([high, low], axis=0), sel_ref[...])
    sums = jnp.concatenate([sum1, sum2, jnp.zeros((32, 128), F32)], axis=0)
    biases = dot_nt(jnp.ones((16, 128), BF16), jnp.concatenate(halves(sums), axis=0))[0:8]
    biases = biases[:, :128] + biases[:, 128:]

    low_lanes = iota((288, 128), 1) < 64
    left, right = [], []
    for c in range(3):
        one, two = kg_ref[0:288, c * 128 : c * 128 + 128], kg_ref[96:384, c * 128 : c * 128 + 128]
        left.append(one + pltpu.roll(two, 64, 1))
        right.append(pltpu.roll(one, 64, 1) + two)
    packed_ref[0:288, :] = jnp.where(low_lanes, left[0], right[1]).astype(BF16)
    packed_ref[288:432, :] = jnp.where(low_lanes[0:144], left[2][0:144], right[2][144:288]).astype(BF16)
    first = first[:32] + first[32:]
    for block in range(5):
        rows = first[block * 8 : block * 8 + 8] if block < 4 else biases
        at = PLAIN * 16 + block * 16
        packed_ref[at : at + 16, :] = jnp.concatenate(halves(rows), axis=0)


def halves(rows):
    high = rows.astype(BF16)
    return high, (rows - high.astype(F32)).astype(BF16)


def sum_kernel(in_ref, out_ref):
    total = in_ref[0:CHUNK, :].astype(F32)
    for i in range(1, in_ref.shape[0] // CHUNK):
        total = total + in_ref[CHUNK * i : CHUNK * i + CHUNK, :].astype(F32)
    blocks = []
    for i in range(CHUNK // 16):
        split = lax.axis_index(PLANE) * (CHUNK // 16) + i >= PLAIN
        upper, lower = total[16 * i : 16 * i + 8], total[16 * i + 8 : 16 * i + 16]
        upper = jnp.where(split, upper + lower, upper)
        lower = jnp.where(split, upper - upper.astype(BF16).astype(F32), lower)
        blocks += [upper, lower]
    chunk = jnp.concatenate(blocks, axis=0).astype(BF16)
    for i in range(out_ref.shape[0] // CHUNK):
        out_ref[CHUNK * i : CHUNK * i + CHUNK, :] = chunk


def unpack_kernel(in_ref, deep_in_ref, deep_ref, second_ref, first_ref, bias1_ref, bias2_ref):
    deep_ref[...] = deep_in_ref[...]
    for tap in range(9):
        for c in range(2):
            at = (tap * 3 + c) * 32
            second_ref[at : at + 32, :] = in_ref[tap * 32 : tap * 32 + 32, c * 64 : c * 64 + 64].astype(F32)
        for half in range(2):
            at = (tap * 3 + 2) * 32 + half * 16
            column, row = divmod(tap * 32 + half * 16, 144)
            rows = in_ref[288 + row : 304 + row, column * 64 : column * 64 + 64]
            second_ref[at : at + 16, :] = rows.astype(F32)
    blocks = [in_ref[at : at + 16, :].astype(F32) for at in range(PLAIN * 16, ROWS, 16)]
    rows = [block[0:8] + block[8:16] for block in blocks]
    first = jnp.concatenate(rows[:4], axis=0).T
    for tap in range(27):
        first_ref[tap] = first[4 * tap : 4 * tap + 4, :]
    bias1_ref[...] = rows[4][0:1, 0:32]
    bias2_ref[...] = rows[4][0:1, 32:96]


def call(kernel, outs, inputs, scratch, limit, flops=0, in_hbm=False):
    place = pl.ANY if in_hbm else pltpu.VMEM
    if in_hbm:
        inputs = [pltpu.with_memory_space_constraint(x, pltpu.HBM) for x in inputs]
    return pl.pallas_call(
        kernel,
        out_shape=outs,
        in_specs=[pl.BlockSpec(memory_space=place) for _ in inputs],
        out_specs=[pl.BlockSpec(memory_space=pltpu.VMEM) for _ in outs],
        scratch_shapes=[pltpu.VMEM(*s) if isinstance(s, tuple) else s for s in scratch],
        compiler_params=pltpu.CompilerParams(vmem_limit_bytes=limit * MIB),
        cost_estimate=pl.CostEstimate(flops=flops, bytes_accessed=10**6, transcendentals=0) if flops else None,
    )(*inputs)


def shape(dims, dtype):
    return jax.ShapeDtypeStruct(dims, dtype)


def exchange(rows, axes):
    blocks = rows.reshape(-1, CHUNK, 128)
    return lax.all_to_all(blocks, axes, split_axis=0, concat_axis=0, tiled=True).reshape(-1, 128)


def per_device(volumes, first_kernel, first_bias, second_kernel, second_bias, deep_grad):
    count = lax.axis_size(DEPTH)
    groups = [
        [slab % count * 4 + y for slab in (odd, odd + 1) for y in range(4)] for odd in range(1, count, 2)
    ]
    twice, *prepared = call(
        front_kernel,
        (
            shape((8,) + volumes.shape[1:], BF16),
            shape((256, 256), BF16), shape((384, 384), BF16), shape((384, 384), BF16), shape((32, 128), F32),
            shape((64, 128), F32), shape((256, 64), BF16), shape((128, 2048), BF16), shape((256, 256), BF16),
            shape((128, 512), BF16),
        ),
        (
            volumes, first_kernel.reshape(27, 4, 32), second_kernel.reshape(864, 64), first_bias.reshape(1, 32),
            second_bias.reshape(1, 64), deep_grad.reshape(64, 256).T,
        ),
        (
            ((27, 4, 32), BF16), ((128, 32), F32), ((864, 64), BF16), ((1, 32), F32), ((1, 64), F32),
            pltpu.SemaphoreType.DMA((7,)),
        ),
        8,
        in_hbm=True,
    )
    w1, _, _, bias1, _, _, _, split, _ = prepared
    pair = lax.all_to_all(twice, DEPTH + ("y",), 0, 0, axis_index_groups=groups, tiled=True)
    chip = lax.ppermute(pair, "core", [(0, 1), (1, 0)])
    early = call(
        early_kernel,
        (shape((384, 1024), BF16), shape((2, 256, 1024), F32), shape((192, 1024), BF16)),
        (pair, w1, bias1, split),
        (((768, 128), F32), ((384, 256), F32), ((384, 256), F32), ((2, 32, 1024), F32)),
        8,
        10**9,
    )
    deep, packed = call(
        main_kernel,
        (shape((256, 64), BF16), shape((ROWS, 128), BF16)),
        (pair, chip, *early, *prepared),
        (
            ((512, 128), F32), ((256, 256), F32), ((256, 256), F32), ((384, 1024), BF16),
            ((2, 256, 1024), F32), ((2, 32, 1024), F32), ((384, 1024), BF16), ((2, 64, 1024), F32),
            ((384, 1024), BF16), ((384, 1024), BF16), ((128, 1024), F32), ((64, 1024), F32), ((256, 1024), BF16),
            ((384, 384), F32),
        ),
        20,
        10**9,
    )
    pieces = exchange(packed, PLANE)
    (copies,) = call(sum_kernel, (shape((128, 128), BF16),), (pieces,), (), 2)
    parts = exchange(copies, LINE)
    (copies,) = call(sum_kernel, (shape((ROWS, 128), BF16),), (parts,), (), 2)
    whole = exchange(copies, PLANE)
    deep, second, first, bias1, bias2 = call(
        unpack_kernel,
        (shape((256, 64), BF16), shape((864, 64), F32), shape((27, 4, 32), F32), shape((1, 32), F32), shape((1, 64), F32)),
        (whole, deep),
        (),
        4,
    )
    return (
        deep.T.reshape(1, 64, 1, 8, 32),
        first.reshape(3, 3, 3, 4, 32),
        bias1.reshape(32),
        second.reshape(3, 3, 3, 32, 64),
        bias2.reshape(64),
    )


def solution(mesh):
    split = Mesh(mesh.devices.reshape(-1, 2, 2, *mesh.devices.shape[1:]), DEPTH + ("y", "x_hi"))
    samples = P(("x_hi", "y"), None, DEPTH, None, None)
    in_specs = (P("x_hi", None, DEPTH, "y", None), P(), P(), P(), P(), samples)
    out_specs = (samples, P(), P(), P(), P())
    return jax.shard_map(per_device, mesh=split, in_specs=in_specs, out_specs=out_specs, check_vma=False)
```

time: 65.6 us -> 64.6 us (0.985)
  Pallas kernels: 7.34 us -> 8.56 us
  other arithmetic: 1 us -> 0 us
  local copies, waits for them, and re-layouts: 0.68 us -> 0 us
    pallas_call x5 -> x6, Pallas kernels: 7.34 us -> 8.56 us  [call(): pl.pallas_call(kernel, out_shape=outs, in_specs=[pl.BlockSpec(memory_spac...]
    concatenate x1 -> x0, other arithmetic: 1 us -> none  [per_device(): twice = jnp.concatenate([volumes, volumes])]
    unnamed x10 -> x0, local copies, waits for them, and re-layouts: 0.66 us -> none
  transfers between devices with their start and end apart: 1 -> 1, of which waited for: 0 -> 0; matrix products, arithmetic and copies ran while one was open for 0% -> 0% of each run, Pallas kernels for 1% -> 2%
where the time goes in v5:
time: 64.6 us; the launch traced here: 64.3 us
  blocking collectives  50.5 us (78%)
  Pallas kernels  8.56 us (13%)
  starting transfers between devices  4.58 us (7%)
  between operations  0.66 us (1%)
    all_to_all x3, blocking collectives, exchange(): lax.all_to_all(blocks, axes, split_axis=0, concat_axis=0, tiled=True)  37.5 us
    all_to_all x1, blocking collectives, per_device(): lax.all_to_all(twice, DEPTH + ('y',), 0, 0, axis_index_groups=groups, til...  13 us
    pallas_call x6, Pallas kernels, call(): pl.pallas_call(kernel, out_shape=outs, in_specs=[pl.BlockSpec(memory_spac...  8.56 us
    ppermute x1, starting transfers between devices, per_device(): chip = lax.ppermute(pair, 'core', [(0, 1), (1, 0)])  4.58 us
  transfers between devices with their start and end apart: 1, of which 0 were waited for; matrix products, arithmetic and copies ran while one was open for 0% of the time, Pallas kernels for 2%

profile of v5, /device:TPU:1, one launch (start us, length us, event | category | flops | bytes accessed | tf_op | source)
XLA Modules:
  0.0 64.3 jit_solution(2247010619733144283)
XLA Ops:
  0.6 1.5 %shard_map.101 = (bf16[8,4,4,8,128]{4,3,2,1,0:T(8,128)(2,1)S(1)}, bf16[256,256]{1,0:T(8,128)(2,1)S(1)}, bf16[384,384]{1,0:T(8,128)(2,1)S(1)}, bf16[384,384]{1,0:...) custom-call(bf16[4,4,4,8,128]{4,3,2,1,0:T(8,128)(2,1)} %volumes_hbm., ...), custom_call_target="tpu_custom_call" | custom-call | tf_op jit(solution)/shard_map/pallas_call | solution.py:422
  2.2 13.0 %all_to_all.20.pair_ref = bf16[8,4,4,8,128]{4,3,2,1,0:T(8,128)(2,1)S(1)} all-to-all(bf16[8,4,4,8,128]{4,3,2,1,0:T(8,128)(2,1)S(1)} %get-tuple-element.25), channel_id=1, replica_groups={{8,10,12,14,16,18,20,22},{24,26,28,30,32,34,36,38},{40,42,44,46,48,50,5..., dimensions={0} | all-to-all | bytes 524288 | tf_op jit(solution)/shard_map/all_to_all | solution.py:467
  15.1 4.6 %collective-permute-start = (bf16[8,4,4,8,128]{4,3,2,1,0:T(8,128)(2,1)S(1)}, bf16[8,4,4,8,128]{4,3,2,1,0:T(8,128)(2,1)S(1)}, u32[]{:S(2)}, u32[]{:S(2)}) collective-permute-start(bf16[8,4,4,8,128]{4,3,2,1,0:T(8,128)(2,1)S(1)} %all_to_all.20.pair_ref), channel_id=1, source_target_pairs={{0,8},{8,0},{1,9},{9,1},{2,10},{10,2},{3,11},{11,3},{4,12},{12,4},... | collective-permute-start | bytes 786440 | tf_op jit(solution)/shard_map/ppermute | solution.py:468
  19.7 1.4 %shard_map.102 = (bf16[384,1024]{1,0:T(8,128)(2,1)S(1)}, f32[2,256,1024]{2,1,0:T(8,128)S(1)}, bf16[192,1024]{1,0:T(8,128)(2,1)S(1)}) custom-call(bf16[8,4,4,8,128]{4,3,2,1,0:T(8,128)(2,1)S(1)} %all_to_all.20.pair_ref, bf16[256,256]{1,0:T(8,128)(2,1)S(1)} %get-tuple-element.26.w1_ref, f32[32,128]{1,0:T(8,128)S(1)} %get-tuple-element.27.b1_ref, ...), custom_call_target="tpu_custom_call" | custom-call | flops 1000000000 | bytes 1000000 | tf_op jit(solution)/shard_map/pallas_call | solution.py:422
  21.1 0.0 collective-permute-done.chip_ref
  21.1 4.7 %shard_map.103 = (bf16[256,64]{1,0:T(8,128)(2,1)S(1)}, bf16[512,128]{1,0:T(8,128)(2,1)S(1)}) custom-call(bf16[8,4,4,8,128]{4,3,2,1,0:T(8,128)(2,1)S(1)} %all_to_all.20.pair_ref, bf16[8,4,4,8,128]{4,3,2,1,0:T(8,128)(2,1)S(1)} %collective-permute-done.chip_ref, bf16[384,1024]{1,0:T(8,128)(2,1)S(1)} %get-tuple-element.29.early_x_ref, ...), custom_call_target="tpu_custom_call" | custom-call | flops 1000000000 | bytes 1000000 | tf_op jit(solution)/shard_map/pallas_call | solution.py:422
  25.8 12.1 %all_to_all.21 = bf16[32,16,128]{2,1,0:T(8,128)(2,1)S(1)} all-to-all(bf16[32,16,128]{2,1,0:T(8,128)(2,1)S(1)} %bitcast.25), channel_id=1, replica_groups=mesh['z'=8,'x_lo'=2,'core'=2,'y'=4,'x_hi'=2] {'x_lo','core','y','x_hi'}, dimensions={0} | all-to-all | bytes 262144 | tf_op jit(solution)/shard_map/all_to_all | solution.py:439
  38.0 12.6 %all_to_all.22 = bf16[8,16,128]{2,1,0:T(8,128)(2,1)S(1)} all-to-all(bf16[8,16,128]{2,1,0:T(8,128)(2,1)S(1)} %bitcast.23), channel_id=1, replica_groups=mesh['z'=8,'x_lo'=2,'core'=2,'y'=4,'x_hi'=2] {'z'}, dimensions={0} | all-to-all | bytes 65536 | tf_op jit(solution)/shard_map/all_to_all | solution.py:439
  50.6 12.8 %all_to_all.23 = bf16[32,16,128]{2,1,0:T(8,128)(2,1)S(1)} all-to-all(bf16[32,16,128]{2,1,0:T(8,128)(2,1)S(1)} %bitcast.21), channel_id=1, replica_groups=mesh['z'=8,'x_lo'=2,'core'=2,'y'=4,'x_hi'=2] {'x_lo','core','y','x_hi'}, dimensions={0} | all-to-all | bytes 262144 | tf_op jit(solution)/shard_map/all_to_all | solution.py:439
  63.4 0.9 %shard_map.106 = (bf16[256,64]{1,0:T(8,128)(2,1)}, f32[864,64]{1,0:T(8,128)}, f32[27,4,32]{2,1,0:T(4,128)}, f32[1,32]{1,0:T(1,128)}, f32[1,64]{1,0:T(1,128)}) custom-call(bf16[512,128]{1,0:T(8,128)(2,1)S(1)} %bitcast.22, bf16[256,64]{1,0:T(8,128)(2,1)S(1)} %get-tuple-element.39.deep_in_ref), custom_call_target="tpu_custom_call" | custom-call | tf_op jit(solution)/shard_map/pallas_call | solution.py:422
  (2 shorter events, 0.1 us)
Async XLA Ops:
  15.1 6.0 %collective-permute-start = (bf16[8,4,4,8,128]{4,3,2,1,0:T(8,128)(2,1)S(1)}, bf16[8,4,4,8,128]{4,3,2,1,0:T(8,128)(2,1)S(1)}, u32[]{:S(2)}, u32[]{:S(2)}) collective-permute-start(bf16[8,4,4,8,128]{4,3,2,1,0:T(8,128)(2,1)S(1)} %all_to_all.20.pair_ref), channel_id=1, source_target_pairs={{0,8},{8,0},{1,9},{9,1},{2,10},{10,2},{3,11},{11,3},{4,12},{12,4},... | collective-permute-start | bytes 786440 | tf_op jit(solution)/shard_map/ppermute | solution.py:468

commit v6 on v5

--- a/solution.py
+++ b/solution.py
@@ -68,8 +68,8 @@
 
 def front_kernel(
     volumes_hbm, k1_hbm, k2_hbm, b1_hbm, b2_hbm, dg_hbm,
-    twice_ref, w1_ref, w2_ref, wb_ref, bias1_ref, bias2_ref, dg_ref, sel_ref, split_ref, pool_ref,
-    k1_in, k1_ref, k2_ref, b1_ref, b2_ref, sems,
+    twice_ref, w1_ref, k2_ref, bias1_ref, bias2_ref, dg_ref, sel_ref, split_ref, pool_ref,
+    k1_in, k1_ref, b1_ref, b2_ref, sems,
 ):
     pairs = (
         (k1_hbm, k1_in), (k2_hbm, k2_ref), (b1_hbm, b1_ref), (b2_hbm, b2_ref), (dg_hbm, dg_ref),
@@ -93,6 +93,11 @@
     k1 = k1_ref[...].astype(BF16)
     for pos in range(8):
         w1_ref[pos * 32 : pos * 32 + 32, :] = dot_tn(k1, sels[pos]).astype(BF16)
+    for copy in copies[5:]:
+        copy.wait()
+
+
+def store_second_weights(k2_ref, w2_ref, wb_ref):
     half_eye = jnp.where(iota((64, 64), 0) == iota((64, 64), 1), 0.5, 0.0).astype(BF16)
     none = jnp.zeros((32, 64), BF16)
 
@@ -109,8 +114,6 @@
             row = [tap(rim - plane, 2 - b, 2 - c).astype(F32) for plane in range(2) for b in range(3)]
             at = (c * 4 + rim) * 32
             wb_ref[at : at + 32, :] = jnp.concatenate(row, axis=1).astype(BF16)
-    for copy in copies[5:]:
-        copy.wait()
 
 
 def lane_masks(rows):
@@ -223,9 +226,11 @@
 
 
 def early_kernel(
-    pair_ref, w1_ref, b1_ref, split_ref, x_ref, slope_ref, z_ref, f_ref, l_ref, g_ref, y_ref
+    pair_ref, w1_ref, k2_ref, b1_ref, split_ref,
+    x_ref, slope_ref, z_ref, w2_ref, wb_ref, f_ref, l_ref, g_ref, y_ref,
 ):
     _, keep_low, keep_high = grid_ends()
+    store_second_weights(k2_ref, w2_ref, wb_ref)
     for cell in range(1, 7):
         fill(f_ref, pair_ref, cell, cell - 1, keep_low if cell < 4 else keep_high)
     split_rows(f_ref, l_ref, g_ref, split_ref, 24)
@@ -244,8 +249,8 @@
 
 
 def main_kernel(
-    pair_ref, chip_ref, early_x_ref, early_slope_ref, early_z_ref,
-    w1_ref, w2_ref, wb_ref, b1_ref, b2_ref, dg_ref, sel_ref, split_ref, pool_ref,
+    pair_ref, chip_ref, early_x_ref, early_slope_ref, early_z_ref, w2_ref, wb_ref,
+    w1_ref, b1_ref, b2_ref, dg_ref, sel_ref, split_ref, pool_ref,
     deep_ref, packed_ref,
     f_ref, l_ref, g_ref, x_ref, slope_ref, y_ref, z_ref, g2_ref, gg_ref, gz_ref, back_ref, ds_ref, g1_ref, kg_ref,
 ):
@@ -448,8 +453,7 @@
         front_kernel,
         (
             shape((8,) + volumes.shape[1:], BF16),
-            shape((256, 256), BF16), shape((384, 384), BF16), shape((384, 384), BF16), shape((32, 128), F32),
-            shape((64, 128), F32), shape((256, 64), BF16), shape((128, 2048), BF16), shape((256, 256), BF16),
+            shape((256, 256), BF16), shape((864, 64), BF16), shape((32, 128), F32), shape((64, 128), F32), shape((256, 64), BF16), shape((128, 2048), BF16), shape((256, 256), BF16),
             shape((128, 512), BF16),
         ),
         (
@@ -457,19 +461,19 @@
             second_bias.reshape(1, 64), deep_grad.reshape(64, 256).T,
         ),
         (
-            ((27, 4, 32), BF16), ((128, 32), F32), ((864, 64), BF16), ((1, 32), F32), ((1, 64), F32),
+            ((27, 4, 32), BF16), ((128, 32), F32), ((1, 32), F32), ((1, 64), F32),
             pltpu.SemaphoreType.DMA((7,)),
         ),
         8,
         in_hbm=True,
     )
-    w1, _, _, bias1, _, _, _, split, _ = prepared
+    w1, k2, bias1, bias2, dg, sel, split, pool = prepared
     pair = lax.all_to_all(twice, DEPTH + ("y",), 0, 0, axis_index_groups=groups, tiled=True)
     chip = lax.ppermute(pair, "core", [(0, 1), (1, 0)])
     early = call(
         early_kernel,
-        (shape((384, 1024), BF16), shape((2, 256, 1024), F32), shape((192, 1024), BF16)),
-        (pair, w1, bias1, split),
+        (shape((384, 1024), BF16), shape((2, 256, 1024), F32), shape((192, 1024), BF16), shape((384, 384), BF16), shape((384, 384), BF16)),
+        (pair, w1, k2, bias1, split),
         (((768, 128), F32), ((384, 256), F32), ((384, 256), F32), ((2, 32, 1024), F32)),
         8,
         10**9,
@@ -477,7 +481,7 @@
     deep, packed = call(
         main_kernel,
         (shape((256, 64), BF16), shape((ROWS, 128), BF16)),
-        (pair, chip, *early, *prepared),
+        (pair, chip, *early, w1, bias1, bias2, dg, sel, split, pool),
         (
             ((512, 128), F32), ((256, 256), F32), ((256, 256), F32), ((384, 1024), BF16),
             ((2, 256, 1024), F32), ((2, 32, 1024), F32), ((384, 1024), BF16), ((2, 64, 1024), F32),

time: 64.6 us -> 64.5 us (level)
  no operation moved by 1% of the time
where the time goes in v6:
time: 64.5 us; the launch traced here: 64.3 us
  blocking collectives  50.5 us (78%)
  Pallas kernels  8.56 us (13%)
  starting transfers between devices  4.58 us (7%)
  between operations  0.66 us (1%)
    all_to_all x3, blocking collectives, exchange(): lax.all_to_all(blocks, axes, split_axis=0, concat_axis=0, tiled=True)  37.5 us
    all_to_all x1, blocking collectives, per_device(): lax.all_to_all(twice, DEPTH + ('y',), 0, 0, axis_index_groups=groups, til...  13 us
    pallas_call x6, Pallas kernels, call(): pl.pallas_call(kernel, out_shape=outs, in_specs=[pl.BlockSpec(memory_spac...  8.56 us
    ppermute x1, starting transfers between devices, per_device(): chip = lax.ppermute(pair, 'core', [(0, 1), (1, 0)])  4.58 us
  transfers between devices with their start and end apart: 1, of which 0 were waited for; matrix products, arithmetic and copies ran while one was open for 0% of the time, Pallas kernels for 2%

profile of v6, /device:TPU:1, one launch (start us, length us, event | category | flops | bytes accessed | tf_op | source)
XLA Modules:
  0.0 64.3 jit_solution(11291215445113686591)
XLA Ops:
  0.6 1.3 %shard_map.101 = (bf16[8,4,4,8,128]{4,3,2,1,0:T(8,128)(2,1)S(1)}, bf16[256,256]{1,0:T(8,128)(2,1)S(1)}, bf16[864,64]{1,0:T(8,128)(2,1)S(1)}, f32[32,128]{1,0:T(8...) custom-call(bf16[4,4,4,8,128]{4,3,2,1,0:T(8,128)(2,1)} %volumes_hbm., ...), custom_call_target="tpu_custom_call" | custom-call | tf_op jit(solution)/shard_map/pallas_call | solution.py:427
  2.0 13.0 %all_to_all.20.pair_ref = bf16[8,4,4,8,128]{4,3,2,1,0:T(8,128)(2,1)S(1)} all-to-all(bf16[8,4,4,8,128]{4,3,2,1,0:T(8,128)(2,1)S(1)} %get-tuple-element.26), channel_id=1, replica_groups={{8,10,12,14,16,18,20,22},{24,26,28,30,32,34,36,38},{40,42,44,46,48,50,5..., dimensions={0} | all-to-all | bytes 524288 | tf_op jit(solution)/shard_map/all_to_all | solution.py:471
  14.9 4.6 %collective-permute-start = (bf16[8,4,4,8,128]{4,3,2,1,0:T(8,128)(2,1)S(1)}, bf16[8,4,4,8,128]{4,3,2,1,0:T(8,128)(2,1)S(1)}, u32[]{:S(2)}, u32[]{:S(2)}) collective-permute-start(bf16[8,4,4,8,128]{4,3,2,1,0:T(8,128)(2,1)S(1)} %all_to_all.20.pair_ref), channel_id=1, source_target_pairs={{0,8},{8,0},{1,9},{9,1},{2,10},{10,2},{3,11},{11,3},{4,12},{12,4},... | collective-permute-start | bytes 786440 | tf_op jit(solution)/shard_map/ppermute | solution.py:472
  19.5 1.6 %shard_map.102 = (bf16[384,1024]{1,0:T(8,128)(2,1)S(1)}, f32[2,256,1024]{2,1,0:T(8,128)S(1)}, bf16[192,1024]{1,0:T(8,128)(2,1)S(1)}, bf16[384,384]{1,0:T(8,128)(2,1)S(1)}, bf16[384,384]{1,0:T(8,128)(2,1)S(1)}) custom-call(bf16[8,4,4,8,128]{4,3,2,1,0:T(8,128)(2,1)S(1)} %all_to_all.20.pair_ref, bf16[256,256]{1,0:T(8,128)(2,1)S(1)} %get-tuple-element.27.w1_ref, ...), custom_call_target="tpu_custom_call" | custom-call | flops 1000000000 | bytes 1000000 | tf_op jit(solution)/shard_map/pallas_call | solution.py:427
  21.1 0.0 collective-permute-done.chip_ref
  21.1 4.7 %shard_map.103 = (bf16[256,64]{1,0:T(8,128)(2,1)S(1)}, bf16[512,128]{1,0:T(8,128)(2,1)S(1)}) custom-call(bf16[8,4,4,8,128]{4,3,2,1,0:T(8,128)(2,1)S(1)} %all_to_all.20.pair_ref, bf16[8,4,4,8,128]{4,3,2,1,0:T(8,128)(2,1)S(1)} %collective-permute-done.chip_ref, bf16[384,1024]{1,0:T(8,128)(2,1)S(1)} %get-tuple-element.31.early_x_ref, ...), custom_call_target="tpu_custom_call" | custom-call | flops 1000000000 | bytes 1000000 | tf_op jit(solution)/shard_map/pallas_call | solution.py:427
  25.8 12.1 %all_to_all.21 = bf16[32,16,128]{2,1,0:T(8,128)(2,1)S(1)} all-to-all(bf16[32,16,128]{2,1,0:T(8,128)(2,1)S(1)} %bitcast.25), channel_id=1, replica_groups=mesh['z'=8,'x_lo'=2,'core'=2,'y'=4,'x_hi'=2] {'x_lo','core','y','x_hi'}, dimensions={0} | all-to-all | bytes 262144 | tf_op jit(solution)/shard_map/all_to_all | solution.py:444
  37.9 12.6 %all_to_all.22 = bf16[8,16,128]{2,1,0:T(8,128)(2,1)S(1)} all-to-all(bf16[8,16,128]{2,1,0:T(8,128)(2,1)S(1)} %bitcast.23), channel_id=1, replica_groups=mesh['z'=8,'x_lo'=2,'core'=2,'y'=4,'x_hi'=2] {'z'}, dimensions={0} | all-to-all | bytes 65536 | tf_op jit(solution)/shard_map/all_to_all | solution.py:444
  50.6 12.8 %all_to_all.23 = bf16[32,16,128]{2,1,0:T(8,128)(2,1)S(1)} all-to-all(bf16[32,16,128]{2,1,0:T(8,128)(2,1)S(1)} %bitcast.21), channel_id=1, replica_groups=mesh['z'=8,'x_lo'=2,'core'=2,'y'=4,'x_hi'=2] {'x_lo','core','y','x_hi'}, dimensions={0} | all-to-all | bytes 262144 | tf_op jit(solution)/shard_map/all_to_all | solution.py:444
  63.4 0.9 %shard_map.106 = (bf16[256,64]{1,0:T(8,128)(2,1)}, f32[864,64]{1,0:T(8,128)}, f32[27,4,32]{2,1,0:T(4,128)}, f32[1,32]{1,0:T(1,128)}, f32[1,64]{1,0:T(1,128)}) custom-call(bf16[512,128]{1,0:T(8,128)(2,1)S(1)} %bitcast.22, bf16[256,64]{1,0:T(8,128)(2,1)S(1)} %get-tuple-element.41.deep_in_ref), custom_call_target="tpu_custom_call" | custom-call | tf_op jit(solution)/shard_map/pallas_call | solution.py:427
  (2 shorter events, 0.1 us)
Async XLA Ops:
  14.9 6.2 %collective-permute-start = (bf16[8,4,4,8,128]{4,3,2,1,0:T(8,128)(2,1)S(1)}, bf16[8,4,4,8,128]{4,3,2,1,0:T(8,128)(2,1)S(1)}, u32[]{:S(2)}, u32[]{:S(2)}) collective-permute-start(bf16[8,4,4,8,128]{4,3,2,1,0:T(8,128)(2,1)S(1)} %all_to_all.20.pair_ref), channel_id=1, source_target_pairs={{0,8},{8,0},{1,9},{9,1},{2,10},{10,2},{3,11},{11,3},{4,12},{12,4},... | collective-permute-start | bytes 786440 | tf_op jit(solution)/shard_map/ppermute | solution.py:472

commit v7 on v6

--- a/solution.py
+++ b/solution.py
@@ -107,9 +107,10 @@
 
     for c in range(3):
         for plane in range(2):
-            stack = [tap(rim - plane, b, c) for rim in range(4) for b in range(3)]
             at = (c * 2 + plane) * 64
-            w2_ref[at : at + 64, :] = dot_nt(half_eye, jnp.concatenate(stack, axis=0)).astype(BF16)
+            for half in range(2):
+                stack = [tap(rim - plane, b, c) for rim in (2 * half, 2 * half + 1) for b in range(3)]
+                w2_ref[half, at : at + 64, :] = dot_nt(half_eye, jnp.concatenate(stack, axis=0)).astype(BF16)
         for rim in range(4):
             row = [tap(rim - plane, 2 - b, 2 - c).astype(F32) for plane in range(2) for b in range(3)]
             at = (c * 4 + rim) * 32
@@ -252,21 +253,24 @@
     pair_ref, chip_ref, early_x_ref, early_slope_ref, early_z_ref, w2_ref, wb_ref,
     w1_ref, b1_ref, b2_ref, dg_ref, sel_ref, split_ref, pool_ref,
     deep_ref, packed_ref,
-    f_ref, l_ref, g_ref, x_ref, slope_ref, y_ref, z_ref, g2_ref, gg_ref, gz_ref, back_ref, ds_ref, g1_ref, kg_ref,
+    f_ref, l_ref, g_ref, x_ref, slope_ref, y_ref, z_ref, g2_ref, gg_ref, gz_ref, back_ref, ds_ref, g1_ref, kg_ref, taps_ref,
 ):
     parity, keep_low, keep_high = grid_ends()
 
-    @pl.when(parity == 0)
-    def _():
-        fill(f_ref, pair_ref, 7, 0)
-        for cell in range(3):
-            fill(f_ref, chip_ref, cell, 1 + cell)
-
-    @pl.when(parity == 1)
-    def _():
-        for cell in range(3):
-            fill(f_ref, chip_ref, 5 + cell, cell)
-        fill(f_ref, pair_ref, 0, 3)
+    for t in range(4):
+        lanes = slice(t * 256, t * 256 + 256)
+        taps_ref[:, lanes] = dot(w2_ref[parity], early_z_ref[:, lanes])
+
+    for plane in range(4):
+        for y in range(4):
+            for ch in range(4):
+                if plane in (1, 2):
+                    part = chip_ref[4 * parity + y, ch, plane - 1 + 2 * parity].astype(F32)
+                else:
+                    own = pair_ref[4 * (1 - parity) + y, ch, 3 * (1 - parity)].astype(F32)
+                    rim = chip_ref[4 * parity + y, ch, 1 if plane == 0 else 2].astype(F32)
+                    part = jnp.where(parity == (0 if plane == 0 else 1), own, rim)
+                f_ref[pl.ds((plane * 4 + ch) * 32 + y * 8, 8), :] = part
 
     split_rows(f_ref, l_ref, g_ref, split_ref, 16)
     fresh = pl.multiple_of(128 * (1 - parity), 128)
@@ -297,7 +301,7 @@
         g2_ref[0, :, half * 512 : half * 512 + 512] = wide
     for t in range(4):
         lanes = slice(t * 256, t * 256 + 256)
-        taps = dot(w2_ref[...], z_ref[:, lanes])
+        taps = taps_ref[:, lanes] + dot(w2_ref[1 - parity], z_ref[pl.ds(late_at, 192), lanes])
         pre = add_width_shifts([taps[c * 128 : c * 128 + 128] for c in range(3)], masks128)
         given = 0.5 * g2_ref[0, :, lanes]
         total = jnp.zeros((64, 256), F32)
@@ -472,7 +476,7 @@
     chip = lax.ppermute(pair, "core", [(0, 1), (1, 0)])
     early = call(
         early_kernel,
-        (shape((384, 1024), BF16), shape((2, 256, 1024), F32), shape((192, 1024), BF16), shape((384, 384), BF16), shape((384, 384), BF16)),
+        (shape((384, 1024), BF16), shape((2, 256, 1024), F32), shape((192, 1024), BF16), shape((2, 384, 192), BF16), shape((384, 384), BF16)),
         (pair, w1, k2, bias1, split),
         (((768, 128), F32), ((384, 256), F32), ((384, 256), F32), ((2, 32, 1024), F32)),
         8,
@@ -486,7 +490,7 @@
             ((512, 128), F32), ((256, 256), F32), ((256, 256), F32), ((384, 1024), BF16),
             ((2, 256, 1024), F32), ((2, 32, 1024), F32), ((384, 1024), BF16), ((2, 64, 1024), F32),
             ((384, 1024), BF16), ((384, 1024), BF16), ((128, 1024), F32), ((64, 1024), F32), ((256, 1024), BF16),
-            ((384, 384), F32),
+            ((384, 384), F32), ((384, 1024), F32),
         ),
         20,
         10**9,

time: 64.5 us -> 64.3 us (level)
  transfers between devices with their start and end apart: 1 -> 1, of which waited for: 0 -> 0; matrix products, arithmetic and copies ran while one was open for 0% -> 0% of each run, Pallas kernels for 2% -> 3%
where the time goes in v7:
time: 64.3 us; the launch traced here: 64.1 us
  blocking collectives  50.5 us (79%)
  Pallas kernels  8.36 us (13%)
  starting transfers between devices  4.58 us (7%)
  between operations  0.66 us (1%)
    all_to_all x3, blocking collectives, exchange(): lax.all_to_all(blocks, axes, split_axis=0, concat_axis=0, tiled=True)  37.5 us
    all_to_all x1, blocking collectives, per_device(): lax.all_to_all(twice, DEPTH + ('y',), 0, 0, axis_index_groups=groups, til...  13 us
    pallas_call x6, Pallas kernels, call(): pl.pallas_call(kernel, out_shape=outs, in_specs=[pl.BlockSpec(memory_spac...  8.36 us
    ppermute x1, starting transfers between devices, per_device(): chip = lax.ppermute(pair, 'core', [(0, 1), (1, 0)])  4.58 us
  transfers between devices with their start and end apart: 1, of which 0 were waited for; matrix products, arithmetic and copies ran while one was open for 0% of the time, Pallas kernels for 3%

profile of v7, /device:TPU:1, one launch (start us, length us, event | category | flops | bytes accessed | tf_op | source)
XLA Modules:
  0.0 64.1 jit_solution(18271761560515406884)
XLA Ops:
  0.6 1.3 %shard_map.101 = (bf16[8,4,4,8,128]{4,3,2,1,0:T(8,128)(2,1)S(1)}, bf16[256,256]{1,0:T(8,128)(2,1)S(1)}, bf16[864,64]{1,0:T(8,128)(2,1)S(1)}, f32[32,128]{1,0:T(8...) custom-call(bf16[4,4,4,8,128]{4,3,2,1,0:T(8,128)(2,1)} %volumes_hbm., ...), custom_call_target="tpu_custom_call" | custom-call | tf_op jit(solution)/shard_map/pallas_call | solution.py:431
  2.0 13.0 %all_to_all.20.pair_ref = bf16[8,4,4,8,128]{4,3,2,1,0:T(8,128)(2,1)S(1)} all-to-all(bf16[8,4,4,8,128]{4,3,2,1,0:T(8,128)(2,1)S(1)} %get-tuple-element.26), channel_id=1, replica_groups={{8,10,12,14,16,18,20,22},{24,26,28,30,32,34,36,38},{40,42,44,46,48,50,5..., dimensions={0} | all-to-all | bytes 524288 | tf_op jit(solution)/shard_map/all_to_all | solution.py:475
  14.9 4.6 %collective-permute-start = (bf16[8,4,4,8,128]{4,3,2,1,0:T(8,128)(2,1)S(1)}, bf16[8,4,4,8,128]{4,3,2,1,0:T(8,128)(2,1)S(1)}, u32[]{:S(2)}, u32[]{:S(2)}) collective-permute-start(bf16[8,4,4,8,128]{4,3,2,1,0:T(8,128)(2,1)S(1)} %all_to_all.20.pair_ref), channel_id=1, source_target_pairs={{0,8},{8,0},{1,9},{9,1},{2,10},{10,2},{3,11},{11,3},{4,12},{12,4},... | collective-permute-start | bytes 786440 | tf_op jit(solution)/shard_map/ppermute | solution.py:476
  19.5 1.7 %shard_map.102 = (bf16[384,1024]{1,0:T(8,128)(2,1)S(1)}, f32[2,256,1024]{2,1,0:T(8,128)S(1)}, bf16[192,1024]{1,0:T(8,128)(2,1)S(1)}, bf16[2,384,192]{2,1,0:T(8,128)(2,1)S(1)}, bf16[384,384]{1,0:T(8,128)(2,1)S(1)}) custom-call(bf16[8,4,4,8,128]{4,3,2,1,0:T(8,128)(2,1)S(1)} %all_to_all.20.pair_ref, bf16[256,256]{1,0:T(8,128)(2,1)S(1)} %get-tuple-element.27.w1_ref, ...), custom_call_target="tpu_custom_call" | custom-call | flops 1000000000 | bytes 1000000 | tf_op jit(solution)/shard_map/pallas_call | solution.py:431
  21.2 0.0 collective-permute-done.chip_ref
  21.2 4.4 %shard_map.103 = (bf16[256,64]{1,0:T(8,128)(2,1)S(1)}, bf16[512,128]{1,0:T(8,128)(2,1)S(1)}) custom-call(bf16[8,4,4,8,128]{4,3,2,1,0:T(8,128)(2,1)S(1)} %all_to_all.20.pair_ref, bf16[8,4,4,8,128]{4,3,2,1,0:T(8,128)(2,1)S(1)} %collective-permute-done.chip_ref, bf16[384,1024]{1,0:T(8,128)(2,1)S(1)} %get-tuple-element.31.early_x_ref, ...), custom_call_target="tpu_custom_call" | custom-call | flops 1000000000 | bytes 1000000 | tf_op jit(solution)/shard_map/pallas_call | solution.py:431
  25.6 12.1 %all_to_all.21 = bf16[32,16,128]{2,1,0:T(8,128)(2,1)S(1)} all-to-all(bf16[32,16,128]{2,1,0:T(8,128)(2,1)S(1)} %bitcast.25), channel_id=1, replica_groups=mesh['z'=8,'x_lo'=2,'core'=2,'y'=4,'x_hi'=2] {'x_lo','core','y','x_hi'}, dimensions={0} | all-to-all | bytes 262144 | tf_op jit(solution)/shard_map/all_to_all | solution.py:448
  37.7 12.6 %all_to_all.22 = bf16[8,16,128]{2,1,0:T(8,128)(2,1)S(1)} all-to-all(bf16[8,16,128]{2,1,0:T(8,128)(2,1)S(1)} %bitcast.23), channel_id=1, replica_groups=mesh['z'=8,'x_lo'=2,'core'=2,'y'=4,'x_hi'=2] {'z'}, dimensions={0} | all-to-all | bytes 65536 | tf_op jit(solution)/shard_map/all_to_all | solution.py:448
  50.4 12.8 %all_to_all.23 = bf16[32,16,128]{2,1,0:T(8,128)(2,1)S(1)} all-to-all(bf16[32,16,128]{2,1,0:T(8,128)(2,1)S(1)} %bitcast.21), channel_id=1, replica_groups=mesh['z'=8,'x_lo'=2,'core'=2,'y'=4,'x_hi'=2] {'x_lo','core','y','x_hi'}, dimensions={0} | all-to-all | bytes 262144 | tf_op jit(solution)/shard_map/all_to_all | solution.py:448
  63.2 0.9 %shard_map.106 = (bf16[256,64]{1,0:T(8,128)(2,1)}, f32[864,64]{1,0:T(8,128)}, f32[27,4,32]{2,1,0:T(4,128)}, f32[1,32]{1,0:T(1,128)}, f32[1,64]{1,0:T(1,128)}) custom-call(bf16[512,128]{1,0:T(8,128)(2,1)S(1)} %bitcast.22, bf16[256,64]{1,0:T(8,128)(2,1)S(1)} %get-tuple-element.41.deep_in_ref), custom_call_target="tpu_custom_call" | custom-call | tf_op jit(solution)/shard_map/pallas_call | solution.py:431
  (2 shorter events, 0.1 us)
Async XLA Ops:
  14.9 6.3 %collective-permute-start = (bf16[8,4,4,8,128]{4,3,2,1,0:T(8,128)(2,1)S(1)}, bf16[8,4,4,8,128]{4,3,2,1,0:T(8,128)(2,1)S(1)}, u32[]{:S(2)}, u32[]{:S(2)}) collective-permute-start(bf16[8,4,4,8,128]{4,3,2,1,0:T(8,128)(2,1)S(1)} %all_to_all.20.pair_ref), channel_id=1, source_target_pairs={{0,8},{8,0},{1,9},{9,1},{2,10},{10,2},{3,11},{11,3},{4,12},{12,4},... | collective-permute-start | bytes 786440 | tf_op jit(solution)/shard_map/ppermute | solution.py:476

commit v8 on v7

--- a/solution.py
+++ b/solution.py
@@ -68,11 +68,11 @@
 
 def front_kernel(
     volumes_hbm, k1_hbm, k2_hbm, b1_hbm, b2_hbm, dg_hbm,
-    twice_ref, w1_ref, k2_ref, bias1_ref, bias2_ref, dg_ref, sel_ref, split_ref, pool_ref,
-    k1_in, k1_ref, b1_ref, b2_ref, sems,
+    twice_ref, k1_ref, k2_ref, bias1_ref, bias2_ref, dg_ref, sel_ref, split_ref, pool_ref,
+    b1_ref, b2_ref, sems,
 ):
     pairs = (
-        (k1_hbm, k1_in), (k2_hbm, k2_ref), (b1_hbm, b1_ref), (b2_hbm, b2_ref), (dg_hbm, dg_ref),
+        (k1_hbm, k1_ref), (k2_hbm, k2_ref), (b1_hbm, b1_ref), (b2_hbm, b2_ref), (dg_hbm, dg_ref),
         (volumes_hbm, twice_ref.at[pl.ds(0, 4)]), (volumes_hbm, twice_ref.at[pl.ds(4, 4)]),
     )
     copies = [pltpu.make_async_copy(src, dst, sems.at[n]) for n, (src, dst) in enumerate(pairs)]
@@ -80,25 +80,26 @@
         copy.start()
     split_ref[...] = split_width()
     pool_ref[...] = pool_lanes()
-    sels = [select_taps(pos) for pos in range(8)]
     for pos in range(8):
-        sel_ref[:, pos * 256 : pos * 256 + 256] = sels[pos]
-    for copy in copies[:5]:
+        sel_ref[:, pos * 256 : pos * 256 + 256] = select_taps(pos)
+    for copy in copies[2:4]:
         copy.wait()
     bias1_ref[...] = half_column(b1_ref[...], 32)
     bias2_ref[...] = half_column(b2_ref[...], 64)
+    for copy in copies[:2] + copies[4:]:
+        copy.wait()
+
+
+def store_first_weights(k1_ref, sel_ref, rows_ref, w1_ref):
     for tap in range(27):
-        k1_ref[4 * tap : 4 * tap + 4, :] = 0.5 * k1_in[tap].astype(F32)
-    k1_ref[108:128, :] = jnp.zeros((20, 32), F32)
-    k1 = k1_ref[...].astype(BF16)
+        rows_ref[4 * tap : 4 * tap + 4, :] = 0.5 * k1_ref[tap].astype(F32)
+    rows_ref[108:128, :] = jnp.zeros((20, 32), F32)
+    k1 = rows_ref[...].T.astype(BF16)
     for pos in range(8):
-        w1_ref[pos * 32 : pos * 32 + 32, :] = dot_tn(k1, sels[pos]).astype(BF16)
-    for copy in copies[5:]:
-        copy.wait()
+        w1_ref[pos * 32 : pos * 32 + 32, :] = dot(k1, sel_ref[:, pos * 256 : pos * 256 + 256]).astype(BF16)
 
 
 def store_second_weights(k2_ref, w2_ref, wb_ref):
-    half_eye = jnp.where(iota((64, 64), 0) == iota((64, 64), 1), 0.5, 0.0).astype(BF16)
     none = jnp.zeros((32, 64), BF16)
 
     def tap(a, b, c):
@@ -106,14 +107,16 @@
         return k2_ref[at : at + 32, :] if 0 <= a <= 2 else none
 
     for c in range(3):
-        for plane in range(2):
-            at = (c * 2 + plane) * 64
-            for half in range(2):
-                stack = [tap(rim - plane, b, c) for rim in (2 * half, 2 * half + 1) for b in range(3)]
-                w2_ref[half, at : at + 64, :] = dot_nt(half_eye, jnp.concatenate(stack, axis=0)).astype(BF16)
-        for rim in range(4):
-            row = [tap(rim - plane, 2 - b, 2 - c).astype(F32) for plane in range(2) for b in range(3)]
-            at = (c * 4 + rim) * 32
+        for half in range(2):
+            stacks = [
+                jnp.concatenate([tap(rim - plane, b, c) for rim in (2 * half, 2 * half + 1) for b in range(3)], axis=0)
+                for plane in range(2)
+            ]
+            both = 0.5 * jnp.concatenate([stack.astype(F32) for stack in stacks], axis=1)
+            w2_ref[half, c * 128 : c * 128 + 128, :] = both.T.astype(BF16)
+        for a in range(3):
+            row = [tap(a, 2 - b, 2 - c).astype(F32) for b in range(3)]
+            at = (c * 3 + a) * 32
             wb_ref[at : at + 32, :] = jnp.concatenate(row, axis=1).astype(BF16)
 
 
@@ -227,10 +230,11 @@
 
 
 def early_kernel(
-    pair_ref, w1_ref, k2_ref, b1_ref, split_ref,
-    x_ref, slope_ref, z_ref, w2_ref, wb_ref, f_ref, l_ref, g_ref, y_ref,
+    pair_ref, k1_ref, k2_ref, b1_ref, sel_ref, split_ref,
+    x_ref, slope_ref, z_ref, w1_ref, w2_ref, wb_ref, f_ref, l_ref, g_ref, y_ref, rows_ref,
 ):
     _, keep_low, keep_high = grid_ends()
+    store_first_weights(k1_ref, sel_ref, rows_ref, w1_ref)
     store_second_weights(k2_ref, w2_ref, wb_ref)
     for cell in range(1, 7):
         fill(f_ref, pair_ref, cell, cell - 1, keep_low if cell < 4 else keep_high)
@@ -250,8 +254,8 @@
 
 
 def main_kernel(
-    pair_ref, chip_ref, early_x_ref, early_slope_ref, early_z_ref, w2_ref, wb_ref,
-    w1_ref, b1_ref, b2_ref, dg_ref, sel_ref, split_ref, pool_ref,
+    pair_ref, chip_ref, early_x_ref, early_slope_ref, early_z_ref, w1_ref, w2_ref, wb_ref,
+    b1_ref, b2_ref, dg_ref, sel_ref, split_ref, pool_ref,
     deep_ref, packed_ref,
     f_ref, l_ref, g_ref, x_ref, slope_ref, y_ref, z_ref, g2_ref, gg_ref, gz_ref, back_ref, ds_ref, g1_ref, kg_ref, taps_ref,
 ):
@@ -317,7 +321,7 @@
                 tile = grad[:, half * 128 : half * 128 + 128]
                 at = t * 256 + half * 128
                 for c, part in enumerate((width_shift([tile], 1, masks64), [tile], width_shift([tile], -1, masks64))):
-                    row = c * 128 + plane * 64
+                    row = plane * 192 + c * 64
                     gg_ref[row : row + 64, at : at + 128] = part[0].astype(BF16)
             sum2 = sum2 + grad[:, :128] + grad[:, 128:]
         ds_ref[:, lanes] = total
@@ -337,13 +341,18 @@
         store_height_shifts(g2_ref.at[plane], put, masks64)
     for t in range(4):
         lanes = slice(t * 256, t * 256 + 256)
-        taps = dot(wb_ref[...], gz_ref[:, lanes])
-        back = add_width_shifts([taps[c * 128 : c * 128 + 128] for c in range(3)], masks128)
+        one, two = (dot(wb_ref[...], gz_ref[plane * 192 : plane * 192 + 192, lanes]) for plane in range(2))
+        parts = []
+        for c in range(3):
+            at = c * 96
+            both = one[at + 32 : at + 96] + two[at : at + 64]
+            parts.append(jnp.concatenate([one[at : at + 32], both, two[at + 64 : at + 96]], axis=0))
+        back = add_width_shifts(parts, masks128)
         back_ref[0:32, lanes] = back[0:32] * (0.0625 * keep_low)
         back_ref[32:96, lanes] = back[32:96] * 0.0625
         back_ref[96:128, lanes] = back[96:128] * (0.0625 * keep_high)
 
-    kg_ref[...] = dot_nt(z_ref[...], gg_ref[...])
+    kg_ref[...] = dot_nt(z_ref[0:288, :], gg_ref[0:192, :]) + dot_nt(z_ref[96:384, :], gg_ref[192:384, :])
 
     sum1 = jnp.zeros((32, 128), F32)
     grads = jnp.zeros((256, 256), F32)
@@ -368,14 +377,9 @@
     biases = dot_nt(jnp.ones((16, 128), BF16), jnp.concatenate(halves(sums), axis=0))[0:8]
     biases = biases[:, :128] + biases[:, 128:]
 
-    low_lanes = iota((288, 128), 1) < 64
-    left, right = [], []
-    for c in range(3):
-        one, two = kg_ref[0:288, c * 128 : c * 128 + 128], kg_ref[96:384, c * 128 : c * 128 + 128]
-        left.append(one + pltpu.roll(two, 64, 1))
-        right.append(pltpu.roll(one, 64, 1) + two)
-    packed_ref[0:288, :] = jnp.where(low_lanes, left[0], right[1]).astype(BF16)
-    packed_ref[288:432, :] = jnp.where(low_lanes[0:144], left[2][0:144], right[2][144:288]).astype(BF16)
+    packed_ref[0:288, :] = kg_ref[:, 0:128].astype(BF16)
+    last = jnp.concatenate([kg_ref[0:144, 128:192], kg_ref[144:288, 128:192]], axis=1)
+    packed_ref[288:432, :] = last.astype(BF16)
     first = first[:32] + first[32:]
     for block in range(5):
         rows = first[block * 8 : block * 8 + 8] if block < 4 else biases
@@ -457,7 +461,7 @@
         front_kernel,
         (
             shape((8,) + volumes.shape[1:], BF16),
-            shape((256, 256), BF16), shape((864, 64), BF16), shape((32, 128), F32), shape((64, 128), F32), shape((256, 64), BF16), shape((128, 2048), BF16), shape((256, 256), BF16),
+            shape((27, 4, 32), BF16), shape((864, 64), BF16), shape((32, 128), F32), shape((64, 128), F32), shape((256, 64), BF16), shape((128, 2048), BF16), shape((256, 256), BF16),
             shape((128, 512), BF16),
         ),
         (
@@ -465,32 +469,37 @@
             second_bias.reshape(1, 64), deep_grad.reshape(64, 256).T,
         ),
         (
-            ((27, 4, 32), BF16), ((128, 32), F32), ((1, 32), F32), ((1, 64), F32),
+            ((1, 32), F32), ((1, 64), F32),
             pltpu.SemaphoreType.DMA((7,)),
         ),
         8,
         in_hbm=True,
     )
-    w1, k2, bias1, bias2, dg, sel, split, pool = prepared
+    k1, k2, bias1, bias2, dg, sel, split, pool = prepared
     pair = lax.all_to_all(twice, DEPTH + ("y",), 0, 0, axis_index_groups=groups, tiled=True)
     chip = lax.ppermute(pair, "core", [(0, 1), (1, 0)])
     early = call(
         early_kernel,
-        (shape((384, 1024), BF16), shape((2, 256, 1024), F32), shape((192, 1024), BF16), shape((2, 384, 192), BF16), shape((384, 384), BF16)),
-        (pair, w1, k2, bias1, split),
-        (((768, 128), F32), ((384, 256), F32), ((384, 256), F32), ((2, 32, 1024), F32)),
+        (
+            shape((384, 1024), BF16), shape((2, 256, 1024), F32), shape((192, 1024), BF16),
+            shape((256, 256), BF16), shape((2, 384, 192), BF16), shape((288, 192), BF16),
+        ),
+        (pair, k1, k2, bias1, sel, split),
+        (
+            ((768, 128), F32), ((384, 256), F32), ((384, 256), F32), ((2, 32, 1024), F32), ((128, 32), F32),
+        ),
         8,
         10**9,
     )
     deep, packed = call(
         main_kernel,
         (shape((256, 64), BF16), shape((ROWS, 128), BF16)),
-        (pair, chip, *early, w1, bias1, bias2, dg, sel, split, pool),
+        (pair, chip, *early, bias1, bias2, dg, sel, split, pool),
         (
             ((512, 128), F32), ((256, 256), F32), ((256, 256), F32), ((384, 1024), BF16),
             ((2, 256, 1024), F32), ((2, 32, 1024), F32), ((384, 1024), BF16), ((2, 64, 1024), F32),
             ((384, 1024), BF16), ((384, 1024), BF16), ((128, 1024), F32), ((64, 1024), F32), ((256, 1024), BF16),
-            ((384, 384), F32), ((384, 1024), F32),
+            ((288, 192), F32), ((384, 1024), F32),
         ),
         20,
         10**9,

time: 64.3 us -> 64 us (level)
  no operation moved by 1% of the time
where the time goes in v8:
time: 64 us; the launch traced here: 63.7 us
  blocking collectives  50.5 us (79%)
  Pallas kernels  8.01 us (13%)
  starting transfers between devices  4.58 us (7%)
  between operations  0.66 us (1%)
    all_to_all x3, blocking collectives, exchange(): lax.all_to_all(blocks, axes, split_axis=0, concat_axis=0, tiled=True)  37.5 us
    all_to_all x1, blocking collectives, per_device(): lax.all_to_all(twice, DEPTH + ('y',), 0, 0, axis_index_groups=groups, til...  13 us
    pallas_call x6, Pallas kernels, call(): pl.pallas_call(kernel, out_shape=outs, in_specs=[pl.BlockSpec(memory_spac...  8.01 us
    ppermute x1, starting transfers between devices, per_device(): chip = lax.ppermute(pair, 'core', [(0, 1), (1, 0)])  4.58 us
  transfers between devices with their start and end apart: 1, of which 0 were waited for; matrix products, arithmetic and copies ran while one was open for 0% of the time, Pallas kernels for 3%

profile of v8, /device:TPU:1, one launch (start us, length us, event | category | flops | bytes accessed | tf_op | source)
XLA Modules:
  0.0 63.7 jit_solution(12174762285157337668)
XLA Ops:
  0.6 1.2 %shard_map.101 = (bf16[8,4,4,8,128]{4,3,2,1,0:T(8,128)(2,1)S(1)}, bf16[27,4,32]{2,1,0:T(4,128)(2,1)S(1)}, bf16[864,64]{1,0:T(8,128)(2,1)S(1)}, f32[32,128]{1,0:T...) custom-call(bf16[4,4,4,8,128]{4,3,2,1,0:T(8,128)(2,1)} %volumes_hbm., ...), custom_call_target="tpu_custom_call" | custom-call | tf_op jit(solution)/shard_map/pallas_call | solution.py:435
  1.9 13.0 %all_to_all.20.pair_ref = bf16[8,4,4,8,128]{4,3,2,1,0:T(8,128)(2,1)S(1)} all-to-all(bf16[8,4,4,8,128]{4,3,2,1,0:T(8,128)(2,1)S(1)} %get-tuple-element.27), channel_id=1, replica_groups={{8,10,12,14,16,18,20,22},{24,26,28,30,32,34,36,38},{40,42,44,46,48,50,5..., dimensions={0} | all-to-all | bytes 524288 | tf_op jit(solution)/shard_map/all_to_all | solution.py:479
  14.8 4.6 %collective-permute-start = (bf16[8,4,4,8,128]{4,3,2,1,0:T(8,128)(2,1)S(1)}, bf16[8,4,4,8,128]{4,3,2,1,0:T(8,128)(2,1)S(1)}, u32[]{:S(2)}, u32[]{:S(2)}) collective-permute-start(bf16[8,4,4,8,128]{4,3,2,1,0:T(8,128)(2,1)S(1)} %all_to_all.20.pair_ref), channel_id=1, source_target_pairs={{0,8},{8,0},{1,9},{9,1},{2,10},{10,2},{3,11},{11,3},{4,12},{12,4},... | collective-permute-start | bytes 786440 | tf_op jit(solution)/shard_map/ppermute | solution.py:480
  19.4 1.6 %shard_map.102 = (bf16[384,1024]{1,0:T(8,128)(2,1)S(1)}, f32[2,256,1024]{2,1,0:T(8,128)S(1)}, bf16[192,1024]{1,0:T(8,128)(2,1)S(1)}, bf16[256,256]{1,0:T(8,128)(...) custom-call(bf16[8,4,4,8,128]{4,3,2,1,0:T(8,128)(2,1)S(1)} %all_to_all.20.pair_ref, ...), custom_call_target="tpu_custom_call" | custom-call | flops 1000000000 | bytes 1000000 | tf_op jit(solution)/shard_map/pallas_call | solution.py:435
  21.0 0.0 collective-permute-done.chip_ref
  21.0 4.2 %shard_map.103 = (bf16[256,64]{1,0:T(8,128)(2,1)S(1)}, bf16[512,128]{1,0:T(8,128)(2,1)S(1)}) custom-call(bf16[8,4,4,8,128]{4,3,2,1,0:T(8,128)(2,1)S(1)} %all_to_all.20.pair_ref, bf16[8,4,4,8,128]{4,3,2,1,0:T(8,128)(2,1)S(1)} %collective-permute-done.chip_ref, bf16[384,1024]{1,0:T(8,128)(2,1)S(1)} %get-tuple-element.33.early_x_ref, ...), custom_call_target="tpu_custom_call" | custom-call | flops 1000000000 | bytes 1000000 | tf_op jit(solution)/shard_map/pallas_call | solution.py:435
  25.3 12.1 %all_to_all.21 = bf16[32,16,128]{2,1,0:T(8,128)(2,1)S(1)} all-to-all(bf16[32,16,128]{2,1,0:T(8,128)(2,1)S(1)} %bitcast.25), channel_id=1, replica_groups=mesh['z'=8,'x_lo'=2,'core'=2,'y'=4,'x_hi'=2] {'x_lo','core','y','x_hi'}, dimensions={0} | all-to-all | bytes 262144 | tf_op jit(solution)/shard_map/all_to_all | solution.py:452
  37.4 12.6 %all_to_all.22 = bf16[8,16,128]{2,1,0:T(8,128)(2,1)S(1)} all-to-all(bf16[8,16,128]{2,1,0:T(8,128)(2,1)S(1)} %bitcast.23), channel_id=1, replica_groups=mesh['z'=8,'x_lo'=2,'core'=2,'y'=4,'x_hi'=2] {'z'}, dimensions={0} | all-to-all | bytes 65536 | tf_op jit(solution)/shard_map/all_to_all | solution.py:452
  50.0 12.8 %all_to_all.23 = bf16[32,16,128]{2,1,0:T(8,128)(2,1)S(1)} all-to-all(bf16[32,16,128]{2,1,0:T(8,128)(2,1)S(1)} %bitcast.21), channel_id=1, replica_groups=mesh['z'=8,'x_lo'=2,'core'=2,'y'=4,'x_hi'=2] {'x_lo','core','y','x_hi'}, dimensions={0} | all-to-all | bytes 262144 | tf_op jit(solution)/shard_map/all_to_all | solution.py:452
  62.9 0.9 %shard_map.106 = (bf16[256,64]{1,0:T(8,128)(2,1)}, f32[864,64]{1,0:T(8,128)}, f32[27,4,32]{2,1,0:T(4,128)}, f32[1,32]{1,0:T(1,128)}, f32[1,64]{1,0:T(1,128)}) custom-call(bf16[512,128]{1,0:T(8,128)(2,1)S(1)} %bitcast.22, bf16[256,64]{1,0:T(8,128)(2,1)S(1)} %get-tuple-element.43.deep_in_ref), custom_call_target="tpu_custom_call" | custom-call | tf_op jit(solution)/shard_map/pallas_call | solution.py:435
  (2 shorter events, 0.1 us)
Async XLA Ops:
  14.8 6.2 %collective-permute-start = (bf16[8,4,4,8,128]{4,3,2,1,0:T(8,128)(2,1)S(1)}, bf16[8,4,4,8,128]{4,3,2,1,0:T(8,128)(2,1)S(1)}, u32[]{:S(2)}, u32[]{:S(2)}) collective-permute-start(bf16[8,4,4,8,128]{4,3,2,1,0:T(8,128)(2,1)S(1)} %all_to_all.20.pair_ref), channel_id=1, source_target_pairs={{0,8},{8,0},{1,9},{9,1},{2,10},{10,2},{3,11},{11,3},{4,12},{12,4},... | collective-permute-start | bytes 786440 | tf_op jit(solution)/shard_map/ppermute | solution.py:480

commit v9 on v8

--- a/solution.py
+++ b/solution.py
@@ -8,7 +8,7 @@
 F32 = jnp.float32
 BF16 = jnp.bfloat16
 DEPTH = ("z", "x_lo", "core")
-PLANE = ("x_lo", "core", "y", "x_hi")
+PLANE = ("y", "x_hi", "x_lo", "core")
 LINE = ("z",)
 ROWS = 512
 CHUNK = 16

time: 64 us -> 63.8 us (level)
  no operation moved by 1% of the time
where the time goes in v9:
time: 63.8 us; the launch traced here: 63.5 us
  blocking collectives  50.3 us (79%)
  Pallas kernels  8.01 us (13%)
  starting transfers between devices  4.58 us (7%)
  between operations  0.66 us (1%)
    all_to_all x3, blocking collectives, exchange(): lax.all_to_all(blocks, axes, split_axis=0, concat_axis=0, tiled=True)  37.3 us
    all_to_all x1, blocking collectives, per_device(): lax.all_to_all(twice, DEPTH + ('y',), 0, 0, axis_index_groups=groups, til...  13 us
    pallas_call x6, Pallas kernels, call(): pl.pallas_call(kernel, out_shape=outs, in_specs=[pl.BlockSpec(memory_spac...  8.01 us
    ppermute x1, starting transfers between devices, per_device(): chip = lax.ppermute(pair, 'core', [(0, 1), (1, 0)])  4.58 us
  transfers between devices with their start and end apart: 1, of which 0 were waited for; matrix products, arithmetic and copies ran while one was open for 0% of the time, Pallas kernels for 3%

profile of v9, /device:TPU:1, one launch (start us, length us, event | category | flops | bytes accessed | tf_op | source)
XLA Modules:
  0.0 63.5 jit_solution(2228083516824960688)
XLA Ops:
  0.6 1.2 %shard_map.101 = (bf16[8,4,4,8,128]{4,3,2,1,0:T(8,128)(2,1)S(1)}, bf16[27,4,32]{2,1,0:T(4,128)(2,1)S(1)}, bf16[864,64]{1,0:T(8,128)(2,1)S(1)}, f32[32,128]{1,0:T...) custom-call(bf16[4,4,4,8,128]{4,3,2,1,0:T(8,128)(2,1)} %volumes_hbm., ...), custom_call_target="tpu_custom_call" | custom-call | tf_op jit(solution)/shard_map/pallas_call | solution.py:435
  1.9 13.0 %all_to_all.20.pair_ref = bf16[8,4,4,8,128]{4,3,2,1,0:T(8,128)(2,1)S(1)} all-to-all(bf16[8,4,4,8,128]{4,3,2,1,0:T(8,128)(2,1)S(1)} %get-tuple-element.27), channel_id=1, replica_groups={{8,10,12,14,16,18,20,22},{24,26,28,30,32,34,36,38},{40,42,44,46,48,50,5..., dimensions={0} | all-to-all | bytes 524288 | tf_op jit(solution)/shard_map/all_to_all | solution.py:479
  14.8 4.6 %collective-permute-start = (bf16[8,4,4,8,128]{4,3,2,1,0:T(8,128)(2,1)S(1)}, bf16[8,4,4,8,128]{4,3,2,1,0:T(8,128)(2,1)S(1)}, u32[]{:S(2)}, u32[]{:S(2)}) collective-permute-start(bf16[8,4,4,8,128]{4,3,2,1,0:T(8,128)(2,1)S(1)} %all_to_all.20.pair_ref), channel_id=1, source_target_pairs={{0,8},{8,0},{1,9},{9,1},{2,10},{10,2},{3,11},{11,3},{4,12},{12,4},... | collective-permute-start | bytes 786440 | tf_op jit(solution)/shard_map/ppermute | solution.py:480
  19.4 1.6 %shard_map.102 = (bf16[384,1024]{1,0:T(8,128)(2,1)S(1)}, f32[2,256,1024]{2,1,0:T(8,128)S(1)}, bf16[192,1024]{1,0:T(8,128)(2,1)S(1)}, bf16[256,256]{1,0:T(8,128)(...) custom-call(bf16[8,4,4,8,128]{4,3,2,1,0:T(8,128)(2,1)S(1)} %all_to_all.20.pair_ref, ...), custom_call_target="tpu_custom_call" | custom-call | flops 1000000000 | bytes 1000000 | tf_op jit(solution)/shard_map/pallas_call | solution.py:435
  21.0 0.0 collective-permute-done.chip_ref
  21.0 4.2 %shard_map.103 = (bf16[256,64]{1,0:T(8,128)(2,1)S(1)}, bf16[512,128]{1,0:T(8,128)(2,1)S(1)}) custom-call(bf16[8,4,4,8,128]{4,3,2,1,0:T(8,128)(2,1)S(1)} %all_to_all.20.pair_ref, bf16[8,4,4,8,128]{4,3,2,1,0:T(8,128)(2,1)S(1)} %collective-permute-done.chip_ref, bf16[384,1024]{1,0:T(8,128)(2,1)S(1)} %get-tuple-element.33.early_x_ref, ...), custom_call_target="tpu_custom_call" | custom-call | flops 1000000000 | bytes 1000000 | tf_op jit(solution)/shard_map/pallas_call | solution.py:435
  25.3 12.0 %all_to_all.21 = bf16[32,16,128]{2,1,0:T(8,128)(2,1)S(1)} all-to-all(bf16[32,16,128]{2,1,0:T(8,128)(2,1)S(1)} %bitcast.25), channel_id=1, replica_groups=mesh['z'=8,'x_lo'=2,'core'=2,'y'=4,'x_hi'=2] {'y','x_hi','x_lo','core'}, dimensions={0} | all-to-all | bytes 262144 | tf_op jit(solution)/shard_map/all_to_all | solution.py:452
  37.3 12.7 %all_to_all.22 = bf16[8,16,128]{2,1,0:T(8,128)(2,1)S(1)} all-to-all(bf16[8,16,128]{2,1,0:T(8,128)(2,1)S(1)} %bitcast.23), channel_id=1, replica_groups=mesh['z'=8,'x_lo'=2,'core'=2,'y'=4,'x_hi'=2] {'z'}, dimensions={0} | all-to-all | bytes 65536 | tf_op jit(solution)/shard_map/all_to_all | solution.py:452
  50.1 12.6 %all_to_all.23 = bf16[32,16,128]{2,1,0:T(8,128)(2,1)S(1)} all-to-all(bf16[32,16,128]{2,1,0:T(8,128)(2,1)S(1)} %bitcast.21), channel_id=1, replica_groups=mesh['z'=8,'x_lo'=2,'core'=2,'y'=4,'x_hi'=2] {'y','x_hi','x_lo','core'}, dimensions={0} | all-to-all | bytes 262144 | tf_op jit(solution)/shard_map/all_to_all | solution.py:452
  62.7 0.9 %shard_map.106 = (bf16[256,64]{1,0:T(8,128)(2,1)}, f32[864,64]{1,0:T(8,128)}, f32[27,4,32]{2,1,0:T(4,128)}, f32[1,32]{1,0:T(1,128)}, f32[1,64]{1,0:T(1,128)}) custom-call(bf16[512,128]{1,0:T(8,128)(2,1)S(1)} %bitcast.22, bf16[256,64]{1,0:T(8,128)(2,1)S(1)} %get-tuple-element.43.deep_in_ref), custom_call_target="tpu_custom_call" | custom-call | tf_op jit(solution)/shard_map/pallas_call | solution.py:435
  (2 shorter events, 0.1 us)
Async XLA Ops:
  14.8 6.2 %collective-permute-start = (bf16[8,4,4,8,128]{4,3,2,1,0:T(8,128)(2,1)S(1)}, bf16[8,4,4,8,128]{4,3,2,1,0:T(8,128)(2,1)S(1)}, u32[]{:S(2)}, u32[]{:S(2)}) collective-permute-start(bf16[8,4,4,8,128]{4,3,2,1,0:T(8,128)(2,1)S(1)} %all_to_all.20.pair_ref), channel_id=1, source_target_pairs={{0,8},{8,0},{1,9},{9,1},{2,10},{10,2},{3,11},{11,3},{4,12},{12,4},... | collective-permute-start | bytes 786440 | tf_op jit(solution)/shard_map/ppermute | solution.py:480
